TPU v7x, 32 devices: a whole 2x2x4 slice. The times are simulated.
32 devices in a mesh: grp: 2 (over y), dp: 4 (over x, core), tp: 4 (over z).
Axes of the slice: x: 2, y: 2, z: 4, core: 2. Of those that a mesh axis runs over, the one named last changes fastest.
Arguments:
- latents: bfloat16 [1024, 3072], P(('grp', 'dp', 'tp')), parts along dimension 0, may hold values from -6 to 6
- step_index: int32 [16], P(('grp', 'dp')), parts along dimension 0, may hold values from 0 to 2
- mod_table: float32 [4, 3, 3072], replicated, may hold values from -4 to 4
- base_up: bfloat16 [3072, 12288], P(None, 'tp'), may hold values from -0.109375 to 0.109375
- base_down: bfloat16 [12288, 3072], P('tp'), may hold values from -0.0546875 to 0.0546875
- up_a: bfloat16 [3072, 64], P(('dp', 'tp')), may hold values from -0.109375 to 0.109375
- up_b: bfloat16 [64, 12288], P('dp', 'tp'), may hold values from -0.75 to 0.75
- down_a: bfloat16 [12288, 64], P('tp', 'dp'), may hold values from -0.0546875 to 0.0546875
- down_b: bfloat16 [64, 3072], P(None, ('dp', 'tp')), may hold values from -0.75 to 0.75
Outputs:
- velocities: float32 [2, 1024, 3072], P(None, ('grp', 'dp', 'tp')), parts along dimension 1
- final_state: float32 [1024, 3072], P(('grp', 'dp', 'tp')), parts along dimension 0
There are 2 independent parts, one for each index of `grp`. A program takes and returns all parts, laid end to end along the dimension named above; an argument that names none is the same for every part. Nothing has to cross between parts.
Inputs may be any that keep to these rules, and one draw needn't show every extreme that they name: `step_index`: the second step of an image uses the next index of the plan.
All inputs are finite; a program needn't handle non-finite values.
Results may differ from a plain program's by a relative error of at most 0.0061.
Values may be sent and summed in bfloat16 or wider, within the bound.
No kernel may reach another device: no remote copies, remote signals or barrier semaphores. Data moves between devices by JAX's collectives and lax.ppermute only.
A program may use at most 192 MiB of HBM per device.

v0:
```python
import jax
import jax.numpy as jnp
from jax import lax
from jax.sharding import PartitionSpec as P

NSTEPS = 4


def normalize(state, shift, scale):
    mean = jnp.mean(state, axis=1, keepdims=True)
    centered = state - mean
    spread = jnp.mean(centered * centered, axis=1, keepdims=True)
    return (centered * lax.rsqrt(spread + 1e-06) * (1.0 + scale) + shift).astype(jnp.bfloat16)


def local(latents, step_index, mod_table, base_up, base_down, up_a, up_b, down_a, down_b):
    full_up_a, full_down_b = (
        lax.all_gather(up_a, ("dp", "tp"), axis=0, tiled=True),
        lax.all_gather(down_b, ("dp", "tp"), axis=1, tiled=True),
    )
    cols_up_b, rows_down_a = (
        lax.all_gather(up_b, "dp", axis=0, tiled=True),
        lax.all_gather(down_a, "dp", axis=1, tiled=True),
    )
    merged_up = (
        base_up.astype(jnp.float32)
        + jnp.dot(full_up_a, cols_up_b, preferred_element_type=jnp.float32)
    ).astype(jnp.bfloat16)
    merged_down = (
        base_down.astype(jnp.float32)
        + jnp.dot(rows_down_a, full_down_b, preferred_element_type=jnp.float32)
    ).astype(jnp.bfloat16)
    own_count = latents.shape[0]
    group_rows = own_count * lax.axis_size("tp")
    image_count = step_index.shape[0]
    image_rows = group_rows // image_count
    own_start = lax.axis_index("tp") * own_count
    step_size = -1.0 / NSTEPS

    def row_steps(count, offset):
        rows = jnp.arange(count, dtype=jnp.int32)
        image = rows // image_rows
        picks = (image[:, None] == jnp.arange(image_count, dtype=jnp.int32)[None, :]).astype(
            jnp.int32
        )
        return jnp.sum(picks * step_index[None, :], axis=1) + offset

    def modulation(steps):
        onehot = (steps[:, None] == jnp.arange(NSTEPS, dtype=jnp.int32)[None, :]).astype(
            jnp.float32
        )
        shift = jnp.dot(onehot, mod_table[:, 0, :], precision=lax.Precision.HIGHEST)
        scale = jnp.dot(onehot, mod_table[:, 1, :], precision=lax.Precision.HIGHEST)
        gate = jnp.dot(onehot, mod_table[:, 2, :], precision=lax.Precision.HIGHEST)
        return (shift, scale, gate)

    def project(normed):
        upper = jnp.dot(normed, merged_up, preferred_element_type=jnp.float32)
        hidden = jax.nn.gelu(upper, approximate=True).astype(jnp.bfloat16)
        return jnp.dot(hidden, merged_down, preferred_element_type=jnp.float32)

    state_all = lax.all_gather(latents, "tp", axis=0, tiled=True).astype(jnp.float32)
    shift, scale, gate = modulation(row_steps(group_rows, 0))
    normed = normalize(state_all, shift, scale)
    first = gate * lax.psum(project(normed), "tp")
    state_all = state_all + step_size * first
    shift, scale, gate = modulation(row_steps(group_rows, 1))
    normed = normalize(state_all, shift, scale)
    gate_own = lax.dynamic_slice_in_dim(gate, own_start, own_count, 0)
    second = gate_own * lax.psum_scatter(project(normed), "tp", scatter_dimension=0, tiled=True)
    state_own = lax.dynamic_slice_in_dim(state_all, own_start, own_count, 0) + step_size * second
    first_own = lax.dynamic_slice_in_dim(first, own_start, own_count, 0)
    return (jnp.stack([first_own, second]), state_own)


def solution(mesh):
    return jax.shard_map(
        local,
        mesh=mesh,
        in_specs=(
            P(("grp", "dp", "tp"), None),
            P(("grp", "dp")),
            P(),
            P(None, "tp"),
            P("tp", None),
            P(("dp", "tp"), None),
            P("dp", "tp"),
            P("tp", "dp"),
            P(None, ("dp", "tp")),
        ),
        out_specs=(P(None, ("grp", "dp", "tp"), None), P(("grp", "dp", "tp"), None)),
        check_vma=False,
    )
```

profile of v0, /device:TPU:0, one launch (start us, length us, event | category | flops | bytes accessed | tf_op | source)
XLA Modules:
  0.0 294.9 jit_solution(5854867248397038212)
XLA Ops:
  7.2 0.0 copy-start.5
  7.2 0.0 copy-start
  7.2 0.0 all-reduce.2.cloned.1.call-start
  7.2 21.5 %all_gather.15 = bf16[128,3072]{1,0:T(8,128)(2,1)S(1)} all-gather(bf16[32,3072]{1,0:T(8,128)(2,1)} %param.9), channel_id=1, replica_groups=mesh['grp'=2,'dp'=4,'tp'=4] {'tp'}, dimensions={0}, use_global_device_ids=true | all-gather | bytes 983040 | tf_op jit(solution)/shard_map/all_gather | solution.py:62
  28.7 0.2 convert_reduce_fusion
  28.9 0.4 fusion.6
  29.3 0.0 copy-done.5
  29.3 0.1 fusion.55
  29.4 0.0 copy-done
  29.4 1.0 fusion.1
  30.4 0.0 copy-start.3
  30.4 0.8 fusion.2
  31.2 0.0 copy-start.1
  31.2 0.0 copy-start.4
  31.2 0.0 copy-done.3
  31.3 34.6 %all-gather.1 = bf16[16,192,64]{1,2,0:T(8,128)(2,1)S(1)} all-gather(bf16[1,192,64]{1,2,0:T(8,128)(2,1)S(1)} %bitcast.39), channel_id=1, replica_groups=mesh['grp'=2,'dp'=4,'tp'=4] {'dp','tp'}, dimensions={0}, use_global_device_ids=true | all-gather | bytes 417792 | tf_op jit(solution)/shard_map/all_gather | solution.py:19
  65.8 0.3 copy.16
  66.1 0.5 reshape.49
  66.7 0.0 copy-done.1
  66.7 0.0 copy-start.2
  66.7 6.3 %all_gather.18 = bf16[3072,64]{0,1:T(8,128)(2,1)S(1)} all-gather(bf16[3072,16]{0,1:T(8,128)(2,1)S(1)} %copy-done.1), channel_id=1, replica_groups=mesh['grp'=2,'dp'=4,'tp'=4] {'dp'}, dimensions={1}, use_global_device_ids=true | all-gather | bytes 491520 | tf_op jit(solution)/shard_map/all_gather | solution.py:23
  73.0 0.0 copy-done.4
  73.0 34.1 %all-gather = bf16[16,192,64]{1,2,0:T(8,128)(2,1)S(1)} all-gather(bf16[1,192,64]{1,2,0:T(8,128)(2,1)S(1)} %bitcast.40), channel_id=1, replica_groups=mesh['grp'=2,'dp'=4,'tp'=4] {'dp','tp'}, dimensions={0}, use_global_device_ids=true | all-gather | bytes 417792 | tf_op jit(solution)/shard_map/all_gather | solution.py:18
  107.1 0.3 copy.15
  107.4 0.5 reshape.47
  107.9 0.0 copy-done.2
  107.9 6.3 %all_gather.17 = bf16[64,3072]{1,0:T(8,128)(2,1)S(1)} all-gather(bf16[16,3072]{1,0:T(8,128)(2,1)S(1)} %copy-done.2), channel_id=1, replica_groups=mesh['grp'=2,'dp'=4,'tp'=4] {'dp'}, dimensions={0}, use_global_device_ids=true | all-gather | bytes 491520 | tf_op jit(solution)/shard_map/all_gather | solution.py:22
  114.3 12.9 %add_convert_fusion = bf16[3072,3072]{1,0:T(8,128)(2,1)} fusion(bf16[3072,3072]{1,0:T(8,128)(2,1)} %param.13, bf16[3072,64]{0,1:T(8,128)(2,1)S(1)} %all_gather.18, bf16[3072,64]{0,1:T(8,128)(2,1)S(1)} %reshape.49), kind=kOutput, calls=%fused_computation | convolution fusion | flops 1236271104 | bytes 38535168 | tf_op jit(solution)/shard_map/dot_general | solution.py:31
  127.2 13.0 %add_convert_fusion.1 = bf16[3072,3072]{1,0:T(8,128)(2,1)} fusion(bf16[3072,3072]{1,0:T(8,128)(2,1)} %param.12, bf16[3072,64]{0,1:T(8,128)(2,1)S(1)} %reshape.47, bf16[64,3072]{1,0:T(8,128)(2,1)S(1)} %all_gather.17), kind=kOutput, calls=%fused_computation.1 | convolution fusion | flops 1236271104 | bytes 38535168 | tf_op jit(solution)/shard_map/dot_general | solution.py:27
  140.2 18.2 %fusion.25 = f32[128,3072]{1,0:T(8,128)} fusion(bf16[3072,3072]{1,0:T(8,128)(2,1)} %add_convert_fusion, bf16[128,3072]{1,0:T(8,128)(2,1)S(1)} %fusion.2, bf16[3072,3072]{1,0:T(8,128)(2,1)} %add_convert_fusion.1), kind=kOutput, calls=%fused_computation.37 | convolution fusion | flops 4835377152 | bytes 40108032 | tf_op jit(solution)/shard_map/dot_general | solution.py:60
  158.4 0.0 all-reduce.2.cloned.1.call-update
  158.5 0.3 reduce-scatter.2.cloned.1.call-start
  158.7 68.0 %all-reduce.2.cloned.1.call-done = f32[128,3072]{1,0:T(8,128)} async-done(((f32[128,3072]{1,0:T(8,128)}), f32[128,3072]{1,0:T(8,128)}) %all-reduce.2.cloned.1.call-update) | async-done | bytes 1572880 | tf_op jit(solution)/shard_map/psum | solution.py:65
  226.7 3.6 %fusion.64 = (f32[128]{0:T(128)S(1)}, f32[128,3072]{1,0:T(8,128)S(1)}, f32[128,3072]{1,0:T(8,128)}) fusion(bf16[128,3072]{1,0:T(8,128)(2,1)S(1)} %all_gather.15, f32[128,3072]{1,0:T(8,128)} %all-reduce.2.cloned.1.call-done, f32[4,3,3072]{2,0,1:T(4,128)S(1)} %copy-done, s32[128]{0:T(128)S(1)} %fusion.55), kind=kOutput, calls=%fused_computation.91 | convolution fusion | flops 20840832 | bytes 5555200 | tf_op jit(solution)/shard_map/dot_general | solution.py:54
  230.3 0.3 multiply_reduce_fusion
  230.6 1.0 fusion
  231.6 0.8 fusion.3
  232.4 18.3 %fusion.23 = f32[128,3072]{1,0:T(8,128)} fusion(bf16[3072,3072]{1,0:T(8,128)(2,1)} %add_convert_fusion, bf16[128,3072]{1,0:T(8,128)(2,1)S(1)} %fusion.3, bf16[3072,3072]{1,0:T(8,128)(2,1)} %add_convert_fusion.1), kind=kOutput, calls=%fused_computation.36 | convolution fusion | flops 4835377152 | bytes 40108032 | tf_op jit(solution)/shard_map/dot_general | solution.py:60
  250.7 0.0 reduce-scatter.2.cloned.1.call-update
  250.7 2.0 fusion.36
  252.7 1.0 dynamic-slice_bitcast_fusion
  253.7 31.5 %reduce-scatter.2.cloned.1.call-done = f32[32,3072]{1,0:T(8,128)} async-done(((f32[128,3072]{1,0:T(8,128)}), f32[32,3072]{1,0:T(8,128)}) %reduce-scatter.2.cloned.1.call-update) | async-done | bytes 393232 | tf_op jit(solution)/shard_map/reduce_scatter | solution.py:70
  285.2 1.9 multiply_add_fusion
  287.1 0.9 pad_maximum_fusion
  (6 shorter events, 0.0 us)
Async XLA Ops:
  7.2 22.2 %copy-start.5 = (s32[2]{0:T(128)S(1)}, s32[2]{0:T(128)}, u32[]{:S(2)}) copy-start(s32[2]{0:T(128)} %param.10) | copy-start | bytes 28
  7.2 22.2 %copy-start = (f32[4,3,3072]{2,0,1:T(4,128)S(1)}, f32[4,3,3072]{2,0,1:T(4,128)}, u32[]{:S(2)}) copy-start(f32[4,3,3072]{2,0,1:T(4,128)} %param.11) | copy-start | bytes 442372
  7.2 219.5 %all-reduce.2.cloned.1.call-start = ((), (), s32[]{:S(2)}) async-start(), calls=%async_computation.1 | async-start | bytes 3145728 | tf_op jit(solution)/shard_map/psum | solution.py:65
  30.4 0.9 copy-start.3
  31.2 35.4 %copy-start.1 = (bf16[3072,16]{0,1:T(8,128)(2,1)S(1)}, bf16[3072,16]{0,1:T(8,128)(2,1)}, u32[]{:S(2)}) copy-start(bf16[3072,16]{0,1:T(8,128)(2,1)} %param.16) | copy-start | bytes 294916
  31.2 41.7 %copy-start.4 = (bf16[192,64]{0,1:T(8,128)(2,1)S(1)}, bf16[192,64]{0,1:T(8,128)(2,1)}, u32[]{:S(2)}) copy-start(bf16[192,64]{0,1:T(8,128)(2,1)} %param.14) | copy-start | bytes 73732
  66.7 41.2 %copy-start.2 = (bf16[16,3072]{1,0:T(8,128)(2,1)S(1)}, bf16[16,3072]{1,0:T(8,128)(2,1)}, u32[]{:S(2)}) copy-start(bf16[16,3072]{1,0:T(8,128)(2,1)} %param.15) | copy-start | bytes 294916
  158.5 126.7 %reduce-scatter.2.cloned.1.call-start = ((), (), s32[]{:S(2)}) async-start(), calls=%async_computation.2 | async-start | bytes 1966080 | tf_op jit(solution)/shard_map/reduce_scatter | solution.py:70
Sparse Core Ops, SparseCore 0:
  158.6 68.0 all-reduce.1
  250.8 34.3 reduce-scatter.1
where the time goes:
time: 295 us
  blocking collectives  103 us (35%)
  waiting for transfers between devices  99.5 us (34%)
  matrix products  71.5 us (24%)
  between operations  14.2 us (5%)
  other arithmetic  3.84 us (1%)
    psum x1, waiting for transfers between devices, local(): first = gate * lax.psum(project(normed), 'tp')  68 us
    dot_general x2, matrix products, project(): return jnp.dot(hidden, merged_down, preferred_element_type=jnp.float32)  36.5 us
    all_gather x1, blocking collectives, local(): lax.all_gather(down_b, ('dp', 'tp'), axis=1, tiled=True)  34.6 us
    all_gather x1, blocking collectives, local(): lax.all_gather(up_a, ('dp', 'tp'), axis=0, tiled=True)  34.1 us
    reduce_scatter x1, waiting for transfers between devices, local(): lax.psum_scatter(project(normed), 'tp', scatter_dimension=0, tiled=True)  31.5 us
    all_gather x1, blocking collectives, local(): lax.all_gather(latents, 'tp', axis=0, tiled=True).astype(jnp.float32)  21.5 us
    dot_general x1, matrix products, local(): jnp.dot(full_up_a, cols_up_b, preferred_element_type=jnp.float32)  13 us
    dot_general x1, matrix products, local(): jnp.dot(rows_down_a, full_down_b, preferred_element_type=jnp.float32)  12.9 us
  transfers between devices with their start and end apart: 2, of which 2 were waited for; matrix products, arithmetic and copies ran while one was open for 1% of the time, Pallas kernels for 0%

commit v1 on v0

--- a/solution.py
+++ b/solution.py
@@ -1,9 +1,259 @@
+import functools
+
 import jax
 import jax.numpy as jnp
 from jax import lax
+from jax.experimental import pallas as pl
+from jax.experimental.pallas import tpu as pltpu
 from jax.sharding import PartitionSpec as P
 
 NSTEPS = 4
+STEP_SIZE = -1.0 / NSTEPS
+BF16, F32 = jnp.bfloat16, jnp.float32
+VMEM_GRANT = 16 << 20
+VMEM = pl.BlockSpec(memory_space=pltpu.VMEM)
+SMEM = pl.BlockSpec(memory_space=pltpu.SMEM)
+HBM = pl.BlockSpec(memory_space=pltpu.HBM)
+NT = (((1,), (1,)), ((), ()))
+
+
+def call(body, outs, in_specs, out_specs, name, scratch=(), flops=0, bytes_accessed=0):
+    return pl.pallas_call(
+        body,
+        out_shape=outs,
+        in_specs=in_specs,
+        out_specs=out_specs,
+        scratch_shapes=list(scratch),
+        compiler_params=pltpu.CompilerParams(vmem_limit_bytes=VMEM_GRANT),
+        cost_estimate=pl.CostEstimate(
+            flops=flops, bytes_accessed=bytes_accessed, transcendentals=0
+        ),
+        name=name,
+    )
+
+
+def shape(dims, dtype=BF16):
+    return jax.ShapeDtypeStruct(dims, dtype)
+
+
+def modulated(state, shift, scale):
+    mean = jnp.mean(state, axis=1, keepdims=True)
+    centered = state - mean
+    spread = jnp.mean(centered * centered, axis=1, keepdims=True)
+    return (centered * lax.rsqrt(spread + 1e-06) * (1.0 + scale) + shift).astype(BF16)
+
+
+def gelu(x):
+    return x * (0.5 * (1.0 + jnp.tanh(0.7978845608028654 * (x + 0.044715 * (x * x * x)))))
+
+
+def mod_row(mod_ref, which, step):
+    return mod_ref[which, pl.ds(step, 1), :]
+
+
+def pack_body(slots, rank, ua_ref, db_ref, ub_ref, da_ref, p_ref, q_ref):
+    rows = []
+    for slot in range(slots):
+        part = pl.ds(slot * rank, rank)
+        rows += [ua_ref[part, :], db_ref[part, :]]
+    both = jnp.concatenate(rows, axis=0).astype(F32)
+    width = both.shape[0]
+    eye = (
+        lax.broadcasted_iota(jnp.int32, (width, width), 0)
+        == lax.broadcasted_iota(jnp.int32, (width, width), 1)
+    ).astype(F32)
+    cols = lax.dot_general(
+        both.astype(BF16), eye.astype(BF16), (((0,), (0,)), ((), ())), preferred_element_type=F32
+    ).astype(BF16)
+    height = p_ref.shape[0]
+    for piece in range(cols.shape[0] // height):
+        p_ref[:, piece * width : (piece + 1) * width] = cols[piece * height : (piece + 1) * height, :]
+    q_ref[0:rank, :] = ub_ref[...]
+    q_ref[rank : 2 * rank, :] = da_ref[...]
+
+
+def norm_body(steps_ref, place_ref, lat_ref, mod_ref, out_ref):
+    step = steps_ref[place_ref[2]]
+    state = lat_ref[...].astype(F32)
+    out_ref[...] = modulated(state, mod_row(mod_ref, 0, step), mod_row(mod_ref, 1, step))
+
+
+def fetch_body(parts, src_ref, dst_ref, sems):
+    rows = src_ref.shape[0] // parts
+    copies = [
+        pltpu.make_async_copy(
+            src_ref.at[pl.ds(i * rows, rows)], dst_ref.at[pl.ds(i * rows, rows)], sems.at[i]
+        )
+        for i in range(parts)
+    ]
+    for copy in copies:
+        copy.start()
+    for copy in copies:
+        copy.wait()
+
+
+def fetch(src, name):
+    parts = 8
+    return call(
+        functools.partial(fetch_body, parts),
+        pltpu.VMEM(src.shape, src.dtype),
+        [HBM],
+        VMEM,
+        name,
+        [pltpu.SemaphoreType.DMA((parts,))],
+        bytes_accessed=2 * src.size * src.dtype.itemsize,
+    )(src)
+
+
+def assemble_body(tp, dp, place_ref, *refs):
+    p_parts, q_parts, (p_ref, q_ref) = refs[:dp], refs[dp : 2 * dp], refs[2 * dp :]
+    me_tp, me_dp = place_ref[0], place_ref[1]
+    height = q_parts[0].shape[0]
+    width = p_ref.shape[1]
+    per_block = p_ref.shape[0] // (tp * dp)
+    pieces = per_block // height
+    for j in range(dp):
+        owner = me_dp ^ j
+        q_ref[pl.ds(pl.multiple_of(owner * height, height), height), :] = q_parts[j][...]
+        for k in range(tp):
+            base = (owner * tp + (me_tp ^ k)) * per_block
+            for piece in range(pieces):
+                col = (k * pieces + piece) * width
+                p_ref[pl.ds(pl.multiple_of(base + piece * height, height), height), :] = p_parts[j][
+                    :, col : col + width
+                ]
+
+
+def ffn_body(tp, rank, tile, *refs):
+    x_refs, (wu_ref, wd_ref, p_ref, q_ref), rest = refs[:tp], refs[tp : tp + 4], refs[tp + 4 :]
+    own_ref, send_refs, (x_all, hidden) = rest[0], rest[1:tp], rest[tp:]
+    count = x_refs[0].shape[0]
+    for k in range(tp):
+        x_all[k * count : (k + 1) * count, :] = x_refs[k][...]
+    lanes = lax.broadcasted_iota(jnp.int32, (1, p_ref.shape[1]), 1)
+    first_half = (lanes // rank) % 2 == 0
+    low = jnp.dot(x_all[...], p_ref[...], preferred_element_type=F32)
+    low = jnp.where(first_half, low, 0.0).astype(BF16)
+    for i in range(hidden.shape[1] // tile):
+        cols = slice(i * tile, (i + 1) * tile)
+        upper = jnp.dot(x_all[...], wu_ref[:, cols], preferred_element_type=F32)
+        upper += jnp.dot(low, q_ref[:, cols], preferred_element_type=F32)
+        hidden[:, cols] = gelu(upper).astype(BF16)
+    low = lax.dot_general(hidden[...], q_ref[...], NT, preferred_element_type=F32)
+    low = jnp.where(first_half, 0.0, low).astype(BF16)
+    for i in range(x_all.shape[1] // tile):
+        cols = slice(i * tile, (i + 1) * tile)
+        out = jnp.dot(hidden[...], wd_ref[:, cols], preferred_element_type=F32)
+        out += lax.dot_general(low, p_ref[cols, :], NT, preferred_element_type=F32)
+        own_ref[:, cols] = out[:count]
+        for k in range(1, tp):
+            send_refs[k - 1][:, cols] = out[k * count : (k + 1) * count].astype(BF16)
+
+
+def middle_body(tp, steps_ref, place_ref, lat_ref, mod_ref, *refs):
+    parts, (vel_ref, state_ref, out_ref) = refs[:tp], refs[tp:]
+    step = steps_ref[place_ref[2]]
+    total = parts[0][...]
+    for part in parts[1:]:
+        total += part[...].astype(F32)
+    vel = mod_row(mod_ref, 2, step) * total
+    state = lat_ref[...].astype(F32) + STEP_SIZE * vel
+    vel_ref[...] = vel
+    state_ref[...] = state
+    out_ref[...] = modulated(state, mod_row(mod_ref, 0, step + 1), mod_row(mod_ref, 1, step + 1))
+
+
+def last_body(tp, steps_ref, place_ref, state_ref, mod_ref, vel_ref, *refs):
+    parts, (vels_ref, out_ref) = refs[:tp], refs[tp:]
+    step = steps_ref[place_ref[2]] + 1
+    total = parts[0][...]
+    for part in parts[1:]:
+        total += part[...].astype(F32)
+    vel = mod_row(mod_ref, 2, step) * total
+    vels_ref[0] = vel_ref[...]
+    vels_ref[1] = vel
+    out_ref[...] = state_ref[...] + STEP_SIZE * vel
+
+
+def swap(x, axis, flip):
+    return lax.ppermute(x, axis, [(i, i ^ flip) for i in range(lax.axis_size(axis))])
+
+
+def fast(latents, step_index, mod_table, base_up, base_down, up_a, up_b, down_a, down_b):
+    tp, dp = lax.axis_size("tp"), lax.axis_size("dp")
+    count, width = latents.shape
+    hidden = base_up.shape[1]
+    rank = up_b.shape[0]
+    both = 2 * rank * dp
+    height = 2 * rank
+    image_rows = count * tp // step_index.shape[0]
+    me_tp, me_dp = lax.axis_index("tp"), lax.axis_index("dp")
+    place = jnp.stack([me_tp, me_dp, me_tp * count // image_rows]).astype(jnp.int32)
+    mods = jnp.transpose(mod_table, (1, 0, 2))
+
+    p_own, q_own = call(
+        functools.partial(pack_body, dp, rank),
+        (shape((height, up_a.shape[0] // height * both)), shape((height, hidden))),
+        [VMEM] * 4,
+        (VMEM, VMEM),
+        "pack_factors",
+    )(up_a.T, down_b, up_b, down_a.T)
+    normed = call(
+        norm_body, shape((count, width)), [SMEM, SMEM, VMEM, VMEM], VMEM, "first_norm"
+    )(step_index, place, latents, mods)
+
+    p_line = [p_own] + [swap(p_own, "tp", k) for k in range(1, tp)]
+    x_parts = [normed] + [swap(normed, "tp", k) for k in range(1, tp)]
+    q_far = swap(q_own, "dp", 2)
+    merged_up = fetch(base_up, "fetch_up")
+    p_line = jnp.concatenate(p_line, axis=1)
+    p_far = swap(p_line, "dp", 2)
+    merged_down = fetch(base_down, "fetch_down")
+    near = [swap(a, "dp", 1) for a in (p_line, q_own, p_far, q_far)]
+    p_all, q_all = call(
+        functools.partial(assemble_body, tp, dp),
+        (shape((width, both)), shape((both, hidden))),
+        [SMEM] + [VMEM] * (2 * dp),
+        (VMEM, VMEM),
+        "assemble_factors",
+    )(place, p_line, near[0], p_far, near[2], q_own, near[1], q_far, near[3])
+
+    wu = pltpu.with_memory_space_constraint(merged_up, pltpu.VMEM)
+    wd = pltpu.with_memory_space_constraint(merged_down, pltpu.VMEM)
+
+    def block(parts, name):
+        rows = count * tp
+        return call(
+            functools.partial(ffn_body, tp, rank, 1024),
+            (shape((count, width), F32),) + (shape((count, width)),) * (tp - 1),
+            [VMEM] * (tp + 4),
+            (VMEM,) * tp,
+            name,
+            [pltpu.VMEM((rows, width), BF16), pltpu.VMEM((rows, hidden), BF16)],
+            flops=4 * rows * width * hidden,
+            bytes_accessed=4 * width * hidden,
+        )(*parts, wu, wd, p_all, q_all)
+
+    def exchange(parts):
+        return [parts[0]] + [swap(part, "tp", k) for k, part in enumerate(parts[1:], 1)]
+
+    sums = exchange(block(x_parts, "block_first"))
+    vel, state, normed = call(
+        functools.partial(middle_body, tp),
+        (shape((count, width), F32), shape((count, width), F32), shape((count, width))),
+        [SMEM, SMEM] + [VMEM] * (2 + tp),
+        (VMEM,) * 3,
+        "first_update",
+    )(step_index, place, latents, mods, *sums)
+    x_parts = [normed] + [swap(normed, "tp", k) for k in range(1, tp)]
+    sums = exchange(block(x_parts, "block_second"))
+    return call(
+        functools.partial(last_body, tp),
+        (shape((2, count, width), F32), shape((count, width), F32)),
+        [SMEM, SMEM] + [VMEM] * (3 + tp),
+        (VMEM,) * 2,
+        "second_update",
+    )(step_index, place, state, mods, vel, *sums)
 
 
 def normalize(state, shift, scale):
@@ -13,7 +263,7 @@
     return (centered * lax.rsqrt(spread + 1e-06) * (1.0 + scale) + shift).astype(jnp.bfloat16)
 
 
-def local(latents, step_index, mod_table, base_up, base_down, up_a, up_b, down_a, down_b):
+def plain(latents, step_index, mod_table, base_up, base_down, up_a, up_b, down_a, down_b):
     full_up_a, full_down_b = (
         lax.all_gather(up_a, ("dp", "tp"), axis=0, tiled=True),
         lax.all_gather(down_b, ("dp", "tp"), axis=1, tiled=True),
@@ -74,6 +324,22 @@
 
 
 def solution(mesh):
+    tp, dp = mesh.shape["tp"], mesh.shape["dp"]
+
+    def local(*args):
+        latents, step_index, mod_table, base_up, base_down, up_a, up_b = args[:7]
+        whole_tiles = (
+            tp == 4
+            and dp == 4
+            and latents.shape[0] % 16 == 0
+            and base_up.shape[1] % 1024 == 0
+            and base_up.shape[0] % 1024 == 0
+            and up_b.shape[0] % 16 == 0
+            and up_a.shape[0] % (2 * up_b.shape[0]) == 0
+            and (latents.shape[0] * tp // step_index.shape[0]) % latents.shape[0] == 0
+        )
+        return (fast if whole_tiles else plain)(*args)
+
     return jax.shard_map(
         local,
         mesh=mesh,

time: 295 us -> 148 us (0.50)
  blocking collectives: 103 us -> 0 us
  matrix products: 71.5 us -> 0 us
  waiting for transfers between devices: 99.5 us -> 39.8 us
  local copies, waits for them, and re-layouts: 2.73 us -> 50.2 us
  starting transfers between devices: 0.3 us -> 30.2 us
  Pallas kernels: 0 us -> 26 us
  between operations: 14.2 us -> 0.84 us
  other arithmetic: 3.84 us -> 0.08 us
    all_gather x5 -> x0, blocking collectives: 103 us -> none  [the longest x1 34.6 us: local(): lax.all_gather(down_b, ('dp', 'tp'), axis=1, tiled=True)]
    dot_general x10 -> x0, matrix products: 71.5 us -> none  [the longest x2 36.5 us: project(): return jnp.dot(hidden, merged_down, preferred_element_type=jnp.float32)]
    psum x1 -> x0, waiting for transfers between devices: 68 us -> none  [local(): first = gate * lax.psum(project(normed), 'tp')]
    unnamed x14 -> x41, local copies, waits for them, and re-layouts: 1.12 us -> 50.2 us
    ppermute x0 -> x21, waiting for transfers between devices: none -> 39.8 us  [swap(): lax.ppermute(x, axis, [(i, i ^ flip) for i in range(lax.axis_size(axis))])]
    reduce_scatter x1 -> x0, waiting for transfers between devices: 31.5 us -> none  [local(): lax.psum_scatter(project(normed), 'tp', scatter_dimension=0, tiled=True)]
    ppermute x0 -> x21, starting transfers between devices: none -> 30.2 us  [swap(): lax.ppermute(x, axis, [(i, i ^ flip) for i in range(lax.axis_size(axis))])]
    pallas_call x0 -> x9, Pallas kernels: none -> 26 us  [the longest x2 18.9 us: block(): call(functools.partial(ffn_body, tp, rank, 1024), (shape((count, width),...]
  transfers between devices with their start and end apart: 2 -> 21, of which waited for: 2 -> 8; matrix products, arithmetic and copies ran while one was open for 1% -> 0% of each run, Pallas kernels for 0% -> 3%
where the time goes in v1:
time: 148 us; the launch traced here: 147 us
  local copies, waits for them, and re-layouts  50.2 us (34%)
  waiting for transfers between devices  39.8 us (27%)
  starting transfers between devices  30.2 us (20%)
  Pallas kernels  26 us (18%)
    unnamed x41, local copies, waits for them, and re-layouts  50.2 us
    ppermute x21, waiting for transfers between devices, swap(): lax.ppermute(x, axis, [(i, i ^ flip) for i in range(lax.axis_size(axis))])  39.8 us
    ppermute x21, starting transfers between devices, swap(): lax.ppermute(x, axis, [(i, i ^ flip) for i in range(lax.axis_size(axis))])  30.2 us
    pallas_call x2, Pallas kernels, block(): call(functools.partial(ffn_body, tp, rank, 1024), (shape((count, width),...  18.9 us
  transfers between devices with their start and end apart: 21, of which 8 were waited for; matrix products, arithmetic and copies ran while one was open for 0% of the time, Pallas kernels for 3%

profile of v1, /device:TPU:0, one launch (start us, length us, event | category | flops | bytes accessed | tf_op | source)
XLA Modules:
  0.0 147.1 jit_solution(5466009721200675199)
XLA Ops:
  0.6 0.9 copy-done.13
  1.5 0.9 copy-done.14
  2.4 0.8 copy-done.15
  3.2 0.8 copy-done.16
  3.9 0.2 pack_factors.1
  4.1 5.1 %collective-permute-start.5 = (bf16[32,768]{1,0:T(8,128)(2,1)S(1)}, bf16[32,768]{1,0:T(8,128)(2,1)S(1)}, u32[]{:S(2)}, u32[]{:S(2)}) collective-permute-start(bf16[32,768]{1,0:T(8,128)(2,1)S(1)} %get-tuple-element.17), channel_id=1, source_target_pairs={{0,3},{1,2},{2,1},{3,0},{4,7},{5,6},{6,5},{7,4},{8,11},{9,10},{10,... | collective-permute-start | bytes 147464 | tf_op jit(solution)/shard_map/ppermute | solution.py:179
  9.2 0.6 collective-permute-start.3
  9.9 1.6 %collective-permute-start.10 = (bf16[32,3072]{1,0:T(8,128)(2,1)S(1)}, bf16[32,3072]{1,0:T(8,128)(2,1)S(1)}, u32[]{:S(2)}, u32[]{:S(2)}) collective-permute-start(bf16[32,3072]{1,0:T(8,128)(2,1)S(1)} %get-tuple-element.18.refs_4_), channel_id=1, source_target_pairs={{0,8},{4,12},{8,0},{12,4},{1,9},{5,13},{9,1},{13,5},{2,10},{6,14},... | collective-permute-start | bytes 589832 | tf_op jit(solution)/shard_map/ppermute | solution.py:179
  11.5 1.8 %collective-permute-done.3 = bf16[32,768]{1,0:T(8,128)(2,1)S(1)} collective-permute-done((bf16[32,768]{1,0:T(8,128)(2,1)S(1)}, bf16[32,768]{1,0:T(8,128)(2,1)S(1)}, u32[]{:S(2)}, u32[]{:S(2)}) %collective-permute-start.3) | collective-permute-done | bytes 49184 | tf_op jit(solution)/shard_map/ppermute | solution.py:179
  13.4 0.9 collective-permute-done.4
  14.3 1.6 %collective-permute-start.7 = (bf16[32,3072]{1,0:T(8,128)(2,1)S(1)}, bf16[32,3072]{1,0:T(8,128)(2,1)S(1)}, u32[]{:S(2)}, u32[]{:S(2)}) collective-permute-start(bf16[32,3072]{1,0:T(8,128)(2,1)S(1)} %constant_dynamic-update-slice_fusion.refs_0_), channel_id=1, source_target_pairs={{0,8},{4,12},{8,0},{12,4},{1,9},{5,13},{9,1},{13,5},{2,10},{6,14},... | collective-permute-start | bytes 589832 | tf_op jit(solution)/shard_map/ppermute | solution.py:179
  15.8 0.5 collective-permute-start.6
  16.3 0.1 pad_add_fusion.place_ref
  16.4 0.9 copy-done.9
  17.3 0.9 copy-done.11
  18.2 0.7 copy-done.17
  18.9 0.8 first_norm.1.refs_0_
  19.7 2.2 %collective-permute-start.2 = (bf16[32,3072]{1,0:T(8,128)(2,1)S(1)}, bf16[32,3072]{1,0:T(8,128)(2,1)S(1)}, u32[]{:S(2)}, u32[]{:S(2)}) collective-permute-start(bf16[32,3072]{1,0:T(8,128)(2,1)S(1)} %first_norm.1.refs_0_), channel_id=1, source_target_pairs={{0,3},{1,2},{2,1},{3,0},{4,7},{5,6},{6,5},{7,4},{8,11},{9,10},{10,... | collective-permute-start | bytes 589832 | tf_op jit(solution)/shard_map/ppermute | solution.py:179
  21.9 0.5 collective-permute-start.8
  22.5 2.2 %collective-permute-start = (bf16[32,3072]{1,0:T(8,128)(2,1)S(1)}, bf16[32,3072]{1,0:T(8,128)(2,1)S(1)}, u32[]{:S(2)}, u32[]{:S(2)}) collective-permute-start(bf16[32,3072]{1,0:T(8,128)(2,1)S(1)} %first_norm.1.refs_0_), channel_id=1, source_target_pairs={{0,1},{1,0},{2,3},{3,2},{4,5},{5,4},{6,7},{7,6},{8,9},{9,8},{10,11... | collective-permute-start | bytes 589832 | tf_op jit(solution)/shard_map/ppermute | solution.py:179
  24.7 6.4 %copy-done.5 = bf16[3072,3072]{1,0:T(8,128)(2,1)S(1)} copy-done((bf16[3072,3072]{1,0:T(8,128)(2,1)S(1)}, bf16[3072,3072]{1,0:T(8,128)(2,1)}, u32[]{:S(2)}) %copy-start.5) | copy-done | bytes 18874392
  31.1 1.3 fetch_up.1.refs_4_
  32.4 6.5 %copy-done = bf16[3072,3072]{1,0:T(8,128)(2,1)} copy-done((bf16[3072,3072]{1,0:T(8,128)(2,1)}, bf16[3072,3072]{1,0:T(8,128)(2,1)S(1)}, u32[]{:S(2)}) %copy-start) | copy-done | bytes 18874392
  38.9 6.4 %copy-done.6 = bf16[3072,3072]{1,0:T(8,128)(2,1)S(1)} copy-done((bf16[3072,3072]{1,0:T(8,128)(2,1)S(1)}, bf16[3072,3072]{1,0:T(8,128)(2,1)}, u32[]{:S(2)}) %copy-start.6) | copy-done | bytes 18874392
  45.3 1.3 fetch_down.1.refs_5_
  46.6 0.8 assemble_factors.1
  47.5 1.4 copy-done.7
  48.9 1.6 %copy-done.8 = bf16[128,3072]{1,0:T(8,128)(2,1)} copy-done((bf16[128,3072]{1,0:T(8,128)(2,1)}, bf16[128,3072]{1,0:T(8,128)(2,1)S(1)}, u32[]{:S(2)}) %copy-start.8) | copy-done | bytes 786456
  50.5 9.4 %copy-done.1 = bf16[3072,3072]{1,0:T(8,128)(2,1)S(1)} copy-done((bf16[3072,3072]{1,0:T(8,128)(2,1)S(1)}, bf16[3072,3072]{1,0:T(8,128)(2,1)}, u32[]{:S(2)}) %copy-start.1) | copy-done | bytes 18874392
  60.0 9.4 %block_first.1 = (f32[32,3072]{1,0:T(8,128)S(1)}, bf16[32,3072]{1,0:T(8,128)(2,1)S(1)}, bf16[32,3072]{1,0:T(8,128)(2,1)S(1)}, bf16[32,3072]{1,0:T(8,128)(2,1)S(1)}) custom-call(bf16[32,3072]{1,0:T(8,128)(2,1)S(1)} %first_norm.1.refs_0_, bf16[32,3072]{1,0:T(8,128)(2,1)S(1)} %collective-permute-done.refs_1_, ...), custom_call_target="tpu_custom_call" | custom-call | flops 4831838208 | bytes 37748736 | tf_op jit(solution)/shard_map/block_first/pallas_call | solution.py:226
  69.3 0.1 collective-permute-start.12
  69.4 2.7 %collective-permute-start.13 = (bf16[32,3072]{1,0:T(8,128)(2,1)S(1)}, bf16[32,3072]{1,0:T(8,128)(2,1)S(1)}, u32[]{:S(2)}, u32[]{:S(2)}) collective-permute-start(bf16[32,3072]{1,0:T(8,128)(2,1)S(1)} %get-tuple-element.23), channel_id=1, source_target_pairs={{0,2},{1,3},{2,0},{3,1},{4,6},{5,7},{6,4},{7,5},{8,10},{9,11},{10,... | collective-permute-start | bytes 589832 | tf_op jit(solution)/shard_map/ppermute | solution.py:179
  72.1 1.7 %collective-permute-start.14 = (bf16[32,3072]{1,0:T(8,128)(2,1)S(1)}, bf16[32,3072]{1,0:T(8,128)(2,1)S(1)}, u32[]{:S(2)}, u32[]{:S(2)}) collective-permute-start(bf16[32,3072]{1,0:T(8,128)(2,1)S(1)} %get-tuple-element.24), channel_id=1, source_target_pairs={{0,3},{1,2},{2,1},{3,0},{4,7},{5,6},{6,5},{7,4},{8,11},{9,10},{10,... | collective-permute-start | bytes 589832 | tf_op jit(solution)/shard_map/ppermute | solution.py:179
  73.8 5.2 %collective-permute-done.12.refs_1_ = bf16[32,3072]{1,0:T(8,128)(2,1)S(1)} collective-permute-done((bf16[32,3072]{1,0:T(8,128)(2,1)S(1)}, bf16[32,3072]{1,0:T(8,128)(2,1)S(1)}, u32[]{:S(2)}, u32[]{:S(2)}) %collective-permute-start.12) | collective-permute-done | bytes 196640 | tf_op jit(solution)/shard_map/ppermute | solution.py:179
  79.0 7.6 %collective-permute-done.13.refs_2_ = bf16[32,3072]{1,0:T(8,128)(2,1)S(1)} collective-permute-done((bf16[32,3072]{1,0:T(8,128)(2,1)S(1)}, bf16[32,3072]{1,0:T(8,128)(2,1)S(1)}, u32[]{:S(2)}, u32[]{:S(2)}) %collective-permute-start.13) | collective-permute-done | bytes 196640 | tf_op jit(solution)/shard_map/ppermute | solution.py:179
  86.7 0.9 first_update.1
  87.6 2.6 %collective-permute-start.17 = (bf16[32,3072]{1,0:T(8,128)(2,1)S(1)}, bf16[32,3072]{1,0:T(8,128)(2,1)S(1)}, u32[]{:S(2)}, u32[]{:S(2)}) collective-permute-start(bf16[32,3072]{1,0:T(8,128)(2,1)S(1)} %get-tuple-element.27.refs_0_), channel_id=1, source_target_pairs={{0,3},{1,2},{2,1},{3,0},{4,7},{5,6},{6,5},{7,4},{8,11},{9,10},{10,... | collective-permute-start | bytes 589832 | tf_op jit(solution)/shard_map/ppermute | solution.py:179
  90.2 4.3 %collective-permute-start.16 = (bf16[32,3072]{1,0:T(8,128)(2,1)S(1)}, bf16[32,3072]{1,0:T(8,128)(2,1)S(1)}, u32[]{:S(2)}, u32[]{:S(2)}) collective-permute-start(bf16[32,3072]{1,0:T(8,128)(2,1)S(1)} %get-tuple-element.27.refs_0_), channel_id=1, source_target_pairs={{0,2},{1,3},{2,0},{3,1},{4,6},{5,7},{6,4},{7,5},{8,10},{9,11},{10,... | collective-permute-start | bytes 589832 | tf_op jit(solution)/shard_map/ppermute | solution.py:179
  94.5 2.5 %collective-permute-done.17.refs_3_ = bf16[32,3072]{1,0:T(8,128)(2,1)S(1)} collective-permute-done((bf16[32,3072]{1,0:T(8,128)(2,1)S(1)}, bf16[32,3072]{1,0:T(8,128)(2,1)S(1)}, u32[]{:S(2)}, u32[]{:S(2)}) %collective-permute-start.17) | collective-permute-done | bytes 196640 | tf_op jit(solution)/shard_map/ppermute | solution.py:179
  97.0 9.3 %collective-permute-done.16.refs_2_ = bf16[32,3072]{1,0:T(8,128)(2,1)S(1)} collective-permute-done((bf16[32,3072]{1,0:T(8,128)(2,1)S(1)}, bf16[32,3072]{1,0:T(8,128)(2,1)S(1)}, u32[]{:S(2)}, u32[]{:S(2)}) %collective-permute-start.16) | collective-permute-done | bytes 196640 | tf_op jit(solution)/shard_map/ppermute | solution.py:179
  106.4 6.4 %copy-done.2 = bf16[3072,3072]{1,0:T(8,128)(2,1)S(1)} copy-done((bf16[3072,3072]{1,0:T(8,128)(2,1)S(1)}, bf16[3072,3072]{1,0:T(8,128)(2,1)}, u32[]{:S(2)}) %copy-start.2) | copy-done | bytes 18874392
  112.8 6.4 %copy-done.4 = bf16[3072,3072]{1,0:T(8,128)(2,1)S(1)} copy-done((bf16[3072,3072]{1,0:T(8,128)(2,1)S(1)}, bf16[3072,3072]{1,0:T(8,128)(2,1)}, u32[]{:S(2)}) %copy-start.4) | copy-done | bytes 18874392
  119.1 9.5 %block_second.1 = (f32[32,3072]{1,0:T(8,128)S(1)}, bf16[32,3072]{1,0:T(8,128)(2,1)S(1)}, bf16[32,3072]{1,0:T(8,128)(2,1)S(1)}, bf16[32,3072]{1,0:T(8,128)(2,1)S(1)}) custom-call(bf16[32,3072]{1,0:T(8,128)(2,1)S(1)} %get-tuple-element.27.refs_0_, bf16[32,3072]{1,0:T(8,128)(2,1)S(1)} %collective-permute-done.15.refs_1_, ...), custom_call_target="tpu_custom_call" | custom-call | flops 4831838208 | bytes 37748736 | tf_op jit(solution)/shard_map/block_second/pallas_call | solution.py:226
  128.7 2.7 %collective-permute-start.19 = (bf16[32,3072]{1,0:T(8,128)(2,1)S(1)}, bf16[32,3072]{1,0:T(8,128)(2,1)S(1)}, u32[]{:S(2)}, u32[]{:S(2)}) collective-permute-start(bf16[32,3072]{1,0:T(8,128)(2,1)S(1)} %get-tuple-element.30), channel_id=1, source_target_pairs={{0,2},{1,3},{2,0},{3,1},{4,6},{5,7},{6,4},{7,5},{8,10},{9,11},{10,... | collective-permute-start | bytes 589832 | tf_op jit(solution)/shard_map/ppermute | solution.py:179
  131.4 1.7 %collective-permute-start.20 = (bf16[32,3072]{1,0:T(8,128)(2,1)S(1)}, bf16[32,3072]{1,0:T(8,128)(2,1)S(1)}, u32[]{:S(2)}, u32[]{:S(2)}) collective-permute-start(bf16[32,3072]{1,0:T(8,128)(2,1)S(1)} %get-tuple-element.31), channel_id=1, source_target_pairs={{0,3},{1,2},{2,1},{3,0},{4,7},{5,6},{6,5},{7,4},{8,11},{9,10},{10,... | collective-permute-start | bytes 589832 | tf_op jit(solution)/shard_map/ppermute | solution.py:179
  133.1 4.5 %collective-permute-done.18.refs_1_ = bf16[32,3072]{1,0:T(8,128)(2,1)S(1)} collective-permute-done((bf16[32,3072]{1,0:T(8,128)(2,1)S(1)}, bf16[32,3072]{1,0:T(8,128)(2,1)S(1)}, u32[]{:S(2)}, u32[]{:S(2)}) %collective-permute-start.18) | collective-permute-done | bytes 196640 | tf_op jit(solution)/shard_map/ppermute | solution.py:179
  137.6 7.8 %collective-permute-done.19.refs_2_ = bf16[32,3072]{1,0:T(8,128)(2,1)S(1)} collective-permute-done((bf16[32,3072]{1,0:T(8,128)(2,1)S(1)}, bf16[32,3072]{1,0:T(8,128)(2,1)S(1)}, u32[]{:S(2)}, u32[]{:S(2)}) %collective-permute-start.19) | collective-permute-done | bytes 196640 | tf_op jit(solution)/shard_map/ppermute | solution.py:179
  145.4 1.7 %second_update.1 = (f32[2,32,3072]{2,1,0:T(8,128)}, f32[32,3072]{1,0:T(8,128)}) custom-call(s32[2]{0:T(128)S(1)} %copy-done.18, s32[3]{0:T(128)S(1)} %pad_add_fusion.place_ref, f32[32,3072]{1,0:T(8,128)S(1)} %get-tuple-element.25.state_ref, f32[3,4,3072]{2,1,0:T(4,128)S(1)} %bitcast.8, f32[32,3072]{1,0:T(8,128)S(1)} %get-tuple-element.26.vel_ref, ...), custom_call_target="tpu_custom_call" | custom-call | tf_op jit(solution)/shard_map/second_update/pallas_call | solution.py:250
  (46 shorter events, 0.2 us)
Async XLA Ops:
  0.6 0.9 copy-start.13
  1.5 0.9 copy-start.14
  2.4 0.8 copy-start.15
  3.2 0.8 copy-start.16
  4.1 10.1 %collective-permute-start.5 = (bf16[32,768]{1,0:T(8,128)(2,1)S(1)}, bf16[32,768]{1,0:T(8,128)(2,1)S(1)}, u32[]{:S(2)}, u32[]{:S(2)}) collective-permute-start(bf16[32,768]{1,0:T(8,128)(2,1)S(1)} %get-tuple-element.17), channel_id=1, source_target_pairs={{0,3},{1,2},{2,1},{3,0},{4,7},{5,6},{6,5},{7,4},{8,11},{9,10},{10,... | collective-permute-start | bytes 147464 | tf_op jit(solution)/shard_map/ppermute | solution.py:179
  9.2 5.0 %collective-permute-start.4 = (bf16[32,768]{1,0:T(8,128)(2,1)S(1)}, bf16[32,768]{1,0:T(8,128)(2,1)S(1)}, u32[]{:S(2)}, u32[]{:S(2)}) collective-permute-start(bf16[32,768]{1,0:T(8,128)(2,1)S(1)} %get-tuple-element.17), channel_id=1, source_target_pairs={{0,2},{1,3},{2,0},{3,1},{4,6},{5,7},{6,4},{7,5},{8,10},{9,11},{10,... | collective-permute-start | bytes 147464 | tf_op jit(solution)/shard_map/ppermute | solution.py:179
  9.2 4.1 %collective-permute-start.3 = (bf16[32,768]{1,0:T(8,128)(2,1)S(1)}, bf16[32,768]{1,0:T(8,128)(2,1)S(1)}, u32[]{:S(2)}, u32[]{:S(2)}) collective-permute-start(bf16[32,768]{1,0:T(8,128)(2,1)S(1)} %get-tuple-element.17), channel_id=1, source_target_pairs={{0,1},{1,0},{2,3},{3,2},{4,5},{5,4},{6,7},{7,6},{8,9},{9,8},{10,11... | collective-permute-start | bytes 147464 | tf_op jit(solution)/shard_map/ppermute | solution.py:179
  9.9 12.0 %collective-permute-start.10 = (bf16[32,3072]{1,0:T(8,128)(2,1)S(1)}, bf16[32,3072]{1,0:T(8,128)(2,1)S(1)}, u32[]{:S(2)}, u32[]{:S(2)}) collective-permute-start(bf16[32,3072]{1,0:T(8,128)(2,1)S(1)} %get-tuple-element.18.refs_4_), channel_id=1, source_target_pairs={{0,8},{4,12},{8,0},{12,4},{1,9},{5,13},{9,1},{13,5},{2,10},{6,14},... | collective-permute-start | bytes 589832 | tf_op jit(solution)/shard_map/ppermute | solution.py:179
  14.3 7.6 %collective-permute-start.7 = (bf16[32,3072]{1,0:T(8,128)(2,1)S(1)}, bf16[32,3072]{1,0:T(8,128)(2,1)S(1)}, u32[]{:S(2)}, u32[]{:S(2)}) collective-permute-start(bf16[32,3072]{1,0:T(8,128)(2,1)S(1)} %constant_dynamic-update-slice_fusion.refs_0_), channel_id=1, source_target_pairs={{0,8},{4,12},{8,0},{12,4},{1,9},{5,13},{9,1},{13,5},{2,10},{6,14},... | collective-permute-start | bytes 589832 | tf_op jit(solution)/shard_map/ppermute | solution.py:179
  15.8 6.6 %collective-permute-start.9 = (bf16[32,3072]{1,0:T(8,128)(2,1)S(1)}, bf16[32,3072]{1,0:T(8,128)(2,1)S(1)}, u32[]{:S(2)}, u32[]{:S(2)}) collective-permute-start(bf16[32,3072]{1,0:T(8,128)(2,1)S(1)} %get-tuple-element.18.refs_4_), channel_id=1, source_target_pairs={{0,4},{4,0},{8,12},{12,8},{1,5},{5,1},{9,13},{13,9},{2,6},{6,2},{1... | collective-permute-start | bytes 589832 | tf_op jit(solution)/shard_map/ppermute | solution.py:179
  15.8 6.7 %collective-permute-start.6 = (bf16[32,3072]{1,0:T(8,128)(2,1)S(1)}, bf16[32,3072]{1,0:T(8,128)(2,1)S(1)}, u32[]{:S(2)}, u32[]{:S(2)}) collective-permute-start(bf16[32,3072]{1,0:T(8,128)(2,1)S(1)} %constant_dynamic-update-slice_fusion.refs_0_), channel_id=1, source_target_pairs={{0,4},{4,0},{8,12},{12,8},{1,5},{5,1},{9,13},{13,9},{2,6},{6,2},{1... | collective-permute-start | bytes 589832 | tf_op jit(solution)/shard_map/ppermute | solution.py:179
  16.4 0.9 copy-start.9
  17.3 0.9 copy-start.11
  18.2 0.7 copy-start.17
  19.7 30.8 %collective-permute-start.2 = (bf16[32,3072]{1,0:T(8,128)(2,1)S(1)}, bf16[32,3072]{1,0:T(8,128)(2,1)S(1)}, u32[]{:S(2)}, u32[]{:S(2)}) collective-permute-start(bf16[32,3072]{1,0:T(8,128)(2,1)S(1)} %first_norm.1.refs_0_), channel_id=1, source_target_pairs={{0,3},{1,2},{2,1},{3,0},{4,7},{5,6},{6,5},{7,4},{8,11},{9,10},{10,... | collective-permute-start | bytes 589832 | tf_op jit(solution)/shard_map/ppermute | solution.py:179
  21.9 24.7 %collective-permute-start.11 = (bf16[32,3072]{1,0:T(8,128)(2,1)S(1)}, bf16[32,3072]{1,0:T(8,128)(2,1)S(1)}, u32[]{:S(2)}, u32[]{:S(2)}) collective-permute-start(bf16[32,3072]{1,0:T(8,128)(2,1)S(1)} %collective-permute-done.10.refs_6_), channel_id=1, source_target_pairs={{0,4},{4,0},{8,12},{12,8},{1,5},{5,1},{9,13},{13,9},{2,6},{6,2},{1... | collective-permute-start | bytes 589832 | tf_op jit(solution)/shard_map/ppermute | solution.py:179
  21.9 24.7 %collective-permute-start.8 = (bf16[32,3072]{1,0:T(8,128)(2,1)S(1)}, bf16[32,3072]{1,0:T(8,128)(2,1)S(1)}, u32[]{:S(2)}, u32[]{:S(2)}) collective-permute-start(bf16[32,3072]{1,0:T(8,128)(2,1)S(1)} %collective-permute-done.7.refs_2_), channel_id=1, source_target_pairs={{0,4},{4,0},{8,12},{12,8},{1,5},{5,1},{9,13},{13,9},{2,6},{6,2},{1... | collective-permute-start | bytes 589832 | tf_op jit(solution)/shard_map/ppermute | solution.py:179
  22.4 28.1 %collective-permute-start.1 = (bf16[32,3072]{1,0:T(8,128)(2,1)S(1)}, bf16[32,3072]{1,0:T(8,128)(2,1)S(1)}, u32[]{:S(2)}, u32[]{:S(2)}) collective-permute-start(bf16[32,3072]{1,0:T(8,128)(2,1)S(1)} %first_norm.1.refs_0_), channel_id=1, source_target_pairs={{0,2},{1,3},{2,0},{3,1},{4,6},{5,7},{6,4},{7,5},{8,10},{9,11},{10,... | collective-permute-start | bytes 589832 | tf_op jit(solution)/shard_map/ppermute | solution.py:179
  22.5 28.0 %collective-permute-start = (bf16[32,3072]{1,0:T(8,128)(2,1)S(1)}, bf16[32,3072]{1,0:T(8,128)(2,1)S(1)}, u32[]{:S(2)}, u32[]{:S(2)}) collective-permute-start(bf16[32,3072]{1,0:T(8,128)(2,1)S(1)} %first_norm.1.refs_0_), channel_id=1, source_target_pairs={{0,1},{1,0},{2,3},{3,2},{4,5},{5,4},{6,7},{7,6},{8,9},{9,8},{10,11... | collective-permute-start | bytes 589832 | tf_op jit(solution)/shard_map/ppermute | solution.py:179
  24.7 6.4 %copy-start.5 = (bf16[3072,3072]{1,0:T(8,128)(2,1)S(1)}, bf16[3072,3072]{1,0:T(8,128)(2,1)}, u32[]{:S(2)}) copy-start(bf16[3072,3072]{1,0:T(8,128)(2,1)} %src_ref.2) | copy-start | bytes 56623108
  32.4 6.5 %copy-start = (bf16[3072,3072]{1,0:T(8,128)(2,1)}, bf16[3072,3072]{1,0:T(8,128)(2,1)S(1)}, u32[]{:S(2)}) copy-start(bf16[3072,3072]{1,0:T(8,128)(2,1)S(1)} %fetch_up.1.refs_4_) | copy-start | bytes 56623108
  38.9 6.4 %copy-start.6 = (bf16[3072,3072]{1,0:T(8,128)(2,1)S(1)}, bf16[3072,3072]{1,0:T(8,128)(2,1)}, u32[]{:S(2)}) copy-start(bf16[3072,3072]{1,0:T(8,128)(2,1)} %src_ref.3) | copy-start | bytes 56623108
  46.6 22.7 %copy-start.3 = (bf16[3072,3072]{1,0:T(8,128)(2,1)}, bf16[3072,3072]{1,0:T(8,128)(2,1)S(1)}, u32[]{:S(2)}) copy-start(bf16[3072,3072]{1,0:T(8,128)(2,1)S(1)} %fetch_down.1.refs_5_) | copy-start | bytes 56623108
  47.5 1.4 copy-start.7
  48.9 1.6 %copy-start.8 = (bf16[128,3072]{1,0:T(8,128)(2,1)}, bf16[128,3072]{1,0:T(8,128)(2,1)S(1)}, u32[]{:S(2)}) copy-start(bf16[128,3072]{1,0:T(8,128)(2,1)S(1)} %get-tuple-element.20.refs_7_) | copy-start | bytes 2359300
  50.5 9.4 %copy-start.1 = (bf16[3072,3072]{1,0:T(8,128)(2,1)S(1)}, bf16[3072,3072]{1,0:T(8,128)(2,1)}, u32[]{:S(2)}) copy-start(bf16[3072,3072]{1,0:T(8,128)(2,1)} %copy-done) | copy-start | bytes 56623108
  60.0 26.7 %copy-start.10 = (f32[4,3,3072]{2,0,1:T(4,128)S(1)}, f32[4,3,3072]{2,0,1:T(4,128)}, u32[]{:S(2)}) copy-start(f32[4,3,3072]{2,0,1:T(4,128)} %param.11) | copy-start | bytes 442372
  60.0 26.7 %copy-start.12 = (bf16[32,3072]{1,0:T(8,128)(2,1)S(1)}, bf16[32,3072]{1,0:T(8,128)(2,1)}, u32[]{:S(2)}) copy-start(bf16[32,3072]{1,0:T(8,128)(2,1)} %lat_ref.3) | copy-start | bytes 589828
  60.0 26.7 %copy-start.18 = (s32[2]{0:T(128)S(1)}, s32[2]{0:T(128)}, u32[]{:S(2)}) copy-start(s32[2]{0:T(128)} %steps_ref.5) | copy-start | bytes 28
  69.3 9.7 %collective-permute-start.12 = (bf16[32,3072]{1,0:T(8,128)(2,1)S(1)}, bf16[32,3072]{1,0:T(8,128)(2,1)S(1)}, u32[]{:S(2)}, u32[]{:S(2)}) collective-permute-start(bf16[32,3072]{1,0:T(8,128)(2,1)S(1)} %get-tuple-element.22), channel_id=1, source_target_pairs={{0,1},{1,0},{2,3},{3,2},{4,5},{5,4},{6,7},{7,6},{8,9},{9,8},{10,11... | collective-permute-start | bytes 589832 | tf_op jit(solution)/shard_map/ppermute | solution.py:179
  69.4 17.2 %collective-permute-start.13 = (bf16[32,3072]{1,0:T(8,128)(2,1)S(1)}, bf16[32,3072]{1,0:T(8,128)(2,1)S(1)}, u32[]{:S(2)}, u32[]{:S(2)}) collective-permute-start(bf16[32,3072]{1,0:T(8,128)(2,1)S(1)} %get-tuple-element.23), channel_id=1, source_target_pairs={{0,2},{1,3},{2,0},{3,1},{4,6},{5,7},{6,4},{7,5},{8,10},{9,11},{10,... | collective-permute-start | bytes 589832 | tf_op jit(solution)/shard_map/ppermute | solution.py:179
  72.1 14.6 %collective-permute-start.14 = (bf16[32,3072]{1,0:T(8,128)(2,1)S(1)}, bf16[32,3072]{1,0:T(8,128)(2,1)S(1)}, u32[]{:S(2)}, u32[]{:S(2)}) collective-permute-start(bf16[32,3072]{1,0:T(8,128)(2,1)S(1)} %get-tuple-element.24), channel_id=1, source_target_pairs={{0,3},{1,2},{2,1},{3,0},{4,7},{5,6},{6,5},{7,4},{8,11},{9,10},{10,... | collective-permute-start | bytes 589832 | tf_op jit(solution)/shard_map/ppermute | solution.py:179
  87.6 9.4 %collective-permute-start.17 = (bf16[32,3072]{1,0:T(8,128)(2,1)S(1)}, bf16[32,3072]{1,0:T(8,128)(2,1)S(1)}, u32[]{:S(2)}, u32[]{:S(2)}) collective-permute-start(bf16[32,3072]{1,0:T(8,128)(2,1)S(1)} %get-tuple-element.27.refs_0_), channel_id=1, source_target_pairs={{0,3},{1,2},{2,1},{3,0},{4,7},{5,6},{6,5},{7,4},{8,11},{9,10},{10,... | collective-permute-start | bytes 589832 | tf_op jit(solution)/shard_map/ppermute | solution.py:179
  90.2 16.2 %collective-permute-start.16 = (bf16[32,3072]{1,0:T(8,128)(2,1)S(1)}, bf16[32,3072]{1,0:T(8,128)(2,1)S(1)}, u32[]{:S(2)}, u32[]{:S(2)}) collective-permute-start(bf16[32,3072]{1,0:T(8,128)(2,1)S(1)} %get-tuple-element.27.refs_0_), channel_id=1, source_target_pairs={{0,2},{1,3},{2,0},{3,1},{4,6},{5,7},{6,4},{7,5},{8,10},{9,11},{10,... | collective-permute-start | bytes 589832 | tf_op jit(solution)/shard_map/ppermute | solution.py:179
  94.5 11.9 %collective-permute-start.15 = (bf16[32,3072]{1,0:T(8,128)(2,1)S(1)}, bf16[32,3072]{1,0:T(8,128)(2,1)S(1)}, u32[]{:S(2)}, u32[]{:S(2)}) collective-permute-start(bf16[32,3072]{1,0:T(8,128)(2,1)S(1)} %get-tuple-element.27.refs_0_), channel_id=1, source_target_pairs={{0,1},{1,0},{2,3},{3,2},{4,5},{5,4},{6,7},{7,6},{8,9},{9,8},{10,11... | collective-permute-start | bytes 589832 | tf_op jit(solution)/shard_map/ppermute | solution.py:179
  106.4 6.4 %copy-start.2 = (bf16[3072,3072]{1,0:T(8,128)(2,1)S(1)}, bf16[3072,3072]{1,0:T(8,128)(2,1)}, u32[]{:S(2)}) copy-start(bf16[3072,3072]{1,0:T(8,128)(2,1)} %copy-done) | copy-start | bytes 56623108
  112.8 6.4 %copy-start.4 = (bf16[3072,3072]{1,0:T(8,128)(2,1)S(1)}, bf16[3072,3072]{1,0:T(8,128)(2,1)}, u32[]{:S(2)}) copy-start(bf16[3072,3072]{1,0:T(8,128)(2,1)} %copy-done.3) | copy-start | bytes 56623108
  128.6 9.0 %collective-permute-start.18 = (bf16[32,3072]{1,0:T(8,128)(2,1)S(1)}, bf16[32,3072]{1,0:T(8,128)(2,1)S(1)}, u32[]{:S(2)}, u32[]{:S(2)}) collective-permute-start(bf16[32,3072]{1,0:T(8,128)(2,1)S(1)} %get-tuple-element.29), channel_id=1, source_target_pairs={{0,1},{1,0},{2,3},{3,2},{4,5},{5,4},{6,7},{7,6},{8,9},{9,8},{10,11... | collective-permute-start | bytes 589832 | tf_op jit(solution)/shard_map/ppermute | solution.py:179
  128.7 16.7 %collective-permute-start.19 = (bf16[32,3072]{1,0:T(8,128)(2,1)S(1)}, bf16[32,3072]{1,0:T(8,128)(2,1)S(1)}, u32[]{:S(2)}, u32[]{:S(2)}) collective-permute-start(bf16[32,3072]{1,0:T(8,128)(2,1)S(1)} %get-tuple-element.30), channel_id=1, source_target_pairs={{0,2},{1,3},{2,0},{3,1},{4,6},{5,7},{6,4},{7,5},{8,10},{9,11},{10,... | collective-permute-start | bytes 589832 | tf_op jit(solution)/shard_map/ppermute | solution.py:179
  131.4 14.0 %collective-permute-start.20 = (bf16[32,3072]{1,0:T(8,128)(2,1)S(1)}, bf16[32,3072]{1,0:T(8,128)(2,1)S(1)}, u32[]{:S(2)}, u32[]{:S(2)}) collective-permute-start(bf16[32,3072]{1,0:T(8,128)(2,1)S(1)} %get-tuple-element.31), channel_id=1, source_target_pairs={{0,3},{1,2},{2,1},{3,0},{4,7},{5,6},{6,5},{7,4},{8,11},{9,10},{10,... | collective-permute-start | bytes 589832 | tf_op jit(solution)/shard_map/ppermute | solution.py:179

commit v2 on v1

--- a/solution.py
+++ b/solution.py
@@ -10,7 +10,7 @@
 NSTEPS = 4
 STEP_SIZE = -1.0 / NSTEPS
 BF16, F32 = jnp.bfloat16, jnp.float32
-VMEM_GRANT = 16 << 20
+VMEM_GRANT = 4 << 20
 VMEM = pl.BlockSpec(memory_space=pltpu.VMEM)
 SMEM = pl.BlockSpec(memory_space=pltpu.SMEM)
 HBM = pl.BlockSpec(memory_space=pltpu.HBM)
@@ -102,7 +102,7 @@
         name,
         [pltpu.SemaphoreType.DMA((parts,))],
         bytes_accessed=2 * src.size * src.dtype.itemsize,
-    )(src)
+    )(pltpu.with_memory_space_constraint(src, pltpu.HBM))
 
 
 def assemble_body(tp, dp, place_ref, *refs):
@@ -212,7 +212,7 @@
     near = [swap(a, "dp", 1) for a in (p_line, q_own, p_far, q_far)]
     p_all, q_all = call(
         functools.partial(assemble_body, tp, dp),
-        (shape((width, both)), shape((both, hidden))),
+        (pltpu.VMEM((width, both), BF16), pltpu.VMEM((both, hidden), BF16)),
         [SMEM] + [VMEM] * (2 * dp),
         (VMEM, VMEM),
         "assemble_factors",
@@ -220,6 +220,8 @@
 
     wu = pltpu.with_memory_space_constraint(merged_up, pltpu.VMEM)
     wd = pltpu.with_memory_space_constraint(merged_down, pltpu.VMEM)
+    p_all = pltpu.with_memory_space_constraint(p_all, pltpu.VMEM)
+    q_all = pltpu.with_memory_space_constraint(q_all, pltpu.VMEM)
 
     def block(parts, name):
         rows = count * tp

time: 148 us -> 112 us (0.76)
  local copies, waits for them, and re-layouts: 50.2 us -> 5.82 us
  Pallas kernels: 26 us -> 33.8 us
    unnamed x41 -> x23, local copies, waits for them, and re-layouts: 50.2 us -> 5.81 us
    pallas_call x2, Pallas kernels: 2.68 us -> 13 us  [fetch(): call(functools.partial(fetch_body, parts), pltpu.VMEM(src.shape, src.dtyp...]
    pallas_call x2, Pallas kernels: 18.9 us -> 16.3 us  [block(): call(functools.partial(ffn_body, tp, rank, 1024), (shape((count, width),...]
  transfers between devices with their start and end apart: 21 -> 21, of which waited for: 8 -> 9; matrix products, arithmetic and copies ran while one was open for 0% -> 0% of each run, Pallas kernels for 3% -> 13%
where the time goes in v2:
time: 112 us
  waiting for transfers between devices  41.2 us (37%)
  Pallas kernels  33.8 us (30%)
  starting transfers between devices  30 us (27%)
  local copies, waits for them, and re-layouts  5.82 us (5%)
    ppermute x21, waiting for transfers between devices, swap(): lax.ppermute(x, axis, [(i, i ^ flip) for i in range(lax.axis_size(axis))])  41.2 us
    ppermute x21, starting transfers between devices, swap(): lax.ppermute(x, axis, [(i, i ^ flip) for i in range(lax.axis_size(axis))])  30 us
    pallas_call x2, Pallas kernels, block(): call(functools.partial(ffn_body, tp, rank, 1024), (shape((count, width),...  16.3 us
    pallas_call x2, Pallas kernels, fetch(): call(functools.partial(fetch_body, parts), pltpu.VMEM(src.shape, src.dtyp...  13 us
    unnamed x23, local copies, waits for them, and re-layouts  5.81 us
  transfers between devices with their start and end apart: 21, of which 9 were waited for; matrix products, arithmetic and copies ran while one was open for 0% of the time, Pallas kernels for 13%

profile of v2, /device:TPU:0, one launch (start us, length us, event | category | flops | bytes accessed | tf_op | source)
XLA Modules:
  0.0 111.6 jit_solution(16441121120678555853)
XLA Ops:
  0.6 0.9 copy-done.4
  1.5 0.9 copy-done.5
  2.4 0.8 copy-done.6
  3.2 0.8 copy-done.7
  3.9 0.2 pack_factors.1
  4.1 5.1 %collective-permute-start.5 = (bf16[32,768]{1,0:T(8,128)(2,1)S(1)}, bf16[32,768]{1,0:T(8,128)(2,1)S(1)}, u32[]{:S(2)}, u32[]{:S(2)}) collective-permute-start(bf16[32,768]{1,0:T(8,128)(2,1)S(1)} %get-tuple-element.17), channel_id=1, source_target_pairs={{0,3},{1,2},{2,1},{3,0},{4,7},{5,6},{6,5},{7,4},{8,11},{9,10},{10,... | collective-permute-start | bytes 147464 | tf_op jit(solution)/shard_map/ppermute | solution.py:179
  9.2 0.6 collective-permute-start.3
  9.9 1.6 %collective-permute-start.10 = (bf16[32,3072]{1,0:T(8,128)(2,1)S(1)}, bf16[32,3072]{1,0:T(8,128)(2,1)S(1)}, u32[]{:S(2)}, u32[]{:S(2)}) collective-permute-start(bf16[32,3072]{1,0:T(8,128)(2,1)S(1)} %get-tuple-element.18.refs_4_), channel_id=1, source_target_pairs={{0,8},{4,12},{8,0},{12,4},{1,9},{5,13},{9,1},{13,5},{2,10},{6,14},... | collective-permute-start | bytes 589832 | tf_op jit(solution)/shard_map/ppermute | solution.py:179
  11.5 1.8 %collective-permute-done.3 = bf16[32,768]{1,0:T(8,128)(2,1)S(1)} collective-permute-done((bf16[32,768]{1,0:T(8,128)(2,1)S(1)}, bf16[32,768]{1,0:T(8,128)(2,1)S(1)}, u32[]{:S(2)}, u32[]{:S(2)}) %collective-permute-start.3) | collective-permute-done | bytes 49184 | tf_op jit(solution)/shard_map/ppermute | solution.py:179
  13.4 0.9 collective-permute-done.4
  14.2 0.0 collective-permute-done.5
  14.3 1.6 %collective-permute-start.7 = (bf16[32,3072]{1,0:T(8,128)(2,1)S(1)}, bf16[32,3072]{1,0:T(8,128)(2,1)S(1)}, u32[]{:S(2)}, u32[]{:S(2)}) collective-permute-start(bf16[32,3072]{1,0:T(8,128)(2,1)S(1)} %constant_dynamic-update-slice_fusion.refs_0_), channel_id=1, source_target_pairs={{0,8},{4,12},{8,0},{12,4},{1,9},{5,13},{9,1},{13,5},{2,10},{6,14},... | collective-permute-start | bytes 589832 | tf_op jit(solution)/shard_map/ppermute | solution.py:179
  15.8 0.0 collective-permute-start.9
  15.8 0.5 collective-permute-start.6
  16.3 0.1 pad_add_fusion.place_ref
  16.4 0.9 copy-done
  17.3 0.9 copy-done.2
  18.2 0.7 copy-done.8
  18.9 0.8 first_norm.1.refs_0_
  19.7 2.2 %collective-permute-start.2 = (bf16[32,3072]{1,0:T(8,128)(2,1)S(1)}, bf16[32,3072]{1,0:T(8,128)(2,1)S(1)}, u32[]{:S(2)}, u32[]{:S(2)}) collective-permute-start(bf16[32,3072]{1,0:T(8,128)(2,1)S(1)} %first_norm.1.refs_0_), channel_id=1, source_target_pairs={{0,3},{1,2},{2,1},{3,0},{4,7},{5,6},{6,5},{7,4},{8,11},{9,10},{10,... | collective-permute-start | bytes 589832 | tf_op jit(solution)/shard_map/ppermute | solution.py:179
  21.9 0.0 collective-permute-done.7.refs_2_
  21.9 0.5 collective-permute-start.8
  22.4 0.1 collective-permute-start.1
  22.5 0.0 collective-permute-done.6.refs_1_
  22.5 2.2 %collective-permute-start = (bf16[32,3072]{1,0:T(8,128)(2,1)S(1)}, bf16[32,3072]{1,0:T(8,128)(2,1)S(1)}, u32[]{:S(2)}, u32[]{:S(2)}) collective-permute-start(bf16[32,3072]{1,0:T(8,128)(2,1)S(1)} %first_norm.1.refs_0_), channel_id=1, source_target_pairs={{0,1},{1,0},{2,3},{3,2},{4,5},{5,4},{6,7},{7,6},{8,9},{9,8},{10,11... | collective-permute-start | bytes 589832 | tf_op jit(solution)/shard_map/ppermute | solution.py:179
  24.7 6.5 %fetch_up.1.refs_4_ = bf16[3072,3072]{1,0:T(8,128)(2,1)S(1)} custom-call(bf16[3072,3072]{1,0:T(8,128)(2,1)} %src_ref.2), custom_call_target="tpu_custom_call" | custom-call | bytes 37748736 | tf_op jit(solution)/shard_map/fetch_up/pallas_call | solution.py:97
  31.2 6.5 %fetch_down.1.refs_5_ = bf16[3072,3072]{1,0:T(8,128)(2,1)S(1)} custom-call(bf16[3072,3072]{1,0:T(8,128)(2,1)} %src_ref.3), custom_call_target="tpu_custom_call" | custom-call | bytes 37748736 | tf_op jit(solution)/shard_map/fetch_down/pallas_call | solution.py:97
  37.8 0.8 assemble_factors.1
  38.6 0.9 collective-permute-done.1.refs_2_
  39.6 8.0 %block_first.1 = (f32[32,3072]{1,0:T(8,128)S(1)}, bf16[32,3072]{1,0:T(8,128)(2,1)S(1)}, bf16[32,3072]{1,0:T(8,128)(2,1)S(1)}, bf16[32,3072]{1,0:T(8,128)(2,1)S(1)}) custom-call(bf16[32,3072]{1,0:T(8,128)(2,1)S(1)} %first_norm.1.refs_0_, bf16[32,3072]{1,0:T(8,128)(2,1)S(1)} %collective-permute-done.refs_1_, ...), custom_call_target="tpu_custom_call" | custom-call | flops 4831838208 | bytes 37748736 | tf_op jit(solution)/shard_map/block_first/pallas_call | solution.py:228
  47.6 0.1 collective-permute-start.12
  47.7 3.2 %collective-permute-start.13 = (bf16[32,3072]{1,0:T(8,128)(2,1)S(1)}, bf16[32,3072]{1,0:T(8,128)(2,1)S(1)}, u32[]{:S(2)}, u32[]{:S(2)}) collective-permute-start(bf16[32,3072]{1,0:T(8,128)(2,1)S(1)} %get-tuple-element.23), channel_id=1, source_target_pairs={{0,2},{1,3},{2,0},{3,1},{4,6},{5,7},{6,4},{7,5},{8,10},{9,11},{10,... | collective-permute-start | bytes 589832 | tf_op jit(solution)/shard_map/ppermute | solution.py:179
  50.9 1.2 %collective-permute-start.14 = (bf16[32,3072]{1,0:T(8,128)(2,1)S(1)}, bf16[32,3072]{1,0:T(8,128)(2,1)S(1)}, u32[]{:S(2)}, u32[]{:S(2)}) collective-permute-start(bf16[32,3072]{1,0:T(8,128)(2,1)S(1)} %get-tuple-element.24), channel_id=1, source_target_pairs={{0,3},{1,2},{2,1},{3,0},{4,7},{5,6},{6,5},{7,4},{8,11},{9,10},{10,... | collective-permute-start | bytes 589832 | tf_op jit(solution)/shard_map/ppermute | solution.py:179
  52.1 5.0 %collective-permute-done.12.refs_1_ = bf16[32,3072]{1,0:T(8,128)(2,1)S(1)} collective-permute-done((bf16[32,3072]{1,0:T(8,128)(2,1)S(1)}, bf16[32,3072]{1,0:T(8,128)(2,1)S(1)}, u32[]{:S(2)}, u32[]{:S(2)}) %collective-permute-start.12) | collective-permute-done | bytes 196640 | tf_op jit(solution)/shard_map/ppermute | solution.py:179
  57.1 8.1 %collective-permute-done.13.refs_2_ = bf16[32,3072]{1,0:T(8,128)(2,1)S(1)} collective-permute-done((bf16[32,3072]{1,0:T(8,128)(2,1)S(1)}, bf16[32,3072]{1,0:T(8,128)(2,1)S(1)}, u32[]{:S(2)}, u32[]{:S(2)}) %collective-permute-start.13) | collective-permute-done | bytes 196640 | tf_op jit(solution)/shard_map/ppermute | solution.py:179
  65.1 0.9 first_update.1
  66.1 0.0 copy-start.9
  66.1 2.4 %collective-permute-start.17 = (bf16[32,3072]{1,0:T(8,128)(2,1)S(1)}, bf16[32,3072]{1,0:T(8,128)(2,1)S(1)}, u32[]{:S(2)}, u32[]{:S(2)}) collective-permute-start(bf16[32,3072]{1,0:T(8,128)(2,1)S(1)} %get-tuple-element.27.refs_0_), channel_id=1, source_target_pairs={{0,3},{1,2},{2,1},{3,0},{4,7},{5,6},{6,5},{7,4},{8,11},{9,10},{10,... | collective-permute-start | bytes 589832 | tf_op jit(solution)/shard_map/ppermute | solution.py:179
  68.5 4.3 %collective-permute-start.16 = (bf16[32,3072]{1,0:T(8,128)(2,1)S(1)}, bf16[32,3072]{1,0:T(8,128)(2,1)S(1)}, u32[]{:S(2)}, u32[]{:S(2)}) collective-permute-start(bf16[32,3072]{1,0:T(8,128)(2,1)S(1)} %get-tuple-element.27.refs_0_), channel_id=1, source_target_pairs={{0,2},{1,3},{2,0},{3,1},{4,6},{5,7},{6,4},{7,5},{8,10},{9,11},{10,... | collective-permute-start | bytes 589832 | tf_op jit(solution)/shard_map/ppermute | solution.py:179
  72.8 2.8 %collective-permute-done.17.refs_3_ = bf16[32,3072]{1,0:T(8,128)(2,1)S(1)} collective-permute-done((bf16[32,3072]{1,0:T(8,128)(2,1)S(1)}, bf16[32,3072]{1,0:T(8,128)(2,1)S(1)}, u32[]{:S(2)}, u32[]{:S(2)}) %collective-permute-start.17) | collective-permute-done | bytes 196640 | tf_op jit(solution)/shard_map/ppermute | solution.py:179
  75.7 8.7 %collective-permute-done.16.refs_2_ = bf16[32,3072]{1,0:T(8,128)(2,1)S(1)} collective-permute-done((bf16[32,3072]{1,0:T(8,128)(2,1)S(1)}, bf16[32,3072]{1,0:T(8,128)(2,1)S(1)}, u32[]{:S(2)}, u32[]{:S(2)}) %collective-permute-start.16) | collective-permute-done | bytes 196640 | tf_op jit(solution)/shard_map/ppermute | solution.py:179
  84.4 8.2 %block_second.1 = (f32[32,3072]{1,0:T(8,128)S(1)}, bf16[32,3072]{1,0:T(8,128)(2,1)S(1)}, bf16[32,3072]{1,0:T(8,128)(2,1)S(1)}, bf16[32,3072]{1,0:T(8,128)(2,1)S(1)}) custom-call(bf16[32,3072]{1,0:T(8,128)(2,1)S(1)} %get-tuple-element.27.refs_0_, bf16[32,3072]{1,0:T(8,128)(2,1)S(1)} %collective-permute-done.15.refs_1_, ...), custom_call_target="tpu_custom_call" | custom-call | flops 4831838208 | bytes 37748736 | tf_op jit(solution)/shard_map/block_second/pallas_call | solution.py:228
  92.6 0.1 collective-permute-start.18
  92.7 3.0 %collective-permute-start.19 = (bf16[32,3072]{1,0:T(8,128)(2,1)S(1)}, bf16[32,3072]{1,0:T(8,128)(2,1)S(1)}, u32[]{:S(2)}, u32[]{:S(2)}) collective-permute-start(bf16[32,3072]{1,0:T(8,128)(2,1)S(1)} %get-tuple-element.30), channel_id=1, source_target_pairs={{0,2},{1,3},{2,0},{3,1},{4,6},{5,7},{6,4},{7,5},{8,10},{9,11},{10,... | collective-permute-start | bytes 589832 | tf_op jit(solution)/shard_map/ppermute | solution.py:179
  95.7 1.4 %collective-permute-start.20 = (bf16[32,3072]{1,0:T(8,128)(2,1)S(1)}, bf16[32,3072]{1,0:T(8,128)(2,1)S(1)}, u32[]{:S(2)}, u32[]{:S(2)}) collective-permute-start(bf16[32,3072]{1,0:T(8,128)(2,1)S(1)} %get-tuple-element.31), channel_id=1, source_target_pairs={{0,3},{1,2},{2,1},{3,0},{4,7},{5,6},{6,5},{7,4},{8,11},{9,10},{10,... | collective-permute-start | bytes 589832 | tf_op jit(solution)/shard_map/ppermute | solution.py:179
  97.1 3.4 %collective-permute-done.18.refs_1_ = bf16[32,3072]{1,0:T(8,128)(2,1)S(1)} collective-permute-done((bf16[32,3072]{1,0:T(8,128)(2,1)S(1)}, bf16[32,3072]{1,0:T(8,128)(2,1)S(1)}, u32[]{:S(2)}, u32[]{:S(2)}) %collective-permute-start.18) | collective-permute-done | bytes 196640 | tf_op jit(solution)/shard_map/ppermute | solution.py:179
  100.5 9.4 %collective-permute-done.19.refs_2_ = bf16[32,3072]{1,0:T(8,128)(2,1)S(1)} collective-permute-done((bf16[32,3072]{1,0:T(8,128)(2,1)S(1)}, bf16[32,3072]{1,0:T(8,128)(2,1)S(1)}, u32[]{:S(2)}, u32[]{:S(2)}) %collective-permute-start.19) | collective-permute-done | bytes 196640 | tf_op jit(solution)/shard_map/ppermute | solution.py:179
  110.0 1.7 %second_update.1 = (f32[2,32,3072]{2,1,0:T(8,128)}, f32[32,3072]{1,0:T(8,128)}) custom-call(s32[2]{0:T(128)S(1)} %copy-done.9, s32[3]{0:T(128)S(1)} %pad_add_fusion.place_ref, f32[32,3072]{1,0:T(8,128)S(1)} %get-tuple-element.25.state_ref, f32[3,4,3072]{2,1,0:T(4,128)S(1)} %bitcast.8, f32[32,3072]{1,0:T(8,128)S(1)} %get-tuple-element.26.vel_ref, ...), custom_call_target="tpu_custom_call" | custom-call | tf_op jit(solution)/shard_map/second_update/pallas_call | solution.py:252
  (28 shorter events, 0.1 us)
Async XLA Ops:
  0.6 0.9 copy-start.4
  1.5 0.9 copy-start.5
  2.4 0.8 copy-start.6
  3.2 0.8 copy-start.7
  4.1 10.1 %collective-permute-start.5 = (bf16[32,768]{1,0:T(8,128)(2,1)S(1)}, bf16[32,768]{1,0:T(8,128)(2,1)S(1)}, u32[]{:S(2)}, u32[]{:S(2)}) collective-permute-start(bf16[32,768]{1,0:T(8,128)(2,1)S(1)} %get-tuple-element.17), channel_id=1, source_target_pairs={{0,3},{1,2},{2,1},{3,0},{4,7},{5,6},{6,5},{7,4},{8,11},{9,10},{10,... | collective-permute-start | bytes 147464 | tf_op jit(solution)/shard_map/ppermute | solution.py:179
  9.2 5.0 %collective-permute-start.4 = (bf16[32,768]{1,0:T(8,128)(2,1)S(1)}, bf16[32,768]{1,0:T(8,128)(2,1)S(1)}, u32[]{:S(2)}, u32[]{:S(2)}) collective-permute-start(bf16[32,768]{1,0:T(8,128)(2,1)S(1)} %get-tuple-element.17), channel_id=1, source_target_pairs={{0,2},{1,3},{2,0},{3,1},{4,6},{5,7},{6,4},{7,5},{8,10},{9,11},{10,... | collective-permute-start | bytes 147464 | tf_op jit(solution)/shard_map/ppermute | solution.py:179
  9.2 4.1 %collective-permute-start.3 = (bf16[32,768]{1,0:T(8,128)(2,1)S(1)}, bf16[32,768]{1,0:T(8,128)(2,1)S(1)}, u32[]{:S(2)}, u32[]{:S(2)}) collective-permute-start(bf16[32,768]{1,0:T(8,128)(2,1)S(1)} %get-tuple-element.17), channel_id=1, source_target_pairs={{0,1},{1,0},{2,3},{3,2},{4,5},{5,4},{6,7},{7,6},{8,9},{9,8},{10,11... | collective-permute-start | bytes 147464 | tf_op jit(solution)/shard_map/ppermute | solution.py:179
  9.9 12.0 %collective-permute-start.10 = (bf16[32,3072]{1,0:T(8,128)(2,1)S(1)}, bf16[32,3072]{1,0:T(8,128)(2,1)S(1)}, u32[]{:S(2)}, u32[]{:S(2)}) collective-permute-start(bf16[32,3072]{1,0:T(8,128)(2,1)S(1)} %get-tuple-element.18.refs_4_), channel_id=1, source_target_pairs={{0,8},{4,12},{8,0},{12,4},{1,9},{5,13},{9,1},{13,5},{2,10},{6,14},... | collective-permute-start | bytes 589832 | tf_op jit(solution)/shard_map/ppermute | solution.py:179
  14.3 7.6 %collective-permute-start.7 = (bf16[32,3072]{1,0:T(8,128)(2,1)S(1)}, bf16[32,3072]{1,0:T(8,128)(2,1)S(1)}, u32[]{:S(2)}, u32[]{:S(2)}) collective-permute-start(bf16[32,3072]{1,0:T(8,128)(2,1)S(1)} %constant_dynamic-update-slice_fusion.refs_0_), channel_id=1, source_target_pairs={{0,8},{4,12},{8,0},{12,4},{1,9},{5,13},{9,1},{13,5},{2,10},{6,14},... | collective-permute-start | bytes 589832 | tf_op jit(solution)/shard_map/ppermute | solution.py:179
  15.8 6.6 %collective-permute-start.9 = (bf16[32,3072]{1,0:T(8,128)(2,1)S(1)}, bf16[32,3072]{1,0:T(8,128)(2,1)S(1)}, u32[]{:S(2)}, u32[]{:S(2)}) collective-permute-start(bf16[32,3072]{1,0:T(8,128)(2,1)S(1)} %get-tuple-element.18.refs_4_), channel_id=1, source_target_pairs={{0,4},{4,0},{8,12},{12,8},{1,5},{5,1},{9,13},{13,9},{2,6},{6,2},{1... | collective-permute-start | bytes 589832 | tf_op jit(solution)/shard_map/ppermute | solution.py:179
  15.8 6.7 %collective-permute-start.6 = (bf16[32,3072]{1,0:T(8,128)(2,1)S(1)}, bf16[32,3072]{1,0:T(8,128)(2,1)S(1)}, u32[]{:S(2)}, u32[]{:S(2)}) collective-permute-start(bf16[32,3072]{1,0:T(8,128)(2,1)S(1)} %constant_dynamic-update-slice_fusion.refs_0_), channel_id=1, source_target_pairs={{0,4},{4,0},{8,12},{12,8},{1,5},{5,1},{9,13},{13,9},{2,6},{6,2},{1... | collective-permute-start | bytes 589832 | tf_op jit(solution)/shard_map/ppermute | solution.py:179
  16.4 0.9 copy-start
  17.3 0.9 copy-start.2
  18.2 0.7 copy-start.8
  19.7 18.9 %collective-permute-start.2 = (bf16[32,3072]{1,0:T(8,128)(2,1)S(1)}, bf16[32,3072]{1,0:T(8,128)(2,1)S(1)}, u32[]{:S(2)}, u32[]{:S(2)}) collective-permute-start(bf16[32,3072]{1,0:T(8,128)(2,1)S(1)} %first_norm.1.refs_0_), channel_id=1, source_target_pairs={{0,3},{1,2},{2,1},{3,0},{4,7},{5,6},{6,5},{7,4},{8,11},{9,10},{10,... | collective-permute-start | bytes 589832 | tf_op jit(solution)/shard_map/ppermute | solution.py:179
  21.9 15.9 %collective-permute-start.11 = (bf16[32,3072]{1,0:T(8,128)(2,1)S(1)}, bf16[32,3072]{1,0:T(8,128)(2,1)S(1)}, u32[]{:S(2)}, u32[]{:S(2)}) collective-permute-start(bf16[32,3072]{1,0:T(8,128)(2,1)S(1)} %collective-permute-done.10.refs_6_), channel_id=1, source_target_pairs={{0,4},{4,0},{8,12},{12,8},{1,5},{5,1},{9,13},{13,9},{2,6},{6,2},{1... | collective-permute-start | bytes 589832 | tf_op jit(solution)/shard_map/ppermute | solution.py:179
  21.9 15.9 %collective-permute-start.8 = (bf16[32,3072]{1,0:T(8,128)(2,1)S(1)}, bf16[32,3072]{1,0:T(8,128)(2,1)S(1)}, u32[]{:S(2)}, u32[]{:S(2)}) collective-permute-start(bf16[32,3072]{1,0:T(8,128)(2,1)S(1)} %collective-permute-done.7.refs_2_), channel_id=1, source_target_pairs={{0,4},{4,0},{8,12},{12,8},{1,5},{5,1},{9,13},{13,9},{2,6},{6,2},{1... | collective-permute-start | bytes 589832 | tf_op jit(solution)/shard_map/ppermute | solution.py:179
  22.4 17.1 %collective-permute-start.1 = (bf16[32,3072]{1,0:T(8,128)(2,1)S(1)}, bf16[32,3072]{1,0:T(8,128)(2,1)S(1)}, u32[]{:S(2)}, u32[]{:S(2)}) collective-permute-start(bf16[32,3072]{1,0:T(8,128)(2,1)S(1)} %first_norm.1.refs_0_), channel_id=1, source_target_pairs={{0,2},{1,3},{2,0},{3,1},{4,6},{5,7},{6,4},{7,5},{8,10},{9,11},{10,... | collective-permute-start | bytes 589832 | tf_op jit(solution)/shard_map/ppermute | solution.py:179
  22.5 17.1 %collective-permute-start = (bf16[32,3072]{1,0:T(8,128)(2,1)S(1)}, bf16[32,3072]{1,0:T(8,128)(2,1)S(1)}, u32[]{:S(2)}, u32[]{:S(2)}) collective-permute-start(bf16[32,3072]{1,0:T(8,128)(2,1)S(1)} %first_norm.1.refs_0_), channel_id=1, source_target_pairs={{0,1},{1,0},{2,3},{3,2},{4,5},{5,4},{6,7},{7,6},{8,9},{9,8},{10,11... | collective-permute-start | bytes 589832 | tf_op jit(solution)/shard_map/ppermute | solution.py:179
  39.6 25.6 %copy-start.1 = (f32[4,3,3072]{2,0,1:T(4,128)S(1)}, f32[4,3,3072]{2,0,1:T(4,128)}, u32[]{:S(2)}) copy-start(f32[4,3,3072]{2,0,1:T(4,128)} %param.11) | copy-start | bytes 442372
  39.6 25.6 %copy-start.3 = (bf16[32,3072]{1,0:T(8,128)(2,1)S(1)}, bf16[32,3072]{1,0:T(8,128)(2,1)}, u32[]{:S(2)}) copy-start(bf16[32,3072]{1,0:T(8,128)(2,1)} %lat_ref.3) | copy-start | bytes 589828
  47.6 9.4 %collective-permute-start.12 = (bf16[32,3072]{1,0:T(8,128)(2,1)S(1)}, bf16[32,3072]{1,0:T(8,128)(2,1)S(1)}, u32[]{:S(2)}, u32[]{:S(2)}) collective-permute-start(bf16[32,3072]{1,0:T(8,128)(2,1)S(1)} %get-tuple-element.22), channel_id=1, source_target_pairs={{0,1},{1,0},{2,3},{3,2},{4,5},{5,4},{6,7},{7,6},{8,9},{9,8},{10,11... | collective-permute-start | bytes 589832 | tf_op jit(solution)/shard_map/ppermute | solution.py:179
  47.7 17.4 %collective-permute-start.13 = (bf16[32,3072]{1,0:T(8,128)(2,1)S(1)}, bf16[32,3072]{1,0:T(8,128)(2,1)S(1)}, u32[]{:S(2)}, u32[]{:S(2)}) collective-permute-start(bf16[32,3072]{1,0:T(8,128)(2,1)S(1)} %get-tuple-element.23), channel_id=1, source_target_pairs={{0,2},{1,3},{2,0},{3,1},{4,6},{5,7},{6,4},{7,5},{8,10},{9,11},{10,... | collective-permute-start | bytes 589832 | tf_op jit(solution)/shard_map/ppermute | solution.py:179
  50.9 14.2 %collective-permute-start.14 = (bf16[32,3072]{1,0:T(8,128)(2,1)S(1)}, bf16[32,3072]{1,0:T(8,128)(2,1)S(1)}, u32[]{:S(2)}, u32[]{:S(2)}) collective-permute-start(bf16[32,3072]{1,0:T(8,128)(2,1)S(1)} %get-tuple-element.24), channel_id=1, source_target_pairs={{0,3},{1,2},{2,1},{3,0},{4,7},{5,6},{6,5},{7,4},{8,11},{9,10},{10,... | collective-permute-start | bytes 589832 | tf_op jit(solution)/shard_map/ppermute | solution.py:179
  66.1 43.9 %copy-start.9 = (s32[2]{0:T(128)S(1)}, s32[2]{0:T(128)}, u32[]{:S(2)}) copy-start(s32[2]{0:T(128)} %steps_ref.5) | copy-start | bytes 28
  66.1 9.6 %collective-permute-start.17 = (bf16[32,3072]{1,0:T(8,128)(2,1)S(1)}, bf16[32,3072]{1,0:T(8,128)(2,1)S(1)}, u32[]{:S(2)}, u32[]{:S(2)}) collective-permute-start(bf16[32,3072]{1,0:T(8,128)(2,1)S(1)} %get-tuple-element.27.refs_0_), channel_id=1, source_target_pairs={{0,3},{1,2},{2,1},{3,0},{4,7},{5,6},{6,5},{7,4},{8,11},{9,10},{10,... | collective-permute-start | bytes 589832 | tf_op jit(solution)/shard_map/ppermute | solution.py:179
  68.5 15.9 %collective-permute-start.16 = (bf16[32,3072]{1,0:T(8,128)(2,1)S(1)}, bf16[32,3072]{1,0:T(8,128)(2,1)S(1)}, u32[]{:S(2)}, u32[]{:S(2)}) collective-permute-start(bf16[32,3072]{1,0:T(8,128)(2,1)S(1)} %get-tuple-element.27.refs_0_), channel_id=1, source_target_pairs={{0,2},{1,3},{2,0},{3,1},{4,6},{5,7},{6,4},{7,5},{8,10},{9,11},{10,... | collective-permute-start | bytes 589832 | tf_op jit(solution)/shard_map/ppermute | solution.py:179
  72.8 11.6 %collective-permute-start.15 = (bf16[32,3072]{1,0:T(8,128)(2,1)S(1)}, bf16[32,3072]{1,0:T(8,128)(2,1)S(1)}, u32[]{:S(2)}, u32[]{:S(2)}) collective-permute-start(bf16[32,3072]{1,0:T(8,128)(2,1)S(1)} %get-tuple-element.27.refs_0_), channel_id=1, source_target_pairs={{0,1},{1,0},{2,3},{3,2},{4,5},{5,4},{6,7},{7,6},{8,9},{9,8},{10,11... | collective-permute-start | bytes 589832 | tf_op jit(solution)/shard_map/ppermute | solution.py:179
  92.6 7.9 %collective-permute-start.18 = (bf16[32,3072]{1,0:T(8,128)(2,1)S(1)}, bf16[32,3072]{1,0:T(8,128)(2,1)S(1)}, u32[]{:S(2)}, u32[]{:S(2)}) collective-permute-start(bf16[32,3072]{1,0:T(8,128)(2,1)S(1)} %get-tuple-element.29), channel_id=1, source_target_pairs={{0,1},{1,0},{2,3},{3,2},{4,5},{5,4},{6,7},{7,6},{8,9},{9,8},{10,11... | collective-permute-start | bytes 589832 | tf_op jit(solution)/shard_map/ppermute | solution.py:179
  92.7 17.2 %collective-permute-start.19 = (bf16[32,3072]{1,0:T(8,128)(2,1)S(1)}, bf16[32,3072]{1,0:T(8,128)(2,1)S(1)}, u32[]{:S(2)}, u32[]{:S(2)}) collective-permute-start(bf16[32,3072]{1,0:T(8,128)(2,1)S(1)} %get-tuple-element.30), channel_id=1, source_target_pairs={{0,2},{1,3},{2,0},{3,1},{4,6},{5,7},{6,4},{7,5},{8,10},{9,11},{10,... | collective-permute-start | bytes 589832 | tf_op jit(solution)/shard_map/ppermute | solution.py:179
  95.7 14.3 %collective-permute-start.20 = (bf16[32,3072]{1,0:T(8,128)(2,1)S(1)}, bf16[32,3072]{1,0:T(8,128)(2,1)S(1)}, u32[]{:S(2)}, u32[]{:S(2)}) collective-permute-start(bf16[32,3072]{1,0:T(8,128)(2,1)S(1)} %get-tuple-element.31), channel_id=1, source_target_pairs={{0,3},{1,2},{2,1},{3,0},{4,7},{5,6},{6,5},{7,4},{8,11},{9,10},{10,... | collective-permute-start | bytes 589832 | tf_op jit(solution)/shard_map/ppermute | solution.py:179

commit v3 on v2

v3 whole, which is shorter than its diff:
```python
import functools

import jax
import jax.numpy as jnp
from jax import lax
from jax.experimental import pallas as pl
from jax.experimental.pallas import tpu as pltpu
from jax.sharding import PartitionSpec as P

NSTEPS = 4
STREAMS = 4
TOKEN_ORDER = (1, 3, 2)
STEP_SIZE = -1.0 / NSTEPS
BF16, F32 = jnp.bfloat16, jnp.float32
VMEM_GRANT = 4 << 20
VMEM = pl.BlockSpec(memory_space=pltpu.VMEM)
SMEM = pl.BlockSpec(memory_space=pltpu.SMEM)
HBM = pl.BlockSpec(memory_space=pltpu.HBM)
NT = (((1,), (1,)), ((), ()))


def call(body, outs, in_specs, out_specs, name, scratch=(), flops=0, bytes_accessed=0):
    return pl.pallas_call(
        body,
        out_shape=outs,
        in_specs=in_specs,
        out_specs=out_specs,
        scratch_shapes=list(scratch),
        compiler_params=pltpu.CompilerParams(vmem_limit_bytes=VMEM_GRANT),
        cost_estimate=pl.CostEstimate(
            flops=flops, bytes_accessed=bytes_accessed, transcendentals=0
        ),
        name=name,
    )


def shape(dims, dtype=BF16):
    return jax.ShapeDtypeStruct(dims, dtype)


def modulated(state, shift, scale):
    mean = jnp.mean(state, axis=1, keepdims=True)
    centered = state - mean
    spread = jnp.mean(centered * centered, axis=1, keepdims=True)
    return (centered * lax.rsqrt(spread + 1e-06) * (1.0 + scale) + shift).astype(BF16)


def gelu(x):
    return x * (0.5 * (1.0 + jnp.tanh(0.7978845608028654 * (x + 0.044715 * (x * x * x)))))


def own_image(count, images):
    tp = lax.axis_size("tp")
    return lax.axis_index("tp") * images // tp


def mod_row(mod_ref, which, step):
    return mod_ref[which, pl.ds(step, 1), :]


def prepare_body(slots, rank, *refs):
    sources, outs, held, sems = refs[:7], refs[7:10], refs[10:17], refs[-1]
    copies = [
        pltpu.make_async_copy(src, dst, sems.at[i])
        for i, (src, dst) in enumerate(zip(sources, held))
    ]
    for copy in copies:
        copy.start()
    for copy in copies:
        copy.wait()
    ua_ref, db_ref, ub_ref, da_ref, steps_ref, lat_ref, mod_ref = held
    p_ref, q_ref = outs[:2]
    rows = []
    for slot in range(slots):
        part = pl.ds(slot * rank, rank)
        rows += [ua_ref[part, :], db_ref[part, :]]
    both = jnp.concatenate(rows, axis=0)
    width = both.shape[0]
    eye = (
        lax.broadcasted_iota(jnp.int32, (width, width), 0)
        == lax.broadcasted_iota(jnp.int32, (width, width), 1)
    ).astype(F32)
    cols = lax.dot_general(
        both, eye.astype(BF16), (((0,), (0,)), ((), ())), preferred_element_type=F32
    ).astype(BF16)
    height = p_ref.shape[0]
    for piece in range(cols.shape[0] // height):
        p_ref[:, piece * width : (piece + 1) * width] = cols[piece * height : (piece + 1) * height, :]
    q_ref[0:rank, :] = ub_ref[...]
    q_ref[rank : 2 * rank, :] = da_ref[...]
    step = steps_ref[own_image(lat_ref.shape[0], steps_ref.shape[0])]
    state = lat_ref[...].astype(F32)
    outs[2][...] = modulated(state, mod_row(mod_ref, 0, step), mod_row(mod_ref, 1, step))


def fetch_body(start, source, target, sems):
    copies = stream_copies(source, target, sems, start)
    for copy in copies:
        copy.start()
    for copy in copies:
        copy.wait()


def assemble_body(tp, dp, *refs):
    p_parts, q_parts, (p_ref, q_ref, pt_ref, qt_ref) = refs[:dp], refs[dp : 2 * dp], refs[2 * dp :]
    me_tp, me_dp = lax.axis_index("tp"), lax.axis_index("dp")
    height = q_parts[0].shape[0]
    width = p_ref.shape[1]
    per_block = p_ref.shape[0] // (tp * dp)
    pieces = per_block // height
    for j in range(dp):
        owner = me_dp ^ j
        q_ref[pl.ds(pl.multiple_of(owner * height, height), height), :] = q_parts[j][...]
        for k in range(tp):
            base = (owner * tp + (me_tp ^ k)) * per_block
            for piece in range(pieces):
                col = (k * pieces + piece) * width
                p_ref[pl.ds(pl.multiple_of(base + piece * height, height), height), :] = p_parts[j][
                    :, col : col + width
                ]
    pt_ref[...] = p_ref[...].T
    qt_ref[...] = q_ref[...].T


def stream_copies(source, target, sems, start):
    rows = target.shape[0] // STREAMS
    copies = []
    for i in range(STREAMS):
        block = pl.ds(i * rows, rows)
        copies.append(
            pltpu.make_async_copy(
                source.at[block, pl.ds(start, target.shape[1])], target.at[block], sems.at[i]
            )
        )
    return copies


def start_stream(source, target, sems, start):
    rows = target.shape[0] // STREAMS
    cols = pl.ds(start, target.shape[1])

    @pl.loop(0, STREAMS)
    def _(i):
        block = pl.ds(pl.multiple_of(i * rows, rows), rows)
        pltpu.make_async_copy(source.at[block, cols], target.at[block], sems.at[i]).start()


def block_body(streamed, rank, *refs):
    given = 4 if streamed else 6
    x_refs, refs = refs[:given], refs[given:]
    (p_ref, q_ref, pt_ref, qt_ref), wu_refs, refs = refs[:4], refs[4:6], refs[6:]
    if streamed:
        source, outs, wd_refs, (x_all, hidden, sems) = refs[0], refs[1:7], refs[7:9], refs[9:]
        for i, target in enumerate(wd_refs):
            start_stream(source, target, sems.at[i], i * target.shape[1])
    else:
        wd_refs, outs, (x_all, hidden) = refs[:2], refs[2:8], refs[8:]
    count, width = x_refs[0].shape
    half = width // 2
    if streamed:
        for k, x_ref in enumerate(x_refs):
            x_all[k * count : (k + 1) * count, :] = x_ref[...]
    else:
        own_ref, near_ref, far_ref, over_ref, rest_2_ref, rest_3_ref = x_refs
        x_all[:count, :] = own_ref[...]
        x_all[count : 2 * count, :] = near_ref[...]
        x_all[2 * count : 3 * count, :half] = far_ref[...]
        x_all[2 * count : 3 * count, half:] = rest_2_ref[...]
        x_all[3 * count :, :half] = over_ref[...]
        x_all[3 * count :, half:] = rest_3_ref[...]
    lanes = lax.broadcasted_iota(jnp.int32, (1, p_ref.shape[1]), 1)
    first_half = (lanes // rank) % 2 == 0
    low = jnp.dot(x_all[...], p_ref[...], preferred_element_type=F32)
    low = jnp.where(first_half, low, 0.0).astype(BF16)
    tile = wu_refs[0].shape[1]
    for i, wu_ref in enumerate(wu_refs):
        cols = slice(i * tile, (i + 1) * tile)
        upper = jnp.dot(x_all[...], wu_ref[...], preferred_element_type=F32)
        upper += jnp.dot(low, q_ref[:, cols], preferred_element_type=F32)
        hidden[:, cols] = gelu(upper).astype(BF16)
    low = jnp.dot(hidden[...], qt_ref[...], preferred_element_type=F32)
    low = jnp.where(first_half, 0.0, low).astype(BF16)
    own_out, near_out, over_out, far_out, rest_2_out, rest_3_out = outs
    for i, wd_ref in enumerate(wd_refs):
        cols = slice(i * half, (i + 1) * half)
        if streamed:
            for copy in stream_copies(source, wd_ref, sems.at[i], i * half):
                copy.wait()
        out = jnp.dot(hidden[...], wd_ref[...], preferred_element_type=F32)
        out += jnp.dot(low, pt_ref[:, cols], preferred_element_type=F32)
        own_out[:, cols] = out[:count]
        near_out[:, cols] = out[count : 2 * count].astype(BF16)
        if i == 0:
            far_out[...] = out[2 * count : 3 * count]
            over_out[...] = out[3 * count :].astype(BF16)
        else:
            rest_2_out[...] = out[2 * count : 3 * count].astype(BF16)
            rest_3_out[...] = out[3 * count :].astype(BF16)


def relay_body(mine_ref, got_ref, out_ref):
    out_ref[...] = (mine_ref[...] + got_ref[...].astype(F32)).astype(BF16)


def summed(own_ref, near_ref, far_ref, rest_2_ref, rest_3_ref):
    half = far_ref.shape[1]
    total = own_ref[...] + near_ref[...].astype(F32)
    first = total[:, :half] + far_ref[...].astype(F32)
    second = total[:, half:] + rest_2_ref[...].astype(F32) + rest_3_ref[...].astype(F32)
    return jnp.concatenate([first, second], axis=1)


def middle_body(steps_ref, lat_ref, mod_ref, *refs):
    parts, (vel_ref, state_ref, out_ref, far_ref, rest_ref) = refs[:5], refs[5:]
    step = steps_ref[own_image(lat_ref.shape[0], steps_ref.shape[0])]
    vel = mod_row(mod_ref, 2, step) * summed(*parts)
    state = lat_ref[...].astype(F32) + STEP_SIZE * vel
    vel_ref[...] = vel
    state_ref[...] = state
    normed = modulated(state, mod_row(mod_ref, 0, step + 1), mod_row(mod_ref, 1, step + 1))
    half = far_ref.shape[1]
    out_ref[...] = normed
    far_ref[...] = normed[:, :half]
    rest_ref[...] = normed[:, half:]


def last_body(steps_ref, mod_ref, vel_ref, state_ref, *refs):
    parts, (vels_ref, out_ref) = refs[:-2], refs[-2:]
    step = steps_ref[own_image(out_ref.shape[0], steps_ref.shape[0])] + 1
    vel = mod_row(mod_ref, 2, step) * summed(*parts)
    vels_ref[0] = vel_ref[...]
    vels_ref[1] = vel
    out_ref[...] = state_ref[...] + STEP_SIZE * vel


def swap(x, axis, flip):
    return lax.ppermute(x, axis, [(i, i ^ flip) for i in range(lax.axis_size(axis))])


def spread(whole, rest, far):
    return dict(
        over=swap(far, "tp", 1),
        near=swap(whole, "tp", 1),
        rest_2=swap(rest, "tp", 2),
        rest_3=swap(rest, "tp", 3),
    )


def gather(own, got, far):
    return [own, got["near"], far, got["over"], got["rest_2"], got["rest_3"]]


def reduce(own, near, over, far, rest_2, rest_3):
    count, half = far.shape
    relayed = call(relay_body, shape((count, half)), [VMEM] * 2, VMEM, "relay")(
        far, swap(over, "tp", 1)
    )
    return (
        own,
        swap(near, "tp", 1),
        swap(relayed, "tp", 2),
        swap(rest_2, "tp", 2),
        swap(rest_3, "tp", 3),
    )


def pinned(x, space):
    return pltpu.with_memory_space_constraint(x, space)


def fast(latents, step_index, mod_table, base_up, base_down, up_a, up_b, down_a, down_b):
    tp, dp = lax.axis_size("tp"), lax.axis_size("dp")
    count, width = latents.shape
    rows = count * tp
    half = width // 2
    hidden = base_up.shape[1]
    rank = up_b.shape[0]
    both = 2 * rank * dp
    height = 2 * rank
    extra = up_a.shape[0] // height * both
    mods = jnp.transpose(mod_table, (1, 0, 2))
    spread_shapes = (shape((count, width)), shape((count, half)), shape((count, half)))

    sources = (up_a.T, down_b, up_b, down_a.T, step_index, latents, mods)
    p_own, q_own, normed = call(
        functools.partial(prepare_body, dp, rank),
        (
            shape((height, extra)),
            shape((height, hidden)),
            shape((count, width)),
        ),
        [HBM] * 7,
        (VMEM,) * 3,
        "prepare",
        [(pltpu.SMEM if a is step_index else pltpu.VMEM)(a.shape, a.dtype) for a in sources]
        + [pltpu.SemaphoreType.DMA((7,))],
    )(*[pinned(a, pltpu.HBM) for a in sources])

    def fetch(start, name):
        return call(
            functools.partial(fetch_body, start),
            pltpu.VMEM((width, hidden // 2), BF16),
            [HBM],
            VMEM,
            name,
            [pltpu.SemaphoreType.DMA((STREAMS,))],
            bytes_accessed=base_up.size * 2,
        )(pinned(base_up, pltpu.HBM))

    p_line = jnp.concatenate([p_own] + [swap(p_own, "tp", k) for k in (1, 2, 3)], axis=1)
    up_0, up_1 = fetch(0, "fetch_up_0"), fetch(hidden // 2, "fetch_up_1")
    p_line, up_0, up_1 = lax.optimization_barrier((p_line, up_0, up_1))
    p_far = swap(p_line, "dp", 2)
    q_far = swap(q_own, "dp", 2)
    tokens = [normed] + [swap(normed, "tp", k) for k in TOKEN_ORDER]
    p_far, q_far, tokens = lax.optimization_barrier((p_far, q_far, tokens))
    near = [swap(a, "dp", 1) for a in (p_line, q_own, p_far, q_far)]
    factors = call(
        functools.partial(assemble_body, tp, dp),
        (
            pltpu.VMEM((width, both), BF16),
            pltpu.VMEM((both, hidden), BF16),
            pltpu.VMEM((both, width), BF16),
            pltpu.VMEM((hidden, both), BF16),
        ),
        [VMEM] * (2 * dp),
        (VMEM,) * 4,
        "assemble_factors",
    )(p_line, near[0], p_far, near[2], q_own, near[1], q_far, near[3])
    resident = [pinned(a, pltpu.VMEM) for a in (*factors, up_0, up_1)]

    def block(parts, downs):
        streamed = downs is None
        given = [pinned(base_down, pltpu.HBM)] if streamed else [pinned(a, pltpu.VMEM) for a in downs]
        return call(
            functools.partial(block_body, streamed, rank),
            (
                shape((count, width), F32),
                shape((count, width)),
                shape((count, half)),
                shape((count, half), F32),
                shape((count, half)),
                shape((count, half)),
            )
            + (pltpu.VMEM((hidden, half), BF16),) * (2 * streamed),
            [VMEM] * (len(parts) + 6) + [HBM if streamed else VMEM] * len(given),
            (VMEM,) * (6 + 2 * streamed),
            "block",
            [pltpu.VMEM((rows, width), BF16), pltpu.VMEM((rows, hidden), BF16)]
            + [pltpu.SemaphoreType.DMA((2, STREAMS))] * streamed,
            flops=4 * rows * width * hidden,
            bytes_accessed=4 * width * hidden,
        )(*parts, *resident, *given)

    tokens = [tokens[0]] + [tokens[1 + TOKEN_ORDER.index(k)] for k in (1, 2, 3)]
    *sums, down_0, down_1 = block(tokens, None)
    vel, state, normed, far, rest = call(
        middle_body,
        (shape((count, width), F32), shape((count, width), F32)) + spread_shapes,
        [SMEM] + [VMEM] * 7,
        (VMEM,) * 5,
        "first_update",
    )(step_index, latents, mods, *reduce(*sums))
    far = swap(far, "tp", 2)
    sums = block(gather(normed, spread(normed, rest, far), far), (down_0, down_1))
    return call(
        last_body,
        (shape((2, count, width), F32), shape((count, width), F32)),
        [SMEM] + [VMEM] * 8,
        (VMEM,) * 2,
        "second_update",
    )(step_index, mods, vel, state, *reduce(*sums))


def normalize(state, shift, scale):
    mean = jnp.mean(state, axis=1, keepdims=True)
    centered = state - mean
    spread = jnp.mean(centered * centered, axis=1, keepdims=True)
    return (centered * lax.rsqrt(spread + 1e-06) * (1.0 + scale) + shift).astype(jnp.bfloat16)


def plain(latents, step_index, mod_table, base_up, base_down, up_a, up_b, down_a, down_b):
    full_up_a, full_down_b = (
        lax.all_gather(up_a, ("dp", "tp"), axis=0, tiled=True),
        lax.all_gather(down_b, ("dp", "tp"), axis=1, tiled=True),
    )
    cols_up_b, rows_down_a = (
        lax.all_gather(up_b, "dp", axis=0, tiled=True),
        lax.all_gather(down_a, "dp", axis=1, tiled=True),
    )
    merged_up = (
        base_up.astype(jnp.float32)
        + jnp.dot(full_up_a, cols_up_b, preferred_element_type=jnp.float32)
    ).astype(jnp.bfloat16)
    merged_down = (
        base_down.astype(jnp.float32)
        + jnp.dot(rows_down_a, full_down_b, preferred_element_type=jnp.float32)
    ).astype(jnp.bfloat16)
    own_count = latents.shape[0]
    group_rows = own_count * lax.axis_size("tp")
    image_count = step_index.shape[0]
    image_rows = group_rows // image_count
    own_start = lax.axis_index("tp") * own_count
    step_size = -1.0 / NSTEPS

    def row_steps(count, offset):
        rows = jnp.arange(count, dtype=jnp.int32)
        image = rows // image_rows
        picks = (image[:, None] == jnp.arange(image_count, dtype=jnp.int32)[None, :]).astype(
            jnp.int32
        )
        return jnp.sum(picks * step_index[None, :], axis=1) + offset

    def modulation(steps):
        onehot = (steps[:, None] == jnp.arange(NSTEPS, dtype=jnp.int32)[None, :]).astype(
            jnp.float32
        )
        shift = jnp.dot(onehot, mod_table[:, 0, :], precision=lax.Precision.HIGHEST)
        scale = jnp.dot(onehot, mod_table[:, 1, :], precision=lax.Precision.HIGHEST)
        gate = jnp.dot(onehot, mod_table[:, 2, :], precision=lax.Precision.HIGHEST)
        return (shift, scale, gate)

    def project(normed):
        upper = jnp.dot(normed, merged_up, preferred_element_type=jnp.float32)
        hidden = jax.nn.gelu(upper, approximate=True).astype(jnp.bfloat16)
        return jnp.dot(hidden, merged_down, preferred_element_type=jnp.float32)

    state_all = lax.all_gather(latents, "tp", axis=0, tiled=True).astype(jnp.float32)
    shift, scale, gate = modulation(row_steps(group_rows, 0))
    normed = normalize(state_all, shift, scale)
    first = gate * lax.psum(project(normed), "tp")
    state_all = state_all + step_size * first
    shift, scale, gate = modulation(row_steps(group_rows, 1))
    normed = normalize(state_all, shift, scale)
    gate_own = lax.dynamic_slice_in_dim(gate, own_start, own_count, 0)
    second = gate_own * lax.psum_scatter(project(normed), "tp", scatter_dimension=0, tiled=True)
    state_own = lax.dynamic_slice_in_dim(state_all, own_start, own_count, 0) + step_size * second
    first_own = lax.dynamic_slice_in_dim(first, own_start, own_count, 0)
    return (jnp.stack([first_own, second]), state_own)


def solution(mesh):
    tp, dp = mesh.shape["tp"], mesh.shape["dp"]

    def local(*args):
        latents, step_index, mod_table, base_up, base_down, up_a, up_b = args[:7]
        whole_tiles = (
            tp == 4
            and dp == 4
            and latents.shape[0] == 2 * up_b.shape[0]
            and base_up.shape[1] % 256 == 0
            and base_up.shape[0] % 256 == 0
            and up_b.shape[0] % 16 == 0
            and up_a.shape[0] % (2 * up_b.shape[0]) == 0
            and tp % step_index.shape[0] == 0
        )
        return (fast if whole_tiles else plain)(*args)

    return jax.shard_map(
        local,
        mesh=mesh,
        in_specs=(
            P(("grp", "dp", "tp"), None),
            P(("grp", "dp")),
            P(),
            P(None, "tp"),
            P("tp", None),
            P(("dp", "tp"), None),
            P("dp", "tp"),
            P("tp", "dp"),
            P(None, ("dp", "tp")),
        ),
        out_specs=(P(None, ("grp", "dp", "tp"), None), P(("grp", "dp", "tp"), None)),
        check_vma=False,
    )
```

time: 112 us -> 97.2 us (0.87)
  Pallas kernels: 33.8 us -> 26.5 us
  local copies, waits for them, and re-layouts: 5.82 us -> 0.02 us
  waiting for transfers between devices: 41.2 us -> 38.6 us
    pallas_call x8 -> x9, Pallas kernels: 33 us -> 25.9 us  [the longest x2 14.2 us: block(): call(functools.partial(block_body, streamed, rank), (shape((count, width)...]
    unnamed x23 -> x6, local copies, waits for them, and re-layouts: 5.81 us -> 0.02 us
    ppermute x21 -> x27, waiting for transfers between devices: 41.2 us -> 38.6 us  [swap(): lax.ppermute(x, axis, [(i, i ^ flip) for i in range(lax.axis_size(axis))])]
    ppermute x21 -> x27, starting transfers between devices: 30 us -> 31.1 us  [swap(): lax.ppermute(x, axis, [(i, i ^ flip) for i in range(lax.axis_size(axis))])]
  transfers between devices with their start and end apart: 21 -> 27, of which waited for: 9 -> 17; matrix products, arithmetic and copies ran while one was open for 0% -> 0% of each run, Pallas kernels for 13% -> 8%
where the time goes in v3:
time: 97.2 us; the launch traced here: 97 us
  waiting for transfers between devices  38.6 us (40%)
  starting transfers between devices  31.1 us (32%)
  Pallas kernels  26.5 us (27%)
    ppermute x27, waiting for transfers between devices, swap(): lax.ppermute(x, axis, [(i, i ^ flip) for i in range(lax.axis_size(axis))])  38.6 us
    ppermute x27, starting transfers between devices, swap(): lax.ppermute(x, axis, [(i, i ^ flip) for i in range(lax.axis_size(axis))])  31.1 us
    pallas_call x2, Pallas kernels, block(): call(functools.partial(block_body, streamed, rank), (shape((count, width)...  14.2 us
    pallas_call x2, Pallas kernels, fetch(): call(functools.partial(fetch_body, start), pltpu.VMEM((width, hidden // 2...  7.6 us
  transfers between devices with their start and end apart: 27, of which 17 were waited for; matrix products, arithmetic and copies ran while one was open for 0% of the time, Pallas kernels for 8%

profile of v3, /device:TPU:0, one launch (start us, length us, event | category | flops | bytes accessed | tf_op | source)
XLA Modules:
  0.0 97.0 jit_solution(18412205258797832721)
XLA Ops:
  0.6 1.5 %prepare.1 = (bf16[32,768]{1,0:T(8,128)(2,1)S(1)}, bf16[32,3072]{1,0:T(8,128)(2,1)S(1)}, bf16[32,3072]{1,0:T(8,128)(2,1)S(1)}) custom-call(bf16[64,192]{1,0:T(8,128)(2,1)} %bitcast.7, bf16[64,192]{1,0:T(8,128)(2,1)} %refs_1_.1, bf16[16,3072]{1,0:T(8,128)(2,1)} %refs_2_.1, bf16[16,3072]{1,0:T(8,128)(2,1)} %bitcast.6, s32[2]{0:T(128)} %steps_ref.3, ...), custom_call_target="tpu_custom_call" | custom-call | tf_op jit(solution)/shard_map/prepare/pallas_call | solution.py:285
  2.1 5.1 %collective-permute-start.2 = (bf16[32,768]{1,0:T(8,128)(2,1)S(1)}, bf16[32,768]{1,0:T(8,128)(2,1)S(1)}, u32[]{:S(2)}, u32[]{:S(2)}) collective-permute-start(bf16[32,768]{1,0:T(8,128)(2,1)S(1)} %get-tuple-element.37), channel_id=1, source_target_pairs={{0,3},{1,2},{2,1},{3,0},{4,7},{5,6},{6,5},{7,4},{8,11},{9,10},{10,... | collective-permute-start | bytes 147464 | tf_op jit(solution)/shard_map/ppermute | solution.py:237
  7.2 0.6 collective-permute-start
  7.9 2.3 %collective-permute-start.7 = (bf16[32,3072]{1,0:T(8,128)(2,1)S(1)}, bf16[32,3072]{1,0:T(8,128)(2,1)S(1)}, u32[]{:S(2)}, u32[]{:S(2)}) collective-permute-start(bf16[32,3072]{1,0:T(8,128)(2,1)S(1)} %get-tuple-element.41.refs_0_), channel_id=1, source_target_pairs={{0,2},{1,3},{2,0},{3,1},{4,6},{5,7},{6,4},{7,5},{8,10},{9,11},{10,... | collective-permute-start | bytes 589832 | tf_op jit(solution)/shard_map/ppermute | solution.py:237
  10.2 1.5 %collective-permute-start.6 = (bf16[32,3072]{1,0:T(8,128)(2,1)S(1)}, bf16[32,3072]{1,0:T(8,128)(2,1)S(1)}, u32[]{:S(2)}, u32[]{:S(2)}) collective-permute-start(bf16[32,3072]{1,0:T(8,128)(2,1)S(1)} %get-tuple-element.41.refs_0_), channel_id=1, source_target_pairs={{0,3},{1,2},{2,1},{3,0},{4,7},{5,6},{6,5},{7,4},{8,11},{9,10},{10,... | collective-permute-start | bytes 589832 | tf_op jit(solution)/shard_map/ppermute | solution.py:237
  11.6 3.8 %fetch_up_1.1.refs_9_.refs_11_ = bf16[3072,1536]{1,0:T(8,128)(2,1)S(1)} custom-call(bf16[3072,3072]{1,0:T(8,128)(2,1)} %source.3), custom_call_target="tpu_custom_call" | custom-call | bytes 18874368 | tf_op jit(solution)/shard_map/fetch_up_1/pallas_call | solution.py:300
  15.4 3.8 %fetch_up_0.1.refs_8_.refs_10_ = bf16[3072,1536]{1,0:T(8,128)(2,1)S(1)} custom-call(bf16[3072,3072]{1,0:T(8,128)(2,1)} %source.3), custom_call_target="tpu_custom_call" | custom-call | bytes 18874368 | tf_op jit(solution)/shard_map/fetch_up_0/pallas_call | solution.py:300
  19.3 0.6 collective-permute-start.5
  19.9 1.4 %collective-permute-done.1 = bf16[32,768]{1,0:T(8,128)(2,1)S(1)} collective-permute-done((bf16[32,768]{1,0:T(8,128)(2,1)S(1)}, bf16[32,768]{1,0:T(8,128)(2,1)S(1)}, u32[]{:S(2)}, u32[]{:S(2)}) %collective-permute-start.1) | collective-permute-done | bytes 49184 | tf_op jit(solution)/shard_map/ppermute | solution.py:237
  21.3 1.5 %collective-permute-start.4 = (bf16[32,3072]{1,0:T(8,128)(2,1)S(1)}, bf16[32,3072]{1,0:T(8,128)(2,1)S(1)}, u32[]{:S(2)}, u32[]{:S(2)}) collective-permute-start(bf16[32,3072]{1,0:T(8,128)(2,1)S(1)} %get-tuple-element.39.refs_4_), channel_id=1, source_target_pairs={{0,8},{4,12},{8,0},{12,4},{1,9},{5,13},{9,1},{13,5},{2,10},{6,14},... | collective-permute-start | bytes 589832 | tf_op jit(solution)/shard_map/ppermute | solution.py:237
  22.8 0.6 collective-permute-start.3
  23.4 3.8 %collective-permute-done.4.refs_6_ = bf16[32,3072]{1,0:T(8,128)(2,1)S(1)} collective-permute-done((bf16[32,3072]{1,0:T(8,128)(2,1)S(1)}, bf16[32,3072]{1,0:T(8,128)(2,1)S(1)}, u32[]{:S(2)}, u32[]{:S(2)}) %collective-permute-start.4) | collective-permute-done | bytes 196640 | tf_op jit(solution)/shard_map/ppermute | solution.py:237
  27.3 0.5 collective-permute-start.8
  27.8 1.0 collective-permute-done.5.refs_1_
  28.7 0.6 collective-permute-done.3.refs_2_
  29.4 0.5 collective-permute-start.11
  29.9 0.9 collective-permute-done.9.refs_3_
  30.8 0.3 collective-permute-done.11.refs_7_
  31.1 0.6 assemble_factors.1
  31.7 0.0 copy-start.1
  31.7 8.1 %block.2 = (f32[32,3072]{1,0:T(8,128)S(1)}, bf16[32,3072]{1,0:T(8,128)(2,1)S(1)}, bf16[32,1536]{1,0:T(8,128)(2,1)S(1)}, f32[32,1536]{1,0:T(8,128)S(1)}, bf16[32,...) custom-call(bf16[32,3072]{1,0:T(8,128)(2,1)S(1)} %get-tuple-element., ...), custom_call_target="tpu_custom_call" | custom-call | flops 4831838208 | bytes 37748736 | tf_op jit(solution)/shard_map/block/pallas_call | solution.py:335
  39.8 1.5 %collective-permute-start.13 = (bf16[32,1536]{1,0:T(8,128)(2,1)S(1)}, bf16[32,1536]{1,0:T(8,128)(2,1)S(1)}, u32[]{:S(2)}, u32[]{:S(2)}) collective-permute-start(bf16[32,1536]{1,0:T(8,128)(2,1)S(1)} %get-tuple-element.56), channel_id=1, source_target_pairs={{0,1},{1,0},{2,3},{3,2},{4,5},{5,4},{6,7},{7,6},{8,9},{9,8},{10,11... | collective-permute-start | bytes 294920 | tf_op jit(solution)/shard_map/ppermute | solution.py:237
  41.3 0.6 collective-permute-start.12
  41.9 2.4 %collective-permute-start.15 = (bf16[32,1536]{1,0:T(8,128)(2,1)S(1)}, bf16[32,1536]{1,0:T(8,128)(2,1)S(1)}, u32[]{:S(2)}, u32[]{:S(2)}) collective-permute-start(bf16[32,1536]{1,0:T(8,128)(2,1)S(1)} %get-tuple-element.57), channel_id=1, source_target_pairs={{0,2},{1,3},{2,0},{3,1},{4,6},{5,7},{6,4},{7,5},{8,10},{9,11},{10,... | collective-permute-start | bytes 294920 | tf_op jit(solution)/shard_map/ppermute | solution.py:237
  44.3 1.5 %collective-permute-start.16 = (bf16[32,1536]{1,0:T(8,128)(2,1)S(1)}, bf16[32,1536]{1,0:T(8,128)(2,1)S(1)}, u32[]{:S(2)}, u32[]{:S(2)}) collective-permute-start(bf16[32,1536]{1,0:T(8,128)(2,1)S(1)} %get-tuple-element.58), channel_id=1, source_target_pairs={{0,3},{1,2},{2,1},{3,0},{4,7},{5,6},{6,5},{7,4},{8,11},{9,10},{10,... | collective-permute-start | bytes 294920 | tf_op jit(solution)/shard_map/ppermute | solution.py:237
  45.7 1.2 %collective-permute-done.13.got_ref = bf16[32,1536]{1,0:T(8,128)(2,1)S(1)} collective-permute-done((bf16[32,1536]{1,0:T(8,128)(2,1)S(1)}, bf16[32,1536]{1,0:T(8,128)(2,1)S(1)}, u32[]{:S(2)}, u32[]{:S(2)}) %collective-permute-start.13) | collective-permute-done | bytes 98336 | tf_op jit(solution)/shard_map/ppermute | solution.py:237
  46.9 1.0 %collective-permute-start.14 = (bf16[32,1536]{1,0:T(8,128)(2,1)S(1)}, bf16[32,1536]{1,0:T(8,128)(2,1)S(1)}, u32[]{:S(2)}, u32[]{:S(2)}) collective-permute-start(bf16[32,1536]{1,0:T(8,128)(2,1)S(1)} %relay.2), channel_id=1, source_target_pairs={{0,2},{1,3},{2,0},{3,1},{4,6},{5,7},{6,4},{7,5},{8,10},{9,11},{10,... | collective-permute-start | bytes 294920 | tf_op jit(solution)/shard_map/ppermute | solution.py:237
  48.0 2.9 %collective-permute-done.15.refs_3_ = bf16[32,1536]{1,0:T(8,128)(2,1)S(1)} collective-permute-done((bf16[32,1536]{1,0:T(8,128)(2,1)S(1)}, bf16[32,1536]{1,0:T(8,128)(2,1)S(1)}, u32[]{:S(2)}, u32[]{:S(2)}) %collective-permute-start.15) | collective-permute-done | bytes 98336 | tf_op jit(solution)/shard_map/ppermute | solution.py:237
  50.9 5.0 %collective-permute-done.16.refs_4_ = bf16[32,1536]{1,0:T(8,128)(2,1)S(1)} collective-permute-done((bf16[32,1536]{1,0:T(8,128)(2,1)S(1)}, bf16[32,1536]{1,0:T(8,128)(2,1)S(1)}, u32[]{:S(2)}, u32[]{:S(2)}) %collective-permute-start.16) | collective-permute-done | bytes 98336 | tf_op jit(solution)/shard_map/ppermute | solution.py:237
  55.8 2.3 %collective-permute-done.14.refs_2_ = bf16[32,1536]{1,0:T(8,128)(2,1)S(1)} collective-permute-done((bf16[32,1536]{1,0:T(8,128)(2,1)S(1)}, bf16[32,1536]{1,0:T(8,128)(2,1)S(1)}, u32[]{:S(2)}, u32[]{:S(2)}) %collective-permute-start.14) | collective-permute-done | bytes 98336 | tf_op jit(solution)/shard_map/ppermute | solution.py:237
  58.2 0.9 first_update.1
  59.1 0.4 collective-permute-start.18
  59.5 2.5 %collective-permute-start.17 = (bf16[32,3072]{1,0:T(8,128)(2,1)S(1)}, bf16[32,3072]{1,0:T(8,128)(2,1)S(1)}, u32[]{:S(2)}, u32[]{:S(2)}) collective-permute-start(bf16[32,3072]{1,0:T(8,128)(2,1)S(1)} %get-tuple-element.61.refs_0_), channel_id=1, source_target_pairs={{0,1},{1,0},{2,3},{3,2},{4,5},{5,4},{6,7},{7,6},{8,9},{9,8},{10,11... | collective-permute-start | bytes 589832 | tf_op jit(solution)/shard_map/ppermute | solution.py:237
  62.0 1.6 %collective-permute-start.21 = (bf16[32,1536]{1,0:T(8,128)(2,1)S(1)}, bf16[32,1536]{1,0:T(8,128)(2,1)S(1)}, u32[]{:S(2)}, u32[]{:S(2)}) collective-permute-start(bf16[32,1536]{1,0:T(8,128)(2,1)S(1)} %get-tuple-element.63), channel_id=1, source_target_pairs={{0,3},{1,2},{2,1},{3,0},{4,7},{5,6},{6,5},{7,4},{8,11},{9,10},{10,... | collective-permute-start | bytes 294920 | tf_op jit(solution)/shard_map/ppermute | solution.py:237
  63.6 4.1 %collective-permute-done.18.refs_2_ = bf16[32,1536]{1,0:T(8,128)(2,1)S(1)} collective-permute-done((bf16[32,1536]{1,0:T(8,128)(2,1)S(1)}, bf16[32,1536]{1,0:T(8,128)(2,1)S(1)}, u32[]{:S(2)}, u32[]{:S(2)}) %collective-permute-start.18) | collective-permute-done | bytes 98336 | tf_op jit(solution)/shard_map/ppermute | solution.py:237
  67.7 3.8 %collective-permute-done.21.refs_5_ = bf16[32,1536]{1,0:T(8,128)(2,1)S(1)} collective-permute-done((bf16[32,1536]{1,0:T(8,128)(2,1)S(1)}, bf16[32,1536]{1,0:T(8,128)(2,1)S(1)}, u32[]{:S(2)}, u32[]{:S(2)}) %collective-permute-start.21) | collective-permute-done | bytes 98336 | tf_op jit(solution)/shard_map/ppermute | solution.py:237
  71.5 1.5 %collective-permute-done.20.refs_4_ = bf16[32,1536]{1,0:T(8,128)(2,1)S(1)} collective-permute-done((bf16[32,1536]{1,0:T(8,128)(2,1)S(1)}, bf16[32,1536]{1,0:T(8,128)(2,1)S(1)}, u32[]{:S(2)}, u32[]{:S(2)}) %collective-permute-start.20) | collective-permute-done | bytes 98336 | tf_op jit(solution)/shard_map/ppermute | solution.py:237
  73.0 6.1 %block.3 = (f32[32,3072]{1,0:T(8,128)S(1)}, bf16[32,3072]{1,0:T(8,128)(2,1)S(1)}, bf16[32,1536]{1,0:T(8,128)(2,1)S(1)}, f32[32,1536]{1,0:T(8,128)S(1)}, bf16[32,...) custom-call(bf16[32,3072]{1,0:T(8,128)(2,1)S(1)} %get-tuple-element.61.refs_0_, ...), custom_call_target="tpu_custom_call" | custom-call | flops 4831838208 | bytes 37748736 | tf_op jit(solution)/shard_map/block/pallas_call | solution.py:335
  79.1 1.7 %collective-permute-start.23 = (bf16[32,1536]{1,0:T(8,128)(2,1)S(1)}, bf16[32,1536]{1,0:T(8,128)(2,1)S(1)}, u32[]{:S(2)}, u32[]{:S(2)}) collective-permute-start(bf16[32,1536]{1,0:T(8,128)(2,1)S(1)} %get-tuple-element.69), channel_id=1, source_target_pairs={{0,1},{1,0},{2,3},{3,2},{4,5},{5,4},{6,7},{7,6},{8,9},{9,8},{10,11... | collective-permute-start | bytes 294920 | tf_op jit(solution)/shard_map/ppermute | solution.py:237
  80.8 0.4 collective-permute-start.22
  81.2 1.5 %collective-permute-start.25 = (bf16[32,1536]{1,0:T(8,128)(2,1)S(1)}, bf16[32,1536]{1,0:T(8,128)(2,1)S(1)}, u32[]{:S(2)}, u32[]{:S(2)}) collective-permute-start(bf16[32,1536]{1,0:T(8,128)(2,1)S(1)} %get-tuple-element.70), channel_id=1, source_target_pairs={{0,2},{1,3},{2,0},{3,1},{4,6},{5,7},{6,4},{7,5},{8,10},{9,11},{10,... | collective-permute-start | bytes 294920 | tf_op jit(solution)/shard_map/ppermute | solution.py:237
  82.7 2.5 %collective-permute-start.26 = (bf16[32,1536]{1,0:T(8,128)(2,1)S(1)}, bf16[32,1536]{1,0:T(8,128)(2,1)S(1)}, u32[]{:S(2)}, u32[]{:S(2)}) collective-permute-start(bf16[32,1536]{1,0:T(8,128)(2,1)S(1)} %get-tuple-element.71), channel_id=1, source_target_pairs={{0,3},{1,2},{2,1},{3,0},{4,7},{5,6},{6,5},{7,4},{8,11},{9,10},{10,... | collective-permute-start | bytes 294920 | tf_op jit(solution)/shard_map/ppermute | solution.py:237
  85.2 0.7 collective-permute-done.23.got_ref
  85.9 0.4 collective-permute-start.24
  86.3 3.7 %collective-permute-done.25.refs_3_ = bf16[32,1536]{1,0:T(8,128)(2,1)S(1)} collective-permute-done((bf16[32,1536]{1,0:T(8,128)(2,1)S(1)}, bf16[32,1536]{1,0:T(8,128)(2,1)S(1)}, u32[]{:S(2)}, u32[]{:S(2)}) %collective-permute-start.25) | collective-permute-done | bytes 98336 | tf_op jit(solution)/shard_map/ppermute | solution.py:237
  90.0 2.0 %collective-permute-done.26.refs_4_ = bf16[32,1536]{1,0:T(8,128)(2,1)S(1)} collective-permute-done((bf16[32,1536]{1,0:T(8,128)(2,1)S(1)}, bf16[32,1536]{1,0:T(8,128)(2,1)S(1)}, u32[]{:S(2)}, u32[]{:S(2)}) %collective-permute-start.26) | collective-permute-done | bytes 98336 | tf_op jit(solution)/shard_map/ppermute | solution.py:237
  92.1 3.3 %collective-permute-done.24.refs_2_ = bf16[32,1536]{1,0:T(8,128)(2,1)S(1)} collective-permute-done((bf16[32,1536]{1,0:T(8,128)(2,1)S(1)}, bf16[32,1536]{1,0:T(8,128)(2,1)S(1)}, u32[]{:S(2)}, u32[]{:S(2)}) %collective-permute-start.24) | collective-permute-done | bytes 98336 | tf_op jit(solution)/shard_map/ppermute | solution.py:237
  95.4 1.7 %second_update.1 = (f32[2,32,3072]{2,1,0:T(8,128)}, f32[32,3072]{1,0:T(8,128)}) custom-call(s32[2]{0:T(128)S(1)} %copy-done.2, f32[3,4,3072]{2,1,0:T(4,128)S(1)} %bitcast.5, f32[32,3072]{1,0:T(8,128)S(1)} %get-tuple-element.59.vel_ref, f32[32,3072]{1,0:T(8,128)S(1)} %get-tuple-element.60.state_ref, f32[32,3072]{1,0:T(8,128)S(1)} %get-tuple-element.66.refs_0_, ...), custom_call_target="tpu_custom_call" | custom-call | tf_op jit(solution)/shard_map/second_update/pallas_call | solution.py:366
  (23 shorter events, 0.1 us)
Async XLA Ops:
  2.1 17.1 %collective-permute-start.2 = (bf16[32,768]{1,0:T(8,128)(2,1)S(1)}, bf16[32,768]{1,0:T(8,128)(2,1)S(1)}, u32[]{:S(2)}, u32[]{:S(2)}) collective-permute-start(bf16[32,768]{1,0:T(8,128)(2,1)S(1)} %get-tuple-element.37), channel_id=1, source_target_pairs={{0,3},{1,2},{2,1},{3,0},{4,7},{5,6},{6,5},{7,4},{8,11},{9,10},{10,... | collective-permute-start | bytes 147464 | tf_op jit(solution)/shard_map/ppermute | solution.py:237
  7.2 14.1 %collective-permute-start.1 = (bf16[32,768]{1,0:T(8,128)(2,1)S(1)}, bf16[32,768]{1,0:T(8,128)(2,1)S(1)}, u32[]{:S(2)}, u32[]{:S(2)}) collective-permute-start(bf16[32,768]{1,0:T(8,128)(2,1)S(1)} %get-tuple-element.37), channel_id=1, source_target_pairs={{0,2},{1,3},{2,0},{3,1},{4,6},{5,7},{6,4},{7,5},{8,10},{9,11},{10,... | collective-permute-start | bytes 147464 | tf_op jit(solution)/shard_map/ppermute | solution.py:237
  7.2 15.5 %collective-permute-start = (bf16[32,768]{1,0:T(8,128)(2,1)S(1)}, bf16[32,768]{1,0:T(8,128)(2,1)S(1)}, u32[]{:S(2)}, u32[]{:S(2)}) collective-permute-start(bf16[32,768]{1,0:T(8,128)(2,1)S(1)} %get-tuple-element.37), channel_id=1, source_target_pairs={{0,1},{1,0},{2,3},{3,2},{4,5},{5,4},{6,7},{7,6},{8,9},{9,8},{10,11... | collective-permute-start | bytes 147464 | tf_op jit(solution)/shard_map/ppermute | solution.py:237
  7.9 19.4 %collective-permute-start.7 = (bf16[32,3072]{1,0:T(8,128)(2,1)S(1)}, bf16[32,3072]{1,0:T(8,128)(2,1)S(1)}, u32[]{:S(2)}, u32[]{:S(2)}) collective-permute-start(bf16[32,3072]{1,0:T(8,128)(2,1)S(1)} %get-tuple-element.41.refs_0_), channel_id=1, source_target_pairs={{0,2},{1,3},{2,0},{3,1},{4,6},{5,7},{6,4},{7,5},{8,10},{9,11},{10,... | collective-permute-start | bytes 589832 | tf_op jit(solution)/shard_map/ppermute | solution.py:237
  10.2 17.6 %collective-permute-start.6 = (bf16[32,3072]{1,0:T(8,128)(2,1)S(1)}, bf16[32,3072]{1,0:T(8,128)(2,1)S(1)}, u32[]{:S(2)}, u32[]{:S(2)}) collective-permute-start(bf16[32,3072]{1,0:T(8,128)(2,1)S(1)} %get-tuple-element.41.refs_0_), channel_id=1, source_target_pairs={{0,3},{1,2},{2,1},{3,0},{4,7},{5,6},{6,5},{7,4},{8,11},{9,10},{10,... | collective-permute-start | bytes 589832 | tf_op jit(solution)/shard_map/ppermute | solution.py:237
  19.3 9.5 %collective-permute-start.5 = (bf16[32,3072]{1,0:T(8,128)(2,1)S(1)}, bf16[32,3072]{1,0:T(8,128)(2,1)S(1)}, u32[]{:S(2)}, u32[]{:S(2)}) collective-permute-start(bf16[32,3072]{1,0:T(8,128)(2,1)S(1)} %get-tuple-element.41.refs_0_), channel_id=1, source_target_pairs={{0,1},{1,0},{2,3},{3,2},{4,5},{5,4},{6,7},{7,6},{8,9},{9,8},{10,11... | collective-permute-start | bytes 589832 | tf_op jit(solution)/shard_map/ppermute | solution.py:237
  21.3 6.0 %collective-permute-start.4 = (bf16[32,3072]{1,0:T(8,128)(2,1)S(1)}, bf16[32,3072]{1,0:T(8,128)(2,1)S(1)}, u32[]{:S(2)}, u32[]{:S(2)}) collective-permute-start(bf16[32,3072]{1,0:T(8,128)(2,1)S(1)} %get-tuple-element.39.refs_4_), channel_id=1, source_target_pairs={{0,8},{4,12},{8,0},{12,4},{1,9},{5,13},{9,1},{13,5},{2,10},{6,14},... | collective-permute-start | bytes 589832 | tf_op jit(solution)/shard_map/ppermute | solution.py:237
  22.8 6.5 %collective-permute-start.3 = (bf16[32,3072]{1,0:T(8,128)(2,1)S(1)}, bf16[32,3072]{1,0:T(8,128)(2,1)S(1)}, u32[]{:S(2)}, u32[]{:S(2)}) collective-permute-start(bf16[32,3072]{1,0:T(8,128)(2,1)S(1)} %pad_maximum_fusion.refs_0_), channel_id=1, source_target_pairs={{0,8},{4,12},{8,0},{12,4},{1,9},{5,13},{9,1},{13,5},{2,10},{6,14},... | collective-permute-start | bytes 589832 | tf_op jit(solution)/shard_map/ppermute | solution.py:237
  27.2 2.6 %collective-permute-start.10 = (bf16[32,3072]{1,0:T(8,128)(2,1)S(1)}, bf16[32,3072]{1,0:T(8,128)(2,1)S(1)}, u32[]{:S(2)}, u32[]{:S(2)}) collective-permute-start(bf16[32,3072]{1,0:T(8,128)(2,1)S(1)} %get-tuple-element.39.refs_4_), channel_id=1, source_target_pairs={{0,4},{4,0},{8,12},{12,8},{1,5},{5,1},{9,13},{13,9},{2,6},{6,2},{1... | collective-permute-start | bytes 589832 | tf_op jit(solution)/shard_map/ppermute | solution.py:237
  27.3 2.6 %collective-permute-start.8 = (bf16[32,3072]{1,0:T(8,128)(2,1)S(1)}, bf16[32,3072]{1,0:T(8,128)(2,1)S(1)}, u32[]{:S(2)}, u32[]{:S(2)}) collective-permute-start(bf16[32,3072]{1,0:T(8,128)(2,1)S(1)} %pad_maximum_fusion.refs_0_), channel_id=1, source_target_pairs={{0,4},{4,0},{8,12},{12,8},{1,5},{5,1},{9,13},{13,9},{2,6},{6,2},{1... | collective-permute-start | bytes 589832 | tf_op jit(solution)/shard_map/ppermute | solution.py:237
  29.4 1.4 %collective-permute-start.9 = (bf16[32,3072]{1,0:T(8,128)(2,1)S(1)}, bf16[32,3072]{1,0:T(8,128)(2,1)S(1)}, u32[]{:S(2)}, u32[]{:S(2)}) collective-permute-start(bf16[32,3072]{1,0:T(8,128)(2,1)S(1)} %collective-permute-done.3.refs_2_), channel_id=1, source_target_pairs={{0,4},{4,0},{8,12},{12,8},{1,5},{5,1},{9,13},{13,9},{2,6},{6,2},{1... | collective-permute-start | bytes 589832 | tf_op jit(solution)/shard_map/ppermute | solution.py:237
  29.4 1.7 %collective-permute-start.11 = (bf16[32,3072]{1,0:T(8,128)(2,1)S(1)}, bf16[32,3072]{1,0:T(8,128)(2,1)S(1)}, u32[]{:S(2)}, u32[]{:S(2)}) collective-permute-start(bf16[32,3072]{1,0:T(8,128)(2,1)S(1)} %collective-permute-done.4.refs_6_), channel_id=1, source_target_pairs={{0,4},{4,0},{8,12},{12,8},{1,5},{5,1},{9,13},{13,9},{2,6},{6,2},{1... | collective-permute-start | bytes 589832 | tf_op jit(solution)/shard_map/ppermute | solution.py:237
  31.7 26.5 %copy-start = (f32[4,3,3072]{2,0,1:T(4,128)S(1)}, f32[4,3,3072]{2,0,1:T(4,128)}, u32[]{:S(2)}) copy-start(f32[4,3,3072]{2,0,1:T(4,128)} %param.11) | copy-start | bytes 442372
  31.7 26.4 %copy-start.1 = (bf16[32,3072]{1,0:T(8,128)(2,1)S(1)}, bf16[32,3072]{1,0:T(8,128)(2,1)}, u32[]{:S(2)}) copy-start(bf16[32,3072]{1,0:T(8,128)(2,1)} %lat_ref.1) | copy-start | bytes 589828
  31.7 26.4 %copy-start.2 = (s32[2]{0:T(128)S(1)}, s32[2]{0:T(128)}, u32[]{:S(2)}) copy-start(s32[2]{0:T(128)} %steps_ref.3) | copy-start | bytes 28
  39.8 7.1 %collective-permute-start.13 = (bf16[32,1536]{1,0:T(8,128)(2,1)S(1)}, bf16[32,1536]{1,0:T(8,128)(2,1)S(1)}, u32[]{:S(2)}, u32[]{:S(2)}) collective-permute-start(bf16[32,1536]{1,0:T(8,128)(2,1)S(1)} %get-tuple-element.56), channel_id=1, source_target_pairs={{0,1},{1,0},{2,3},{3,2},{4,5},{5,4},{6,7},{7,6},{8,9},{9,8},{10,11... | collective-permute-start | bytes 294920 | tf_op jit(solution)/shard_map/ppermute | solution.py:237
  41.3 16.8 %collective-permute-start.12 = (bf16[32,3072]{1,0:T(8,128)(2,1)S(1)}, bf16[32,3072]{1,0:T(8,128)(2,1)S(1)}, u32[]{:S(2)}, u32[]{:S(2)}) collective-permute-start(bf16[32,3072]{1,0:T(8,128)(2,1)S(1)} %get-tuple-element.54), channel_id=1, source_target_pairs={{0,1},{1,0},{2,3},{3,2},{4,5},{5,4},{6,7},{7,6},{8,9},{9,8},{10,11... | collective-permute-start | bytes 589832 | tf_op jit(solution)/shard_map/ppermute | solution.py:237
  41.9 8.9 %collective-permute-start.15 = (bf16[32,1536]{1,0:T(8,128)(2,1)S(1)}, bf16[32,1536]{1,0:T(8,128)(2,1)S(1)}, u32[]{:S(2)}, u32[]{:S(2)}) collective-permute-start(bf16[32,1536]{1,0:T(8,128)(2,1)S(1)} %get-tuple-element.57), channel_id=1, source_target_pairs={{0,2},{1,3},{2,0},{3,1},{4,6},{5,7},{6,4},{7,5},{8,10},{9,11},{10,... | collective-permute-start | bytes 294920 | tf_op jit(solution)/shard_map/ppermute | solution.py:237
  44.3 11.6 %collective-permute-start.16 = (bf16[32,1536]{1,0:T(8,128)(2,1)S(1)}, bf16[32,1536]{1,0:T(8,128)(2,1)S(1)}, u32[]{:S(2)}, u32[]{:S(2)}) collective-permute-start(bf16[32,1536]{1,0:T(8,128)(2,1)S(1)} %get-tuple-element.58), channel_id=1, source_target_pairs={{0,3},{1,2},{2,1},{3,0},{4,7},{5,6},{6,5},{7,4},{8,11},{9,10},{10,... | collective-permute-start | bytes 294920 | tf_op jit(solution)/shard_map/ppermute | solution.py:237
  46.9 11.2 %collective-permute-start.14 = (bf16[32,1536]{1,0:T(8,128)(2,1)S(1)}, bf16[32,1536]{1,0:T(8,128)(2,1)S(1)}, u32[]{:S(2)}, u32[]{:S(2)}) collective-permute-start(bf16[32,1536]{1,0:T(8,128)(2,1)S(1)} %relay.2), channel_id=1, source_target_pairs={{0,2},{1,3},{2,0},{3,1},{4,6},{5,7},{6,4},{7,5},{8,10},{9,11},{10,... | collective-permute-start | bytes 294920 | tf_op jit(solution)/shard_map/ppermute | solution.py:237
  59.1 8.6 %collective-permute-start.18 = (bf16[32,1536]{1,0:T(8,128)(2,1)S(1)}, bf16[32,1536]{1,0:T(8,128)(2,1)S(1)}, u32[]{:S(2)}, u32[]{:S(2)}) collective-permute-start(bf16[32,1536]{1,0:T(8,128)(2,1)S(1)} %get-tuple-element.62), channel_id=1, source_target_pairs={{0,2},{1,3},{2,0},{3,1},{4,6},{5,7},{6,4},{7,5},{8,10},{9,11},{10,... | collective-permute-start | bytes 294920 | tf_op jit(solution)/shard_map/ppermute | solution.py:237
  59.5 13.5 %collective-permute-start.17 = (bf16[32,3072]{1,0:T(8,128)(2,1)S(1)}, bf16[32,3072]{1,0:T(8,128)(2,1)S(1)}, u32[]{:S(2)}, u32[]{:S(2)}) collective-permute-start(bf16[32,3072]{1,0:T(8,128)(2,1)S(1)} %get-tuple-element.61.refs_0_), channel_id=1, source_target_pairs={{0,1},{1,0},{2,3},{3,2},{4,5},{5,4},{6,7},{7,6},{8,9},{9,8},{10,11... | collective-permute-start | bytes 589832 | tf_op jit(solution)/shard_map/ppermute | solution.py:237
  62.0 9.5 %collective-permute-start.21 = (bf16[32,1536]{1,0:T(8,128)(2,1)S(1)}, bf16[32,1536]{1,0:T(8,128)(2,1)S(1)}, u32[]{:S(2)}, u32[]{:S(2)}) collective-permute-start(bf16[32,1536]{1,0:T(8,128)(2,1)S(1)} %get-tuple-element.63), channel_id=1, source_target_pairs={{0,3},{1,2},{2,1},{3,0},{4,7},{5,6},{6,5},{7,4},{8,11},{9,10},{10,... | collective-permute-start | bytes 294920 | tf_op jit(solution)/shard_map/ppermute | solution.py:237
  63.6 9.5 %collective-permute-start.20 = (bf16[32,1536]{1,0:T(8,128)(2,1)S(1)}, bf16[32,1536]{1,0:T(8,128)(2,1)S(1)}, u32[]{:S(2)}, u32[]{:S(2)}) collective-permute-start(bf16[32,1536]{1,0:T(8,128)(2,1)S(1)} %get-tuple-element.63), channel_id=1, source_target_pairs={{0,2},{1,3},{2,0},{3,1},{4,6},{5,7},{6,4},{7,5},{8,10},{9,11},{10,... | collective-permute-start | bytes 294920 | tf_op jit(solution)/shard_map/ppermute | solution.py:237
  67.7 5.3 %collective-permute-start.19 = (bf16[32,1536]{1,0:T(8,128)(2,1)S(1)}, bf16[32,1536]{1,0:T(8,128)(2,1)S(1)}, u32[]{:S(2)}, u32[]{:S(2)}) collective-permute-start(bf16[32,1536]{1,0:T(8,128)(2,1)S(1)} %collective-permute-done.18.refs_2_), channel_id=1, source_target_pairs={{0,1},{1,0},{2,3},{3,2},{4,5},{5,4},{6,7},{7,6},{8,9},{9,8},{10,11... | collective-permute-start | bytes 294920 | tf_op jit(solution)/shard_map/ppermute | solution.py:237
  79.1 6.8 %collective-permute-start.23 = (bf16[32,1536]{1,0:T(8,128)(2,1)S(1)}, bf16[32,1536]{1,0:T(8,128)(2,1)S(1)}, u32[]{:S(2)}, u32[]{:S(2)}) collective-permute-start(bf16[32,1536]{1,0:T(8,128)(2,1)S(1)} %get-tuple-element.69), channel_id=1, source_target_pairs={{0,1},{1,0},{2,3},{3,2},{4,5},{5,4},{6,7},{7,6},{8,9},{9,8},{10,11... | collective-permute-start | bytes 294920 | tf_op jit(solution)/shard_map/ppermute | solution.py:237
  80.8 11.3 %collective-permute-start.22 = (bf16[32,3072]{1,0:T(8,128)(2,1)S(1)}, bf16[32,3072]{1,0:T(8,128)(2,1)S(1)}, u32[]{:S(2)}, u32[]{:S(2)}) collective-permute-start(bf16[32,3072]{1,0:T(8,128)(2,1)S(1)} %get-tuple-element.67), channel_id=1, source_target_pairs={{0,1},{1,0},{2,3},{3,2},{4,5},{5,4},{6,7},{7,6},{8,9},{9,8},{10,11... | collective-permute-start | bytes 589832 | tf_op jit(solution)/shard_map/ppermute | solution.py:237
  81.2 8.8 %collective-permute-start.25 = (bf16[32,1536]{1,0:T(8,128)(2,1)S(1)}, bf16[32,1536]{1,0:T(8,128)(2,1)S(1)}, u32[]{:S(2)}, u32[]{:S(2)}) collective-permute-start(bf16[32,1536]{1,0:T(8,128)(2,1)S(1)} %get-tuple-element.70), channel_id=1, source_target_pairs={{0,2},{1,3},{2,0},{3,1},{4,6},{5,7},{6,4},{7,5},{8,10},{9,11},{10,... | collective-permute-start | bytes 294920 | tf_op jit(solution)/shard_map/ppermute | solution.py:237
  82.7 9.4 %collective-permute-start.26 = (bf16[32,1536]{1,0:T(8,128)(2,1)S(1)}, bf16[32,1536]{1,0:T(8,128)(2,1)S(1)}, u32[]{:S(2)}, u32[]{:S(2)}) collective-permute-start(bf16[32,1536]{1,0:T(8,128)(2,1)S(1)} %get-tuple-element.71), channel_id=1, source_target_pairs={{0,3},{1,2},{2,1},{3,0},{4,7},{5,6},{6,5},{7,4},{8,11},{9,10},{10,... | collective-permute-start | bytes 294920 | tf_op jit(solution)/shard_map/ppermute | solution.py:237
  85.9 9.4 %collective-permute-start.24 = (bf16[32,1536]{1,0:T(8,128)(2,1)S(1)}, bf16[32,1536]{1,0:T(8,128)(2,1)S(1)}, u32[]{:S(2)}, u32[]{:S(2)}) collective-permute-start(bf16[32,1536]{1,0:T(8,128)(2,1)S(1)} %relay.3), channel_id=1, source_target_pairs={{0,2},{1,3},{2,0},{3,1},{4,6},{5,7},{6,4},{7,5},{8,10},{9,11},{10,... | collective-permute-start | bytes 294920 | tf_op jit(solution)/shard_map/ppermute | solution.py:237

commit v4 on v3

--- a/solution.py
+++ b/solution.py
@@ -9,7 +9,6 @@
 
 NSTEPS = 4
 STREAMS = 4
-TOKEN_ORDER = (1, 3, 2)
 STEP_SIZE = -1.0 / NSTEPS
 BF16, F32 = jnp.bfloat16, jnp.float32
 VMEM_GRANT = 4 << 20
@@ -45,6 +44,13 @@
     return (centered * lax.rsqrt(spread + 1e-06) * (1.0 + scale) + shift).astype(BF16)
 
 
+def spread_out(normed, out_ref, far_ref, rest_ref):
+    half = far_ref.shape[1]
+    out_ref[...] = normed
+    far_ref[...] = normed[:, :half]
+    rest_ref[...] = normed[:, half:]
+
+
 def gelu(x):
     return x * (0.5 * (1.0 + jnp.tanh(0.7978845608028654 * (x + 0.044715 * (x * x * x)))))
 
@@ -59,7 +65,7 @@
 
 
 def prepare_body(slots, rank, *refs):
-    sources, outs, held, sems = refs[:7], refs[7:10], refs[10:17], refs[-1]
+    sources, outs, held, sems = refs[:7], refs[7:12], refs[12:19], refs[-1]
     copies = [
         pltpu.make_async_copy(src, dst, sems.at[i])
         for i, (src, dst) in enumerate(zip(sources, held))
@@ -90,7 +96,7 @@
     q_ref[rank : 2 * rank, :] = da_ref[...]
     step = steps_ref[own_image(lat_ref.shape[0], steps_ref.shape[0])]
     state = lat_ref[...].astype(F32)
-    outs[2][...] = modulated(state, mod_row(mod_ref, 0, step), mod_row(mod_ref, 1, step))
+    spread_out(modulated(state, mod_row(mod_ref, 0, step), mod_row(mod_ref, 1, step)), *outs[2:])
 
 
 def fetch_body(start, source, target, sems):
@@ -145,48 +151,34 @@
         pltpu.make_async_copy(source.at[block, cols], target.at[block], sems.at[i]).start()
 
 
-def block_body(streamed, rank, *refs):
-    given = 4 if streamed else 6
-    x_refs, refs = refs[:given], refs[given:]
-    (p_ref, q_ref, pt_ref, qt_ref), wu_refs, refs = refs[:4], refs[4:6], refs[6:]
-    if streamed:
-        source, outs, wd_refs, (x_all, hidden, sems) = refs[0], refs[1:7], refs[7:9], refs[9:]
-        for i, target in enumerate(wd_refs):
-            start_stream(source, target, sems.at[i], i * target.shape[1])
-    else:
-        wd_refs, outs, (x_all, hidden) = refs[:2], refs[2:8], refs[8:]
+def block_body(rank, *refs):
+    x_refs, (p_ref, q_ref, pt_ref, qt_ref, wu_ref, wd_ref), refs = refs[:6], refs[6:12], refs[12:]
+    outs, (x_all, hidden) = refs[:6], refs[6:]
     count, width = x_refs[0].shape
     half = width // 2
-    if streamed:
-        for k, x_ref in enumerate(x_refs):
-            x_all[k * count : (k + 1) * count, :] = x_ref[...]
-    else:
-        own_ref, near_ref, far_ref, over_ref, rest_2_ref, rest_3_ref = x_refs
-        x_all[:count, :] = own_ref[...]
-        x_all[count : 2 * count, :] = near_ref[...]
-        x_all[2 * count : 3 * count, :half] = far_ref[...]
-        x_all[2 * count : 3 * count, half:] = rest_2_ref[...]
-        x_all[3 * count :, :half] = over_ref[...]
-        x_all[3 * count :, half:] = rest_3_ref[...]
+    own_ref, near_ref, far_ref, over_ref, rest_2_ref, rest_3_ref = x_refs
+    x_all[:count, :] = own_ref[...]
+    x_all[count : 2 * count, :] = near_ref[...]
+    x_all[2 * count : 3 * count, :half] = far_ref[...]
+    x_all[2 * count : 3 * count, half:] = rest_2_ref[...]
+    x_all[3 * count :, :half] = over_ref[...]
+    x_all[3 * count :, half:] = rest_3_ref[...]
     lanes = lax.broadcasted_iota(jnp.int32, (1, p_ref.shape[1]), 1)
     first_half = (lanes // rank) % 2 == 0
     low = jnp.dot(x_all[...], p_ref[...], preferred_element_type=F32)
     low = jnp.where(first_half, low, 0.0).astype(BF16)
-    tile = wu_refs[0].shape[1]
-    for i, wu_ref in enumerate(wu_refs):
+    tile = hidden.shape[1] // 2
+    for i in range(2):
         cols = slice(i * tile, (i + 1) * tile)
-        upper = jnp.dot(x_all[...], wu_ref[...], preferred_element_type=F32)
+        upper = jnp.dot(x_all[...], wu_ref[:, cols], preferred_element_type=F32)
         upper += jnp.dot(low, q_ref[:, cols], preferred_element_type=F32)
         hidden[:, cols] = gelu(upper).astype(BF16)
     low = jnp.dot(hidden[...], qt_ref[...], preferred_element_type=F32)
     low = jnp.where(first_half, 0.0, low).astype(BF16)
     own_out, near_out, over_out, far_out, rest_2_out, rest_3_out = outs
-    for i, wd_ref in enumerate(wd_refs):
+    for i in range(2):
         cols = slice(i * half, (i + 1) * half)
-        if streamed:
-            for copy in stream_copies(source, wd_ref, sems.at[i], i * half):
-                copy.wait()
-        out = jnp.dot(hidden[...], wd_ref[...], preferred_element_type=F32)
+        out = jnp.dot(hidden[...], wd_ref[:, cols], preferred_element_type=F32)
         out += jnp.dot(low, pt_ref[:, cols], preferred_element_type=F32)
         own_out[:, cols] = out[:count]
         near_out[:, cols] = out[count : 2 * count].astype(BF16)
@@ -218,10 +210,7 @@
     vel_ref[...] = vel
     state_ref[...] = state
     normed = modulated(state, mod_row(mod_ref, 0, step + 1), mod_row(mod_ref, 1, step + 1))
-    half = far_ref.shape[1]
-    out_ref[...] = normed
-    far_ref[...] = normed[:, :half]
-    rest_ref[...] = normed[:, half:]
+    spread_out(normed, out_ref, far_ref, rest_ref)
 
 
 def last_body(steps_ref, mod_ref, vel_ref, state_ref, *refs):
@@ -251,17 +240,14 @@
 
 
 def reduce(own, near, over, far, rest_2, rest_3):
-    count, half = far.shape
-    relayed = call(relay_body, shape((count, half)), [VMEM] * 2, VMEM, "relay")(
-        far, swap(over, "tp", 1)
-    )
-    return (
-        own,
-        swap(near, "tp", 1),
-        swap(relayed, "tp", 2),
-        swap(rest_2, "tp", 2),
-        swap(rest_3, "tp", 3),
-    )
+    rest_2 = swap(rest_2, "tp", 2)
+    rest_3 = swap(rest_3, "tp", 3)
+    over = swap(over, "tp", 1)
+    over, rest_2 = lax.optimization_barrier((over, rest_2))
+    relayed = call(relay_body, shape(far.shape), [VMEM] * 2, VMEM, "relay")(far, over)
+    relayed = swap(relayed, "tp", 2)
+    near = swap(near, "tp", 1)
+    return own, near, relayed, rest_2, rest_3
 
 
 def pinned(x, space):
@@ -282,17 +268,19 @@
     spread_shapes = (shape((count, width)), shape((count, half)), shape((count, half)))
 
     sources = (up_a.T, down_b, up_b, down_a.T, step_index, latents, mods)
-    p_own, q_own, normed = call(
+    p_own, q_own, normed, far, rest = call(
         functools.partial(prepare_body, dp, rank),
         (
             shape((height, extra)),
             shape((height, hidden)),
-            shape((count, width)),
-        ),
+        )
+        + spread_shapes,
         [HBM] * 7,
-        (VMEM,) * 3,
+        (VMEM,) * 5,
         "prepare",
-        [(pltpu.SMEM if a is step_index else pltpu.VMEM)(a.shape, a.dtype) for a in sources]
+        flops=16 * rows * width * hidden,
+
+        scratch=[(pltpu.SMEM if a is step_index else pltpu.VMEM)(a.shape, a.dtype) for a in sources]
         + [pltpu.SemaphoreType.DMA((7,))],
     )(*[pinned(a, pltpu.HBM) for a in sources])
 
@@ -307,13 +295,15 @@
             bytes_accessed=base_up.size * 2,
         )(pinned(base_up, pltpu.HBM))
 
+    far = swap(far, "tp", 2)
     p_line = jnp.concatenate([p_own] + [swap(p_own, "tp", k) for k in (1, 2, 3)], axis=1)
-    up_0, up_1 = fetch(0, "fetch_up_0"), fetch(hidden // 2, "fetch_up_1")
-    p_line, up_0, up_1 = lax.optimization_barrier((p_line, up_0, up_1))
+    p_line, q_own = lax.optimization_barrier((p_line, q_own))
     p_far = swap(p_line, "dp", 2)
     q_far = swap(q_own, "dp", 2)
-    tokens = [normed] + [swap(normed, "tp", k) for k in TOKEN_ORDER]
-    p_far, q_far, tokens = lax.optimization_barrier((p_far, q_far, tokens))
+    got = spread(normed, rest, far)
+    keys = ("near", "rest_2", "rest_3", "over")
+    p_far, q_far, held = lax.optimization_barrier((p_far, q_far, [got[k] for k in keys]))
+    got.update(zip(keys, held))
     near = [swap(a, "dp", 1) for a in (p_line, q_own, p_far, q_far)]
     factors = call(
         functools.partial(assemble_body, tp, dp),
@@ -327,13 +317,11 @@
         (VMEM,) * 4,
         "assemble_factors",
     )(p_line, near[0], p_far, near[2], q_own, near[1], q_far, near[3])
-    resident = [pinned(a, pltpu.VMEM) for a in (*factors, up_0, up_1)]
-
-    def block(parts, downs):
-        streamed = downs is None
-        given = [pinned(base_down, pltpu.HBM)] if streamed else [pinned(a, pltpu.VMEM) for a in downs]
+    resident = [pinned(a, pltpu.VMEM) for a in (*factors, base_up, base_down)]
+
+    def block(parts):
         return call(
-            functools.partial(block_body, streamed, rank),
+            functools.partial(block_body, rank),
             (
                 shape((count, width), F32),
                 shape((count, width)),
@@ -341,19 +329,16 @@
                 shape((count, half), F32),
                 shape((count, half)),
                 shape((count, half)),
-            )
-            + (pltpu.VMEM((hidden, half), BF16),) * (2 * streamed),
-            [VMEM] * (len(parts) + 6) + [HBM if streamed else VMEM] * len(given),
-            (VMEM,) * (6 + 2 * streamed),
+            ),
+            [VMEM] * 12,
+            (VMEM,) * 6,
             "block",
-            [pltpu.VMEM((rows, width), BF16), pltpu.VMEM((rows, hidden), BF16)]
-            + [pltpu.SemaphoreType.DMA((2, STREAMS))] * streamed,
+            [pltpu.VMEM((rows, width), BF16), pltpu.VMEM((rows, hidden), BF16)],
             flops=4 * rows * width * hidden,
             bytes_accessed=4 * width * hidden,
-        )(*parts, *resident, *given)
-
-    tokens = [tokens[0]] + [tokens[1 + TOKEN_ORDER.index(k)] for k in (1, 2, 3)]
-    *sums, down_0, down_1 = block(tokens, None)
+        )(*parts, *resident)
+
+    sums = block(gather(normed, got, far))
     vel, state, normed, far, rest = call(
         middle_body,
         (shape((count, width), F32), shape((count, width), F32)) + spread_shapes,
@@ -362,7 +347,7 @@
         "first_update",
     )(step_index, latents, mods, *reduce(*sums))
     far = swap(far, "tp", 2)
-    sums = block(gather(normed, spread(normed, rest, far), far), (down_0, down_1))
+    sums = block(gather(normed, spread(normed, rest, far), far))
     return call(
         last_body,
         (shape((2, count, width), F32), shape((count, width), F32)),

time: 97.2 us -> 91.4 us (0.940)
  Pallas kernels: 26.5 us -> 18.2 us
  starting transfers between devices: 31.1 us -> 33.5 us
    pallas_call x6 -> x4, Pallas kernels: 21.8 us -> 13.3 us  [the longest x2 13.3 us: block(): call(functools.partial(block_body, rank), (shape((count, width), F32), sh...]
    ppermute x27 -> x29, starting transfers between devices: 31.1 us -> 33.5 us  [swap(): lax.ppermute(x, axis, [(i, i ^ flip) for i in range(lax.axis_size(axis))])]
    ppermute x27 -> x29, waiting for transfers between devices: 38.6 us -> 38.7 us  [swap(): lax.ppermute(x, axis, [(i, i ^ flip) for i in range(lax.axis_size(axis))])]
  transfers between devices with their start and end apart: 27 -> 29, of which waited for: 17 -> 18; matrix products, arithmetic and copies ran while one was open for 0% -> 0% of each run, Pallas kernels for 8% -> 0%
where the time goes in v4:
time: 91.4 us; the launch traced here: 91.2 us
  waiting for transfers between devices  38.7 us (42%)
  starting transfers between devices  33.5 us (37%)
  Pallas kernels  18.2 us (20%)
    ppermute x29, waiting for transfers between devices, swap(): lax.ppermute(x, axis, [(i, i ^ flip) for i in range(lax.axis_size(axis))])  38.7 us
    ppermute x29, starting transfers between devices, swap(): lax.ppermute(x, axis, [(i, i ^ flip) for i in range(lax.axis_size(axis))])  33.5 us
    pallas_call x2, Pallas kernels, block(): call(functools.partial(block_body, rank), (shape((count, width), F32), sh...  13.3 us
  transfers between devices with their start and end apart: 29, of which 18 were waited for; matrix products, arithmetic and copies ran while one was open for 0% of the time, Pallas kernels for 0%

profile of v4, /device:TPU:0, one launch (start us, length us, event | category | flops | bytes accessed | tf_op | source)
XLA Modules:
  0.0 91.2 jit_solution(6560133034618855996)
XLA Ops:
  0.7 1.6 %prepare.1 = (bf16[32,768]{1,0:T(8,128)(2,1)S(1)}, bf16[32,3072]{1,0:T(8,128)(2,1)S(1)}, bf16[32,3072]{1,0:T(8,128)(2,1)S(1)}, bf16[32,1536]{1,0:T(8,128)(2,1)S(1)}, bf16[32,1536]{1,0:T(8,128)(2,1)S(1)}) custom-call(bf16[64,192]{1,0:T(8,128)(2,1)} %bitcast.7, bf16[64,192]{1,0:T(8,128)(2,1)} %refs_1_.1, bf16[16,3072]{1,0:T(8,128)(2,1)} %refs_2_.1, ...), custom_call_target="tpu_custom_call" | custom-call | flops 19327352832 | tf_op jit(solution)/shard_map/prepare/pallas_call | solution.py:271
  2.3 5.1 %collective-permute-start.2 = (bf16[32,768]{1,0:T(8,128)(2,1)S(1)}, bf16[32,768]{1,0:T(8,128)(2,1)S(1)}, u32[]{:S(2)}, u32[]{:S(2)}) collective-permute-start(bf16[32,768]{1,0:T(8,128)(2,1)S(1)} %get-tuple-element.41), channel_id=1, source_target_pairs={{0,3},{1,2},{2,1},{3,0},{4,7},{5,6},{6,5},{7,4},{8,11},{9,10},{10,... | collective-permute-start | bytes 147464 | tf_op jit(solution)/shard_map/ppermute | solution.py:226
  7.4 0.6 collective-permute-start
  8.1 2.3 %collective-permute-start.8 = (bf16[32,1536]{1,0:T(8,128)(2,1)S(1)}, bf16[32,1536]{1,0:T(8,128)(2,1)S(1)}, u32[]{:S(2)}, u32[]{:S(2)}) collective-permute-start(bf16[32,1536]{1,0:T(8,128)(2,1)S(1)} %get-tuple-element.46), channel_id=1, source_target_pairs={{0,2},{1,3},{2,0},{3,1},{4,6},{5,7},{6,4},{7,5},{8,10},{9,11},{10,... | collective-permute-start | bytes 294920 | tf_op jit(solution)/shard_map/ppermute | solution.py:226
  10.3 1.5 %collective-permute-start.7 = (bf16[32,1536]{1,0:T(8,128)(2,1)S(1)}, bf16[32,1536]{1,0:T(8,128)(2,1)S(1)}, u32[]{:S(2)}, u32[]{:S(2)}) collective-permute-start(bf16[32,1536]{1,0:T(8,128)(2,1)S(1)} %get-tuple-element.45), channel_id=1, source_target_pairs={{0,3},{1,2},{2,1},{3,0},{4,7},{5,6},{6,5},{7,4},{8,11},{9,10},{10,... | collective-permute-start | bytes 294920 | tf_op jit(solution)/shard_map/ppermute | solution.py:226
  11.8 0.6 collective-permute-start.5
  12.4 3.7 %collective-permute-done.1 = bf16[32,768]{1,0:T(8,128)(2,1)S(1)} collective-permute-done((bf16[32,768]{1,0:T(8,128)(2,1)S(1)}, bf16[32,768]{1,0:T(8,128)(2,1)S(1)}, u32[]{:S(2)}, u32[]{:S(2)}) %collective-permute-start.1) | collective-permute-done | bytes 49184 | tf_op jit(solution)/shard_map/ppermute | solution.py:226
  16.1 1.6 %collective-permute-start.3 = (bf16[32,3072]{1,0:T(8,128)(2,1)S(1)}, bf16[32,3072]{1,0:T(8,128)(2,1)S(1)}, u32[]{:S(2)}, u32[]{:S(2)}) collective-permute-start(bf16[32,3072]{1,0:T(8,128)(2,1)S(1)} %pad_maximum_fusion.refs_0_), channel_id=1, source_target_pairs={{0,8},{4,12},{8,0},{12,4},{1,9},{5,13},{9,1},{13,5},{2,10},{6,14},... | collective-permute-start | bytes 589832 | tf_op jit(solution)/shard_map/ppermute | solution.py:226
  17.7 0.5 collective-permute-start.4
  18.2 1.1 %collective-permute-done.8.refs_2_ = bf16[32,1536]{1,0:T(8,128)(2,1)S(1)} collective-permute-done((bf16[32,1536]{1,0:T(8,128)(2,1)S(1)}, bf16[32,1536]{1,0:T(8,128)(2,1)S(1)}, u32[]{:S(2)}, u32[]{:S(2)}) %collective-permute-start.8) | collective-permute-done | bytes 98336 | tf_op jit(solution)/shard_map/ppermute | solution.py:226
  19.3 2.5 %collective-permute-start.9 = (bf16[32,1536]{1,0:T(8,128)(2,1)S(1)}, bf16[32,1536]{1,0:T(8,128)(2,1)S(1)}, u32[]{:S(2)}, u32[]{:S(2)}) collective-permute-start(bf16[32,1536]{1,0:T(8,128)(2,1)S(1)} %collective-permute-done.8.refs_2_), channel_id=1, source_target_pairs={{0,1},{1,0},{2,3},{3,2},{4,5},{5,4},{6,7},{7,6},{8,9},{9,8},{10,11... | collective-permute-start | bytes 294920 | tf_op jit(solution)/shard_map/ppermute | solution.py:226
  21.8 3.2 %collective-permute-done.6.refs_4_ = bf16[32,1536]{1,0:T(8,128)(2,1)S(1)} collective-permute-done((bf16[32,1536]{1,0:T(8,128)(2,1)S(1)}, bf16[32,1536]{1,0:T(8,128)(2,1)S(1)}, u32[]{:S(2)}, u32[]{:S(2)}) %collective-permute-start.6) | collective-permute-done | bytes 98336 | tf_op jit(solution)/shard_map/ppermute | solution.py:226
  25.0 0.6 collective-permute-done.9.refs_3_
  25.6 0.6 collective-permute-start.11
  26.1 0.1 collective-permute-start.13
  26.2 0.2 collective-permute-done.10.refs_1_
  26.4 0.6 collective-permute-done.12.refs_5_
  27.0 0.3 collective-permute-done.11.refs_3_
  27.3 0.3 collective-permute-done.13.refs_7_
  27.6 0.6 assemble_factors.1
  28.2 0.0 copy-start.3
  28.3 6.5 %block.2 = (f32[32,3072]{1,0:T(8,128)S(1)}, bf16[32,3072]{1,0:T(8,128)(2,1)S(1)}, bf16[32,1536]{1,0:T(8,128)(2,1)S(1)}, f32[32,1536]{1,0:T(8,128)S(1)}, bf16[32,...) custom-call(bf16[32,3072]{1,0:T(8,128)(2,1)S(1)} %get-tuple-element.40.refs_0_, ...), custom_call_target="tpu_custom_call" | custom-call | flops 4831838208 | bytes 37748736 | tf_op jit(solution)/shard_map/block/pallas_call | solution.py:323
  34.8 0.9 %collective-permute-start.15 = (bf16[32,1536]{1,0:T(8,128)(2,1)S(1)}, bf16[32,1536]{1,0:T(8,128)(2,1)S(1)}, u32[]{:S(2)}, u32[]{:S(2)}) collective-permute-start(bf16[32,1536]{1,0:T(8,128)(2,1)S(1)} %get-tuple-element.60), channel_id=1, source_target_pairs={{0,1},{1,0},{2,3},{3,2},{4,5},{5,4},{6,7},{7,6},{8,9},{9,8},{10,11... | collective-permute-start | bytes 294920 | tf_op jit(solution)/shard_map/ppermute | solution.py:226
  35.7 2.7 %collective-permute-start.16 = (bf16[32,1536]{1,0:T(8,128)(2,1)S(1)}, bf16[32,1536]{1,0:T(8,128)(2,1)S(1)}, u32[]{:S(2)}, u32[]{:S(2)}) collective-permute-start(bf16[32,1536]{1,0:T(8,128)(2,1)S(1)} %get-tuple-element.61), channel_id=1, source_target_pairs={{0,2},{1,3},{2,0},{3,1},{4,6},{5,7},{6,4},{7,5},{8,10},{9,11},{10,... | collective-permute-start | bytes 294920 | tf_op jit(solution)/shard_map/ppermute | solution.py:226
  38.4 0.3 collective-permute-start.14
  38.7 1.4 %collective-permute-start.18 = (bf16[32,1536]{1,0:T(8,128)(2,1)S(1)}, bf16[32,1536]{1,0:T(8,128)(2,1)S(1)}, u32[]{:S(2)}, u32[]{:S(2)}) collective-permute-start(bf16[32,1536]{1,0:T(8,128)(2,1)S(1)} %get-tuple-element.64), channel_id=1, source_target_pairs={{0,3},{1,2},{2,1},{3,0},{4,7},{5,6},{6,5},{7,4},{8,11},{9,10},{10,... | collective-permute-start | bytes 294920 | tf_op jit(solution)/shard_map/ppermute | solution.py:226
  40.1 2.0 %collective-permute-done.15.got_ref = bf16[32,1536]{1,0:T(8,128)(2,1)S(1)} collective-permute-done((bf16[32,1536]{1,0:T(8,128)(2,1)S(1)}, bf16[32,1536]{1,0:T(8,128)(2,1)S(1)}, u32[]{:S(2)}, u32[]{:S(2)}) %collective-permute-start.15) | collective-permute-done | bytes 98336 | tf_op jit(solution)/shard_map/ppermute | solution.py:226
  42.0 1.5 %collective-permute-done.16.refs_3_ = bf16[32,1536]{1,0:T(8,128)(2,1)S(1)} collective-permute-done((bf16[32,1536]{1,0:T(8,128)(2,1)S(1)}, bf16[32,1536]{1,0:T(8,128)(2,1)S(1)}, u32[]{:S(2)}, u32[]{:S(2)}) %collective-permute-start.16) | collective-permute-done | bytes 98336 | tf_op jit(solution)/shard_map/ppermute | solution.py:226
  43.5 1.5 %collective-permute-start.17 = (bf16[32,1536]{1,0:T(8,128)(2,1)S(1)}, bf16[32,1536]{1,0:T(8,128)(2,1)S(1)}, u32[]{:S(2)}, u32[]{:S(2)}) collective-permute-start(bf16[32,1536]{1,0:T(8,128)(2,1)S(1)} %relay.2), channel_id=1, source_target_pairs={{0,2},{1,3},{2,0},{3,1},{4,6},{5,7},{6,4},{7,5},{8,10},{9,11},{10,... | collective-permute-start | bytes 294920 | tf_op jit(solution)/shard_map/ppermute | solution.py:226
  45.1 5.1 %collective-permute-done.18.refs_4_ = bf16[32,1536]{1,0:T(8,128)(2,1)S(1)} collective-permute-done((bf16[32,1536]{1,0:T(8,128)(2,1)S(1)}, bf16[32,1536]{1,0:T(8,128)(2,1)S(1)}, u32[]{:S(2)}, u32[]{:S(2)}) %collective-permute-start.18) | collective-permute-done | bytes 98336 | tf_op jit(solution)/shard_map/ppermute | solution.py:226
  50.2 2.4 %collective-permute-done.17.refs_2_ = bf16[32,1536]{1,0:T(8,128)(2,1)S(1)} collective-permute-done((bf16[32,1536]{1,0:T(8,128)(2,1)S(1)}, bf16[32,1536]{1,0:T(8,128)(2,1)S(1)}, u32[]{:S(2)}, u32[]{:S(2)}) %collective-permute-start.17) | collective-permute-done | bytes 98336 | tf_op jit(solution)/shard_map/ppermute | solution.py:226
  52.7 0.9 %first_update.1 = (f32[32,3072]{1,0:T(8,128)S(1)}, f32[32,3072]{1,0:T(8,128)S(1)}, bf16[32,3072]{1,0:T(8,128)(2,1)S(1)}, bf16[32,1536]{1,0:T(8,128)(2,1)S(1)}, bf16[32,1536]{1,0:T(8,128)(2,1)S(1)}) custom-call(s32[2]{0:T(128)S(1)} %copy-done.4, bf16[32,3072]{1,0:T(8,128)(2,1)S(1)} %copy-done.3, f32[3,4,3072]{2,1,0:T(4,128)S(1)} %bitcast.4, ...), custom_call_target="tpu_custom_call" | custom-call | tf_op jit(solution)/shard_map/first_update/pallas_call | solution.py:342
  53.6 0.1 collective-permute-start.20
  53.7 2.3 %collective-permute-start.19 = (bf16[32,3072]{1,0:T(8,128)(2,1)S(1)}, bf16[32,3072]{1,0:T(8,128)(2,1)S(1)}, u32[]{:S(2)}, u32[]{:S(2)}) collective-permute-start(bf16[32,3072]{1,0:T(8,128)(2,1)S(1)} %get-tuple-element.67.refs_0_), channel_id=1, source_target_pairs={{0,1},{1,0},{2,3},{3,2},{4,5},{5,4},{6,7},{7,6},{8,9},{9,8},{10,11... | collective-permute-start | bytes 589832 | tf_op jit(solution)/shard_map/ppermute | solution.py:226
  56.0 2.1 %collective-permute-start.23 = (bf16[32,1536]{1,0:T(8,128)(2,1)S(1)}, bf16[32,1536]{1,0:T(8,128)(2,1)S(1)}, u32[]{:S(2)}, u32[]{:S(2)}) collective-permute-start(bf16[32,1536]{1,0:T(8,128)(2,1)S(1)} %get-tuple-element.69), channel_id=1, source_target_pairs={{0,3},{1,2},{2,1},{3,0},{4,7},{5,6},{6,5},{7,4},{8,11},{9,10},{10,... | collective-permute-start | bytes 294920 | tf_op jit(solution)/shard_map/ppermute | solution.py:226
  58.1 3.8 %collective-permute-done.20.refs_2_ = bf16[32,1536]{1,0:T(8,128)(2,1)S(1)} collective-permute-done((bf16[32,1536]{1,0:T(8,128)(2,1)S(1)}, bf16[32,1536]{1,0:T(8,128)(2,1)S(1)}, u32[]{:S(2)}, u32[]{:S(2)}) %collective-permute-start.20) | collective-permute-done | bytes 98336 | tf_op jit(solution)/shard_map/ppermute | solution.py:226
  61.9 4.1 %collective-permute-done.23.refs_5_ = bf16[32,1536]{1,0:T(8,128)(2,1)S(1)} collective-permute-done((bf16[32,1536]{1,0:T(8,128)(2,1)S(1)}, bf16[32,1536]{1,0:T(8,128)(2,1)S(1)}, u32[]{:S(2)}, u32[]{:S(2)}) %collective-permute-start.23) | collective-permute-done | bytes 98336 | tf_op jit(solution)/shard_map/ppermute | solution.py:226
  66.0 1.2 %collective-permute-done.22.refs_4_ = bf16[32,1536]{1,0:T(8,128)(2,1)S(1)} collective-permute-done((bf16[32,1536]{1,0:T(8,128)(2,1)S(1)}, bf16[32,1536]{1,0:T(8,128)(2,1)S(1)}, u32[]{:S(2)}, u32[]{:S(2)}) %collective-permute-start.22) | collective-permute-done | bytes 98336 | tf_op jit(solution)/shard_map/ppermute | solution.py:226
  67.3 6.8 %block.3 = (f32[32,3072]{1,0:T(8,128)S(1)}, bf16[32,3072]{1,0:T(8,128)(2,1)S(1)}, bf16[32,1536]{1,0:T(8,128)(2,1)S(1)}, f32[32,1536]{1,0:T(8,128)S(1)}, bf16[32,...) custom-call(bf16[32,3072]{1,0:T(8,128)(2,1)S(1)} %get-tuple-element.67.refs_0_, ...), custom_call_target="tpu_custom_call" | custom-call | flops 4831838208 | bytes 37748736 | tf_op jit(solution)/shard_map/block/pallas_call | solution.py:323
  74.0 0.6 collective-permute-start.25
  74.7 2.3 %collective-permute-start.26 = (bf16[32,1536]{1,0:T(8,128)(2,1)S(1)}, bf16[32,1536]{1,0:T(8,128)(2,1)S(1)}, u32[]{:S(2)}, u32[]{:S(2)}) collective-permute-start(bf16[32,1536]{1,0:T(8,128)(2,1)S(1)} %get-tuple-element.74), channel_id=1, source_target_pairs={{0,2},{1,3},{2,0},{3,1},{4,6},{5,7},{6,4},{7,5},{8,10},{9,11},{10,... | collective-permute-start | bytes 294920 | tf_op jit(solution)/shard_map/ppermute | solution.py:226
  77.0 0.7 collective-permute-start.24
  77.7 1.4 %collective-permute-start.28 = (bf16[32,1536]{1,0:T(8,128)(2,1)S(1)}, bf16[32,1536]{1,0:T(8,128)(2,1)S(1)}, u32[]{:S(2)}, u32[]{:S(2)}) collective-permute-start(bf16[32,1536]{1,0:T(8,128)(2,1)S(1)} %get-tuple-element.77), channel_id=1, source_target_pairs={{0,3},{1,2},{2,1},{3,0},{4,7},{5,6},{6,5},{7,4},{8,11},{9,10},{10,... | collective-permute-start | bytes 294920 | tf_op jit(solution)/shard_map/ppermute | solution.py:226
  79.1 2.8 %collective-permute-done.25.got_ref = bf16[32,1536]{1,0:T(8,128)(2,1)S(1)} collective-permute-done((bf16[32,1536]{1,0:T(8,128)(2,1)S(1)}, bf16[32,1536]{1,0:T(8,128)(2,1)S(1)}, u32[]{:S(2)}, u32[]{:S(2)}) %collective-permute-start.25) | collective-permute-done | bytes 98336 | tf_op jit(solution)/shard_map/ppermute | solution.py:226
  81.9 1.9 %collective-permute-start.27 = (bf16[32,1536]{1,0:T(8,128)(2,1)S(1)}, bf16[32,1536]{1,0:T(8,128)(2,1)S(1)}, u32[]{:S(2)}, u32[]{:S(2)}) collective-permute-start(bf16[32,1536]{1,0:T(8,128)(2,1)S(1)} %relay.3), channel_id=1, source_target_pairs={{0,2},{1,3},{2,0},{3,1},{4,6},{5,7},{6,4},{7,5},{8,10},{9,11},{10,... | collective-permute-start | bytes 294920 | tf_op jit(solution)/shard_map/ppermute | solution.py:226
  83.8 3.9 %collective-permute-done.28.refs_4_ = bf16[32,1536]{1,0:T(8,128)(2,1)S(1)} collective-permute-done((bf16[32,1536]{1,0:T(8,128)(2,1)S(1)}, bf16[32,1536]{1,0:T(8,128)(2,1)S(1)}, u32[]{:S(2)}, u32[]{:S(2)}) %collective-permute-start.28) | collective-permute-done | bytes 98336 | tf_op jit(solution)/shard_map/ppermute | solution.py:226
  87.7 1.9 %collective-permute-done.27.refs_2_ = bf16[32,1536]{1,0:T(8,128)(2,1)S(1)} collective-permute-done((bf16[32,1536]{1,0:T(8,128)(2,1)S(1)}, bf16[32,1536]{1,0:T(8,128)(2,1)S(1)}, u32[]{:S(2)}, u32[]{:S(2)}) %collective-permute-start.27) | collective-permute-done | bytes 98336 | tf_op jit(solution)/shard_map/ppermute | solution.py:226
  89.6 1.7 %second_update.1 = (f32[2,32,3072]{2,1,0:T(8,128)}, f32[32,3072]{1,0:T(8,128)}) custom-call(s32[2]{0:T(128)S(1)} %copy-done.4, f32[3,4,3072]{2,1,0:T(4,128)S(1)} %bitcast.5, f32[32,3072]{1,0:T(8,128)S(1)} %get-tuple-element.65.vel_ref, f32[32,3072]{1,0:T(8,128)S(1)} %get-tuple-element.66.state_ref, f32[32,3072]{1,0:T(8,128)S(1)} %get-tuple-element.70.refs_0_, ...), custom_call_target="tpu_custom_call" | custom-call | tf_op jit(solution)/shard_map/second_update/pallas_call | solution.py:351
  (29 shorter events, 0.1 us)
Async XLA Ops:
  0.6 27.6 %copy-start = (bf16[3072,3072]{1,0:T(8,128)(2,1)S(1)}, bf16[3072,3072]{1,0:T(8,128)(2,1)}, u32[]{:S(2)}) copy-start(bf16[3072,3072]{1,0:T(8,128)(2,1)} %refs_10_.3) | copy-start | bytes 56623108
  0.6 27.6 %copy-start.1 = (bf16[3072,3072]{1,0:T(8,128)(2,1)S(1)}, bf16[3072,3072]{1,0:T(8,128)(2,1)}, u32[]{:S(2)}) copy-start(bf16[3072,3072]{1,0:T(8,128)(2,1)} %refs_11_.3) | copy-start | bytes 56623108
  2.3 9.5 %collective-permute-start.2 = (bf16[32,768]{1,0:T(8,128)(2,1)S(1)}, bf16[32,768]{1,0:T(8,128)(2,1)S(1)}, u32[]{:S(2)}, u32[]{:S(2)}) collective-permute-start(bf16[32,768]{1,0:T(8,128)(2,1)S(1)} %get-tuple-element.41), channel_id=1, source_target_pairs={{0,3},{1,2},{2,1},{3,0},{4,7},{5,6},{6,5},{7,4},{8,11},{9,10},{10,... | collective-permute-start | bytes 147464 | tf_op jit(solution)/shard_map/ppermute | solution.py:226
  7.4 8.7 %collective-permute-start.1 = (bf16[32,768]{1,0:T(8,128)(2,1)S(1)}, bf16[32,768]{1,0:T(8,128)(2,1)S(1)}, u32[]{:S(2)}, u32[]{:S(2)}) collective-permute-start(bf16[32,768]{1,0:T(8,128)(2,1)S(1)} %get-tuple-element.41), channel_id=1, source_target_pairs={{0,2},{1,3},{2,0},{3,1},{4,6},{5,7},{6,4},{7,5},{8,10},{9,11},{10,... | collective-permute-start | bytes 147464 | tf_op jit(solution)/shard_map/ppermute | solution.py:226
  7.4 8.7 %collective-permute-start = (bf16[32,768]{1,0:T(8,128)(2,1)S(1)}, bf16[32,768]{1,0:T(8,128)(2,1)S(1)}, u32[]{:S(2)}, u32[]{:S(2)}) collective-permute-start(bf16[32,768]{1,0:T(8,128)(2,1)S(1)} %get-tuple-element.41), channel_id=1, source_target_pairs={{0,1},{1,0},{2,3},{3,2},{4,5},{5,4},{6,7},{7,6},{8,9},{9,8},{10,11... | collective-permute-start | bytes 147464 | tf_op jit(solution)/shard_map/ppermute | solution.py:226
  8.1 11.2 %collective-permute-start.8 = (bf16[32,1536]{1,0:T(8,128)(2,1)S(1)}, bf16[32,1536]{1,0:T(8,128)(2,1)S(1)}, u32[]{:S(2)}, u32[]{:S(2)}) collective-permute-start(bf16[32,1536]{1,0:T(8,128)(2,1)S(1)} %get-tuple-element.46), channel_id=1, source_target_pairs={{0,2},{1,3},{2,0},{3,1},{4,6},{5,7},{6,4},{7,5},{8,10},{9,11},{10,... | collective-permute-start | bytes 294920 | tf_op jit(solution)/shard_map/ppermute | solution.py:226
  10.3 9.0 %collective-permute-start.7 = (bf16[32,1536]{1,0:T(8,128)(2,1)S(1)}, bf16[32,1536]{1,0:T(8,128)(2,1)S(1)}, u32[]{:S(2)}, u32[]{:S(2)}) collective-permute-start(bf16[32,1536]{1,0:T(8,128)(2,1)S(1)} %get-tuple-element.45), channel_id=1, source_target_pairs={{0,3},{1,2},{2,1},{3,0},{4,7},{5,6},{6,5},{7,4},{8,11},{9,10},{10,... | collective-permute-start | bytes 294920 | tf_op jit(solution)/shard_map/ppermute | solution.py:226
  11.8 13.7 %collective-permute-start.5 = (bf16[32,3072]{1,0:T(8,128)(2,1)S(1)}, bf16[32,3072]{1,0:T(8,128)(2,1)S(1)}, u32[]{:S(2)}, u32[]{:S(2)}) collective-permute-start(bf16[32,3072]{1,0:T(8,128)(2,1)S(1)} %get-tuple-element.40.refs_0_), channel_id=1, source_target_pairs={{0,1},{1,0},{2,3},{3,2},{4,5},{5,4},{6,7},{7,6},{8,9},{9,8},{10,11... | collective-permute-start | bytes 589832 | tf_op jit(solution)/shard_map/ppermute | solution.py:226
  16.1 9.4 %collective-permute-start.3 = (bf16[32,3072]{1,0:T(8,128)(2,1)S(1)}, bf16[32,3072]{1,0:T(8,128)(2,1)S(1)}, u32[]{:S(2)}, u32[]{:S(2)}) collective-permute-start(bf16[32,3072]{1,0:T(8,128)(2,1)S(1)} %pad_maximum_fusion.refs_0_), channel_id=1, source_target_pairs={{0,8},{4,12},{8,0},{12,4},{1,9},{5,13},{9,1},{13,5},{2,10},{6,14},... | collective-permute-start | bytes 589832 | tf_op jit(solution)/shard_map/ppermute | solution.py:226
  17.7 7.9 %collective-permute-start.4 = (bf16[32,3072]{1,0:T(8,128)(2,1)S(1)}, bf16[32,3072]{1,0:T(8,128)(2,1)S(1)}, u32[]{:S(2)}, u32[]{:S(2)}) collective-permute-start(bf16[32,3072]{1,0:T(8,128)(2,1)S(1)} %get-tuple-element.44.refs_4_), channel_id=1, source_target_pairs={{0,8},{4,12},{8,0},{12,4},{1,9},{5,13},{9,1},{13,5},{2,10},{6,14},... | collective-permute-start | bytes 589832 | tf_op jit(solution)/shard_map/ppermute | solution.py:226
  19.3 5.7 %collective-permute-start.6 = (bf16[32,1536]{1,0:T(8,128)(2,1)S(1)}, bf16[32,1536]{1,0:T(8,128)(2,1)S(1)}, u32[]{:S(2)}, u32[]{:S(2)}) collective-permute-start(bf16[32,1536]{1,0:T(8,128)(2,1)S(1)} %get-tuple-element.45), channel_id=1, source_target_pairs={{0,2},{1,3},{2,0},{3,1},{4,6},{5,7},{6,4},{7,5},{8,10},{9,11},{10,... | collective-permute-start | bytes 294920 | tf_op jit(solution)/shard_map/ppermute | solution.py:226
  19.3 6.2 %collective-permute-start.9 = (bf16[32,1536]{1,0:T(8,128)(2,1)S(1)}, bf16[32,1536]{1,0:T(8,128)(2,1)S(1)}, u32[]{:S(2)}, u32[]{:S(2)}) collective-permute-start(bf16[32,1536]{1,0:T(8,128)(2,1)S(1)} %collective-permute-done.8.refs_2_), channel_id=1, source_target_pairs={{0,1},{1,0},{2,3},{3,2},{4,5},{5,4},{6,7},{7,6},{8,9},{9,8},{10,11... | collective-permute-start | bytes 294920 | tf_op jit(solution)/shard_map/ppermute | solution.py:226
  25.0 1.4 %collective-permute-start.10 = (bf16[32,3072]{1,0:T(8,128)(2,1)S(1)}, bf16[32,3072]{1,0:T(8,128)(2,1)S(1)}, u32[]{:S(2)}, u32[]{:S(2)}) collective-permute-start(bf16[32,3072]{1,0:T(8,128)(2,1)S(1)} %pad_maximum_fusion.refs_0_), channel_id=1, source_target_pairs={{0,4},{4,0},{8,12},{12,8},{1,5},{5,1},{9,13},{13,9},{2,6},{6,2},{1... | collective-permute-start | bytes 589832 | tf_op jit(solution)/shard_map/ppermute | solution.py:226
  25.5 1.4 %collective-permute-start.12 = (bf16[32,3072]{1,0:T(8,128)(2,1)S(1)}, bf16[32,3072]{1,0:T(8,128)(2,1)S(1)}, u32[]{:S(2)}, u32[]{:S(2)}) collective-permute-start(bf16[32,3072]{1,0:T(8,128)(2,1)S(1)} %get-tuple-element.44.refs_4_), channel_id=1, source_target_pairs={{0,4},{4,0},{8,12},{12,8},{1,5},{5,1},{9,13},{13,9},{2,6},{6,2},{1... | collective-permute-start | bytes 589832 | tf_op jit(solution)/shard_map/ppermute | solution.py:226
  25.6 1.7 %collective-permute-start.11 = (bf16[32,3072]{1,0:T(8,128)(2,1)S(1)}, bf16[32,3072]{1,0:T(8,128)(2,1)S(1)}, u32[]{:S(2)}, u32[]{:S(2)}) collective-permute-start(bf16[32,3072]{1,0:T(8,128)(2,1)S(1)} %collective-permute-done.3.refs_2_), channel_id=1, source_target_pairs={{0,4},{4,0},{8,12},{12,8},{1,5},{5,1},{9,13},{13,9},{2,6},{6,2},{1... | collective-permute-start | bytes 589832 | tf_op jit(solution)/shard_map/ppermute | solution.py:226
  26.1 1.4 %collective-permute-start.13 = (bf16[32,3072]{1,0:T(8,128)(2,1)S(1)}, bf16[32,3072]{1,0:T(8,128)(2,1)S(1)}, u32[]{:S(2)}, u32[]{:S(2)}) collective-permute-start(bf16[32,3072]{1,0:T(8,128)(2,1)S(1)} %collective-permute-done.4.refs_6_), channel_id=1, source_target_pairs={{0,4},{4,0},{8,12},{12,8},{1,5},{5,1},{9,13},{13,9},{2,6},{6,2},{1... | collective-permute-start | bytes 589832 | tf_op jit(solution)/shard_map/ppermute | solution.py:226
  28.2 24.4 %copy-start.2 = (f32[4,3,3072]{2,0,1:T(4,128)S(1)}, f32[4,3,3072]{2,0,1:T(4,128)}, u32[]{:S(2)}) copy-start(f32[4,3,3072]{2,0,1:T(4,128)} %param.11) | copy-start | bytes 442372
  28.2 24.4 %copy-start.3 = (bf16[32,3072]{1,0:T(8,128)(2,1)S(1)}, bf16[32,3072]{1,0:T(8,128)(2,1)}, u32[]{:S(2)}) copy-start(bf16[32,3072]{1,0:T(8,128)(2,1)} %lat_ref.1) | copy-start | bytes 589828
  28.2 24.4 %copy-start.4 = (s32[2]{0:T(128)S(1)}, s32[2]{0:T(128)}, u32[]{:S(2)}) copy-start(s32[2]{0:T(128)} %steps_ref.3) | copy-start | bytes 28
  34.8 7.3 %collective-permute-start.15 = (bf16[32,1536]{1,0:T(8,128)(2,1)S(1)}, bf16[32,1536]{1,0:T(8,128)(2,1)S(1)}, u32[]{:S(2)}, u32[]{:S(2)}) collective-permute-start(bf16[32,1536]{1,0:T(8,128)(2,1)S(1)} %get-tuple-element.60), channel_id=1, source_target_pairs={{0,1},{1,0},{2,3},{3,2},{4,5},{5,4},{6,7},{7,6},{8,9},{9,8},{10,11... | collective-permute-start | bytes 294920 | tf_op jit(solution)/shard_map/ppermute | solution.py:226
  35.7 7.8 %collective-permute-start.16 = (bf16[32,1536]{1,0:T(8,128)(2,1)S(1)}, bf16[32,1536]{1,0:T(8,128)(2,1)S(1)}, u32[]{:S(2)}, u32[]{:S(2)}) collective-permute-start(bf16[32,1536]{1,0:T(8,128)(2,1)S(1)} %get-tuple-element.61), channel_id=1, source_target_pairs={{0,2},{1,3},{2,0},{3,1},{4,6},{5,7},{6,4},{7,5},{8,10},{9,11},{10,... | collective-permute-start | bytes 294920 | tf_op jit(solution)/shard_map/ppermute | solution.py:226
  38.4 14.3 %collective-permute-start.14 = (bf16[32,3072]{1,0:T(8,128)(2,1)S(1)}, bf16[32,3072]{1,0:T(8,128)(2,1)S(1)}, u32[]{:S(2)}, u32[]{:S(2)}) collective-permute-start(bf16[32,3072]{1,0:T(8,128)(2,1)S(1)} %get-tuple-element.58), channel_id=1, source_target_pairs={{0,1},{1,0},{2,3},{3,2},{4,5},{5,4},{6,7},{7,6},{8,9},{9,8},{10,11... | collective-permute-start | bytes 589832 | tf_op jit(solution)/shard_map/ppermute | solution.py:226
  38.7 11.6 %collective-permute-start.18 = (bf16[32,1536]{1,0:T(8,128)(2,1)S(1)}, bf16[32,1536]{1,0:T(8,128)(2,1)S(1)}, u32[]{:S(2)}, u32[]{:S(2)}) collective-permute-start(bf16[32,1536]{1,0:T(8,128)(2,1)S(1)} %get-tuple-element.64), channel_id=1, source_target_pairs={{0,3},{1,2},{2,1},{3,0},{4,7},{5,6},{6,5},{7,4},{8,11},{9,10},{10,... | collective-permute-start | bytes 294920 | tf_op jit(solution)/shard_map/ppermute | solution.py:226
  43.5 9.1 %collective-permute-start.17 = (bf16[32,1536]{1,0:T(8,128)(2,1)S(1)}, bf16[32,1536]{1,0:T(8,128)(2,1)S(1)}, u32[]{:S(2)}, u32[]{:S(2)}) collective-permute-start(bf16[32,1536]{1,0:T(8,128)(2,1)S(1)} %relay.2), channel_id=1, source_target_pairs={{0,2},{1,3},{2,0},{3,1},{4,6},{5,7},{6,4},{7,5},{8,10},{9,11},{10,... | collective-permute-start | bytes 294920 | tf_op jit(solution)/shard_map/ppermute | solution.py:226
  53.6 8.3 %collective-permute-start.20 = (bf16[32,1536]{1,0:T(8,128)(2,1)S(1)}, bf16[32,1536]{1,0:T(8,128)(2,1)S(1)}, u32[]{:S(2)}, u32[]{:S(2)}) collective-permute-start(bf16[32,1536]{1,0:T(8,128)(2,1)S(1)} %get-tuple-element.68), channel_id=1, source_target_pairs={{0,2},{1,3},{2,0},{3,1},{4,6},{5,7},{6,4},{7,5},{8,10},{9,11},{10,... | collective-permute-start | bytes 294920 | tf_op jit(solution)/shard_map/ppermute | solution.py:226
  53.7 13.6 %collective-permute-start.19 = (bf16[32,3072]{1,0:T(8,128)(2,1)S(1)}, bf16[32,3072]{1,0:T(8,128)(2,1)S(1)}, u32[]{:S(2)}, u32[]{:S(2)}) collective-permute-start(bf16[32,3072]{1,0:T(8,128)(2,1)S(1)} %get-tuple-element.67.refs_0_), channel_id=1, source_target_pairs={{0,1},{1,0},{2,3},{3,2},{4,5},{5,4},{6,7},{7,6},{8,9},{9,8},{10,11... | collective-permute-start | bytes 589832 | tf_op jit(solution)/shard_map/ppermute | solution.py:226
  56.0 10.0 %collective-permute-start.23 = (bf16[32,1536]{1,0:T(8,128)(2,1)S(1)}, bf16[32,1536]{1,0:T(8,128)(2,1)S(1)}, u32[]{:S(2)}, u32[]{:S(2)}) collective-permute-start(bf16[32,1536]{1,0:T(8,128)(2,1)S(1)} %get-tuple-element.69), channel_id=1, source_target_pairs={{0,3},{1,2},{2,1},{3,0},{4,7},{5,6},{6,5},{7,4},{8,11},{9,10},{10,... | collective-permute-start | bytes 294920 | tf_op jit(solution)/shard_map/ppermute | solution.py:226
  58.0 9.2 %collective-permute-start.22 = (bf16[32,1536]{1,0:T(8,128)(2,1)S(1)}, bf16[32,1536]{1,0:T(8,128)(2,1)S(1)}, u32[]{:S(2)}, u32[]{:S(2)}) collective-permute-start(bf16[32,1536]{1,0:T(8,128)(2,1)S(1)} %get-tuple-element.69), channel_id=1, source_target_pairs={{0,2},{1,3},{2,0},{3,1},{4,6},{5,7},{6,4},{7,5},{8,10},{9,11},{10,... | collective-permute-start | bytes 294920 | tf_op jit(solution)/shard_map/ppermute | solution.py:226
  61.9 5.4 %collective-permute-start.21 = (bf16[32,1536]{1,0:T(8,128)(2,1)S(1)}, bf16[32,1536]{1,0:T(8,128)(2,1)S(1)}, u32[]{:S(2)}, u32[]{:S(2)}) collective-permute-start(bf16[32,1536]{1,0:T(8,128)(2,1)S(1)} %collective-permute-done.20.refs_2_), channel_id=1, source_target_pairs={{0,1},{1,0},{2,3},{3,2},{4,5},{5,4},{6,7},{7,6},{8,9},{9,8},{10,11... | collective-permute-start | bytes 294920 | tf_op jit(solution)/shard_map/ppermute | solution.py:226
  74.0 7.8 %collective-permute-start.25 = (bf16[32,1536]{1,0:T(8,128)(2,1)S(1)}, bf16[32,1536]{1,0:T(8,128)(2,1)S(1)}, u32[]{:S(2)}, u32[]{:S(2)}) collective-permute-start(bf16[32,1536]{1,0:T(8,128)(2,1)S(1)} %get-tuple-element.73), channel_id=1, source_target_pairs={{0,1},{1,0},{2,3},{3,2},{4,5},{5,4},{6,7},{7,6},{8,9},{9,8},{10,11... | collective-permute-start | bytes 294920 | tf_op jit(solution)/shard_map/ppermute | solution.py:226
  74.7 7.2 %collective-permute-start.26 = (bf16[32,1536]{1,0:T(8,128)(2,1)S(1)}, bf16[32,1536]{1,0:T(8,128)(2,1)S(1)}, u32[]{:S(2)}, u32[]{:S(2)}) collective-permute-start(bf16[32,1536]{1,0:T(8,128)(2,1)S(1)} %get-tuple-element.74), channel_id=1, source_target_pairs={{0,2},{1,3},{2,0},{3,1},{4,6},{5,7},{6,4},{7,5},{8,10},{9,11},{10,... | collective-permute-start | bytes 294920 | tf_op jit(solution)/shard_map/ppermute | solution.py:226
  77.0 10.7 %collective-permute-start.24 = (bf16[32,3072]{1,0:T(8,128)(2,1)S(1)}, bf16[32,3072]{1,0:T(8,128)(2,1)S(1)}, u32[]{:S(2)}, u32[]{:S(2)}) collective-permute-start(bf16[32,3072]{1,0:T(8,128)(2,1)S(1)} %get-tuple-element.71), channel_id=1, source_target_pairs={{0,1},{1,0},{2,3},{3,2},{4,5},{5,4},{6,7},{7,6},{8,9},{9,8},{10,11... | collective-permute-start | bytes 589832 | tf_op jit(solution)/shard_map/ppermute | solution.py:226
  77.7 9.9 %collective-permute-start.28 = (bf16[32,1536]{1,0:T(8,128)(2,1)S(1)}, bf16[32,1536]{1,0:T(8,128)(2,1)S(1)}, u32[]{:S(2)}, u32[]{:S(2)}) collective-permute-start(bf16[32,1536]{1,0:T(8,128)(2,1)S(1)} %get-tuple-element.77), channel_id=1, source_target_pairs={{0,3},{1,2},{2,1},{3,0},{4,7},{5,6},{6,5},{7,4},{8,11},{9,10},{10,... | collective-permute-start | bytes 294920 | tf_op jit(solution)/shard_map/ppermute | solution.py:226
  81.9 7.7 %collective-permute-start.27 = (bf16[32,1536]{1,0:T(8,128)(2,1)S(1)}, bf16[32,1536]{1,0:T(8,128)(2,1)S(1)}, u32[]{:S(2)}, u32[]{:S(2)}) collective-permute-start(bf16[32,1536]{1,0:T(8,128)(2,1)S(1)} %relay.3), channel_id=1, source_target_pairs={{0,2},{1,3},{2,0},{3,1},{4,6},{5,7},{6,4},{7,5},{8,10},{9,11},{10,... | collective-permute-start | bytes 294920 | tf_op jit(solution)/shard_map/ppermute | solution.py:226

commit v5 on v4

--- a/solution.py
+++ b/solution.py
@@ -8,7 +8,6 @@
 from jax.sharding import PartitionSpec as P
 
 NSTEPS = 4
-STREAMS = 4
 STEP_SIZE = -1.0 / NSTEPS
 BF16, F32 = jnp.bfloat16, jnp.float32
 VMEM_GRANT = 4 << 20
@@ -55,7 +54,7 @@
     return x * (0.5 * (1.0 + jnp.tanh(0.7978845608028654 * (x + 0.044715 * (x * x * x)))))
 
 
-def own_image(count, images):
+def own_image(images):
     tp = lax.axis_size("tp")
     return lax.axis_index("tp") * images // tp
 
@@ -94,17 +93,9 @@
         p_ref[:, piece * width : (piece + 1) * width] = cols[piece * height : (piece + 1) * height, :]
     q_ref[0:rank, :] = ub_ref[...]
     q_ref[rank : 2 * rank, :] = da_ref[...]
-    step = steps_ref[own_image(lat_ref.shape[0], steps_ref.shape[0])]
+    step = steps_ref[own_image(steps_ref.shape[0])]
     state = lat_ref[...].astype(F32)
     spread_out(modulated(state, mod_row(mod_ref, 0, step), mod_row(mod_ref, 1, step)), *outs[2:])
-
-
-def fetch_body(start, source, target, sems):
-    copies = stream_copies(source, target, sems, start)
-    for copy in copies:
-        copy.start()
-    for copy in copies:
-        copy.wait()
 
 
 def assemble_body(tp, dp, *refs):
@@ -128,29 +119,6 @@
     qt_ref[...] = q_ref[...].T
 
 
-def stream_copies(source, target, sems, start):
-    rows = target.shape[0] // STREAMS
-    copies = []
-    for i in range(STREAMS):
-        block = pl.ds(i * rows, rows)
-        copies.append(
-            pltpu.make_async_copy(
-                source.at[block, pl.ds(start, target.shape[1])], target.at[block], sems.at[i]
-            )
-        )
-    return copies
-
-
-def start_stream(source, target, sems, start):
-    rows = target.shape[0] // STREAMS
-    cols = pl.ds(start, target.shape[1])
-
-    @pl.loop(0, STREAMS)
-    def _(i):
-        block = pl.ds(pl.multiple_of(i * rows, rows), rows)
-        pltpu.make_async_copy(source.at[block, cols], target.at[block], sems.at[i]).start()
-
-
 def block_body(rank, *refs):
     x_refs, (p_ref, q_ref, pt_ref, qt_ref, wu_ref, wd_ref), refs = refs[:6], refs[6:12], refs[12:]
     outs, (x_all, hidden) = refs[:6], refs[6:]
@@ -167,8 +135,8 @@
     first_half = (lanes // rank) % 2 == 0
     low = jnp.dot(x_all[...], p_ref[...], preferred_element_type=F32)
     low = jnp.where(first_half, low, 0.0).astype(BF16)
-    tile = hidden.shape[1] // 2
-    for i in range(2):
+    tile = hidden.shape[1] // 3
+    for i in range(3):
         cols = slice(i * tile, (i + 1) * tile)
         upper = jnp.dot(x_all[...], wu_ref[:, cols], preferred_element_type=F32)
         upper += jnp.dot(low, q_ref[:, cols], preferred_element_type=F32)
@@ -199,13 +167,13 @@
     total = own_ref[...] + near_ref[...].astype(F32)
     first = total[:, :half] + far_ref[...].astype(F32)
     second = total[:, half:] + rest_2_ref[...].astype(F32) + rest_3_ref[...].astype(F32)
-    return jnp.concatenate([first, second], axis=1)
+    return first, second
 
 
 def middle_body(steps_ref, lat_ref, mod_ref, *refs):
     parts, (vel_ref, state_ref, out_ref, far_ref, rest_ref) = refs[:5], refs[5:]
-    step = steps_ref[own_image(lat_ref.shape[0], steps_ref.shape[0])]
-    vel = mod_row(mod_ref, 2, step) * summed(*parts)
+    step = steps_ref[own_image(steps_ref.shape[0])]
+    vel = mod_row(mod_ref, 2, step) * jnp.concatenate(summed(*parts), axis=1)
     state = lat_ref[...].astype(F32) + STEP_SIZE * vel
     vel_ref[...] = vel
     state_ref[...] = state
@@ -214,12 +182,25 @@
 
 
 def last_body(steps_ref, mod_ref, vel_ref, state_ref, *refs):
-    parts, (vels_ref, out_ref) = refs[:-2], refs[-2:]
-    step = steps_ref[own_image(out_ref.shape[0], steps_ref.shape[0])] + 1
-    vel = mod_row(mod_ref, 2, step) * summed(*parts)
-    vels_ref[0] = vel_ref[...]
-    vels_ref[1] = vel
-    out_ref[...] = state_ref[...] + STEP_SIZE * vel
+    parts, (vels_ref, out_ref, vel_held, state_held, sems) = refs[:5], refs[5:]
+    copies = [pltpu.make_async_copy(vel_ref, vels_ref.at[0], sems.at[0])]
+    copies[0].start()
+    step = steps_ref[own_image(steps_ref.shape[0])] + 1
+    gate = mod_row(mod_ref, 2, step)
+    half = state_ref.shape[1] // 2
+    for i, total in enumerate(summed(*parts)):
+        cols = slice(i * half, (i + 1) * half)
+        vel = gate[:, cols] * total
+        vel_held[:, cols] = vel
+        state_held[:, cols] = state_ref[:, cols] + STEP_SIZE * vel
+        place = (slice(None), pl.ds(i * half, half))
+        for k, (source, target) in enumerate(((vel_held, vels_ref.at[1]), (state_held, out_ref))):
+            copies.append(
+                pltpu.make_async_copy(source.at[place], target.at[place], sems.at[1 + 2 * i + k])
+            )
+            copies[-1].start()
+    for copy in copies:
+        copy.wait()
 
 
 def swap(x, axis, flip):
@@ -263,7 +244,6 @@
     rank = up_b.shape[0]
     both = 2 * rank * dp
     height = 2 * rank
-    extra = up_a.shape[0] // height * both
     mods = jnp.transpose(mod_table, (1, 0, 2))
     spread_shapes = (shape((count, width)), shape((count, half)), shape((count, half)))
 
@@ -271,7 +251,7 @@
     p_own, q_own, normed, far, rest = call(
         functools.partial(prepare_body, dp, rank),
         (
-            shape((height, extra)),
+            shape((height, up_a.shape[0] // height * both)),
             shape((height, hidden)),
         )
         + spread_shapes,
@@ -279,21 +259,9 @@
         (VMEM,) * 5,
         "prepare",
         flops=16 * rows * width * hidden,
-
         scratch=[(pltpu.SMEM if a is step_index else pltpu.VMEM)(a.shape, a.dtype) for a in sources]
         + [pltpu.SemaphoreType.DMA((7,))],
     )(*[pinned(a, pltpu.HBM) for a in sources])
-
-    def fetch(start, name):
-        return call(
-            functools.partial(fetch_body, start),
-            pltpu.VMEM((width, hidden // 2), BF16),
-            [HBM],
-            VMEM,
-            name,
-            [pltpu.SemaphoreType.DMA((STREAMS,))],
-            bytes_accessed=base_up.size * 2,
-        )(pinned(base_up, pltpu.HBM))
 
     far = swap(far, "tp", 2)
     p_line = jnp.concatenate([p_own] + [swap(p_own, "tp", k) for k in (1, 2, 3)], axis=1)
@@ -352,8 +320,9 @@
         last_body,
         (shape((2, count, width), F32), shape((count, width), F32)),
         [SMEM] + [VMEM] * 8,
-        (VMEM,) * 2,
+        (HBM,) * 2,
         "second_update",
+        [pltpu.VMEM((count, width), F32)] * 2 + [pltpu.SemaphoreType.DMA((5,))],
     )(step_index, mods, vel, state, *reduce(*sums))
 
 

time: 91.4 us -> 91.4 us (level)
  no operation moved by 1% of the time
where the time goes in v5:
time: 91.4 us; the launch traced here: 91.3 us
  waiting for transfers between devices  38.7 us (42%)
  starting transfers between devices  33.5 us (37%)
  Pallas kernels  18.1 us (20%)
  between operations  0.96 us (1%)
    ppermute x29, waiting for transfers between devices, swap(): lax.ppermute(x, axis, [(i, i ^ flip) for i in range(lax.axis_size(axis))])  38.7 us
    ppermute x29, starting transfers between devices, swap(): lax.ppermute(x, axis, [(i, i ^ flip) for i in range(lax.axis_size(axis))])  33.5 us
    pallas_call x2, Pallas kernels, block(): call(functools.partial(block_body, rank), (shape((count, width), F32), sh...  13.2 us
  transfers between devices with their start and end apart: 29, of which 18 were waited for; matrix products, arithmetic and copies ran while one was open for 0% of the time, Pallas kernels for 0%

profile of v5, /device:TPU:0, one launch (start us, length us, event | category | flops | bytes accessed | tf_op | source)
XLA Modules:
  0.0 91.3 jit_solution(14117489512892527387)
XLA Ops:
  0.7 1.6 %prepare.1 = (bf16[32,768]{1,0:T(8,128)(2,1)S(1)}, bf16[32,3072]{1,0:T(8,128)(2,1)S(1)}, bf16[32,3072]{1,0:T(8,128)(2,1)S(1)}, bf16[32,1536]{1,0:T(8,128)(2,1)S(1)}, bf16[32,1536]{1,0:T(8,128)(2,1)S(1)}) custom-call(bf16[64,192]{1,0:T(8,128)(2,1)} %bitcast.7, bf16[64,192]{1,0:T(8,128)(2,1)} %refs_1_.1, bf16[16,3072]{1,0:T(8,128)(2,1)} %refs_2_.1, ...), custom_call_target="tpu_custom_call" | custom-call | flops 19327352832 | tf_op jit(solution)/shard_map/prepare/pallas_call | solution.py:251
  2.3 5.1 %collective-permute-start.2 = (bf16[32,768]{1,0:T(8,128)(2,1)S(1)}, bf16[32,768]{1,0:T(8,128)(2,1)S(1)}, u32[]{:S(2)}, u32[]{:S(2)}) collective-permute-start(bf16[32,768]{1,0:T(8,128)(2,1)S(1)} %get-tuple-element.41), channel_id=1, source_target_pairs={{0,3},{1,2},{2,1},{3,0},{4,7},{5,6},{6,5},{7,4},{8,11},{9,10},{10,... | collective-permute-start | bytes 147464 | tf_op jit(solution)/shard_map/ppermute | solution.py:207
  7.4 0.6 collective-permute-start
  8.1 2.3 %collective-permute-start.8 = (bf16[32,1536]{1,0:T(8,128)(2,1)S(1)}, bf16[32,1536]{1,0:T(8,128)(2,1)S(1)}, u32[]{:S(2)}, u32[]{:S(2)}) collective-permute-start(bf16[32,1536]{1,0:T(8,128)(2,1)S(1)} %get-tuple-element.46), channel_id=1, source_target_pairs={{0,2},{1,3},{2,0},{3,1},{4,6},{5,7},{6,4},{7,5},{8,10},{9,11},{10,... | collective-permute-start | bytes 294920 | tf_op jit(solution)/shard_map/ppermute | solution.py:207
  10.3 1.5 %collective-permute-start.7 = (bf16[32,1536]{1,0:T(8,128)(2,1)S(1)}, bf16[32,1536]{1,0:T(8,128)(2,1)S(1)}, u32[]{:S(2)}, u32[]{:S(2)}) collective-permute-start(bf16[32,1536]{1,0:T(8,128)(2,1)S(1)} %get-tuple-element.45), channel_id=1, source_target_pairs={{0,3},{1,2},{2,1},{3,0},{4,7},{5,6},{6,5},{7,4},{8,11},{9,10},{10,... | collective-permute-start | bytes 294920 | tf_op jit(solution)/shard_map/ppermute | solution.py:207
  11.8 0.6 collective-permute-start.5
  12.4 3.7 %collective-permute-done.1 = bf16[32,768]{1,0:T(8,128)(2,1)S(1)} collective-permute-done((bf16[32,768]{1,0:T(8,128)(2,1)S(1)}, bf16[32,768]{1,0:T(8,128)(2,1)S(1)}, u32[]{:S(2)}, u32[]{:S(2)}) %collective-permute-start.1) | collective-permute-done | bytes 49184 | tf_op jit(solution)/shard_map/ppermute | solution.py:207
  16.1 1.6 %collective-permute-start.3 = (bf16[32,3072]{1,0:T(8,128)(2,1)S(1)}, bf16[32,3072]{1,0:T(8,128)(2,1)S(1)}, u32[]{:S(2)}, u32[]{:S(2)}) collective-permute-start(bf16[32,3072]{1,0:T(8,128)(2,1)S(1)} %pad_maximum_fusion.refs_0_), channel_id=1, source_target_pairs={{0,8},{4,12},{8,0},{12,4},{1,9},{5,13},{9,1},{13,5},{2,10},{6,14},... | collective-permute-start | bytes 589832 | tf_op jit(solution)/shard_map/ppermute | solution.py:207
  17.7 0.5 collective-permute-start.4
  18.2 1.1 %collective-permute-done.8.refs_2_ = bf16[32,1536]{1,0:T(8,128)(2,1)S(1)} collective-permute-done((bf16[32,1536]{1,0:T(8,128)(2,1)S(1)}, bf16[32,1536]{1,0:T(8,128)(2,1)S(1)}, u32[]{:S(2)}, u32[]{:S(2)}) %collective-permute-start.8) | collective-permute-done | bytes 98336 | tf_op jit(solution)/shard_map/ppermute | solution.py:207
  19.3 2.5 %collective-permute-start.9 = (bf16[32,1536]{1,0:T(8,128)(2,1)S(1)}, bf16[32,1536]{1,0:T(8,128)(2,1)S(1)}, u32[]{:S(2)}, u32[]{:S(2)}) collective-permute-start(bf16[32,1536]{1,0:T(8,128)(2,1)S(1)} %collective-permute-done.8.refs_2_), channel_id=1, source_target_pairs={{0,1},{1,0},{2,3},{3,2},{4,5},{5,4},{6,7},{7,6},{8,9},{9,8},{10,11... | collective-permute-start | bytes 294920 | tf_op jit(solution)/shard_map/ppermute | solution.py:207
  21.8 3.2 %collective-permute-done.6.refs_4_ = bf16[32,1536]{1,0:T(8,128)(2,1)S(1)} collective-permute-done((bf16[32,1536]{1,0:T(8,128)(2,1)S(1)}, bf16[32,1536]{1,0:T(8,128)(2,1)S(1)}, u32[]{:S(2)}, u32[]{:S(2)}) %collective-permute-start.6) | collective-permute-done | bytes 98336 | tf_op jit(solution)/shard_map/ppermute | solution.py:207
  25.0 0.6 collective-permute-done.9.refs_3_
  25.6 0.6 collective-permute-start.11
  26.1 0.1 collective-permute-start.13
  26.2 0.2 collective-permute-done.10.refs_1_
  26.4 0.6 collective-permute-done.12.refs_5_
  27.0 0.3 collective-permute-done.11.refs_3_
  27.3 0.3 collective-permute-done.13.refs_7_
  27.6 0.6 assemble_factors.1
  28.2 0.0 copy-start.2
  28.3 6.5 %block.2 = (f32[32,3072]{1,0:T(8,128)S(1)}, bf16[32,3072]{1,0:T(8,128)(2,1)S(1)}, bf16[32,1536]{1,0:T(8,128)(2,1)S(1)}, f32[32,1536]{1,0:T(8,128)S(1)}, bf16[32,...) custom-call(bf16[32,3072]{1,0:T(8,128)(2,1)S(1)} %get-tuple-element.40.refs_0_, ...), custom_call_target="tpu_custom_call" | custom-call | flops 4831838208 | bytes 37748736 | tf_op jit(solution)/shard_map/block/pallas_call | solution.py:291
  34.8 0.9 %collective-permute-start.15 = (bf16[32,1536]{1,0:T(8,128)(2,1)S(1)}, bf16[32,1536]{1,0:T(8,128)(2,1)S(1)}, u32[]{:S(2)}, u32[]{:S(2)}) collective-permute-start(bf16[32,1536]{1,0:T(8,128)(2,1)S(1)} %get-tuple-element.60), channel_id=1, source_target_pairs={{0,1},{1,0},{2,3},{3,2},{4,5},{5,4},{6,7},{7,6},{8,9},{9,8},{10,11... | collective-permute-start | bytes 294920 | tf_op jit(solution)/shard_map/ppermute | solution.py:207
  35.7 2.7 %collective-permute-start.16 = (bf16[32,1536]{1,0:T(8,128)(2,1)S(1)}, bf16[32,1536]{1,0:T(8,128)(2,1)S(1)}, u32[]{:S(2)}, u32[]{:S(2)}) collective-permute-start(bf16[32,1536]{1,0:T(8,128)(2,1)S(1)} %get-tuple-element.61), channel_id=1, source_target_pairs={{0,2},{1,3},{2,0},{3,1},{4,6},{5,7},{6,4},{7,5},{8,10},{9,11},{10,... | collective-permute-start | bytes 294920 | tf_op jit(solution)/shard_map/ppermute | solution.py:207
  38.4 0.3 collective-permute-start.14
  38.7 1.4 %collective-permute-start.18 = (bf16[32,1536]{1,0:T(8,128)(2,1)S(1)}, bf16[32,1536]{1,0:T(8,128)(2,1)S(1)}, u32[]{:S(2)}, u32[]{:S(2)}) collective-permute-start(bf16[32,1536]{1,0:T(8,128)(2,1)S(1)} %get-tuple-element.64), channel_id=1, source_target_pairs={{0,3},{1,2},{2,1},{3,0},{4,7},{5,6},{6,5},{7,4},{8,11},{9,10},{10,... | collective-permute-start | bytes 294920 | tf_op jit(solution)/shard_map/ppermute | solution.py:207
  40.1 2.0 %collective-permute-done.15.got_ref = bf16[32,1536]{1,0:T(8,128)(2,1)S(1)} collective-permute-done((bf16[32,1536]{1,0:T(8,128)(2,1)S(1)}, bf16[32,1536]{1,0:T(8,128)(2,1)S(1)}, u32[]{:S(2)}, u32[]{:S(2)}) %collective-permute-start.15) | collective-permute-done | bytes 98336 | tf_op jit(solution)/shard_map/ppermute | solution.py:207
  42.0 1.5 %collective-permute-done.16.refs_3_ = bf16[32,1536]{1,0:T(8,128)(2,1)S(1)} collective-permute-done((bf16[32,1536]{1,0:T(8,128)(2,1)S(1)}, bf16[32,1536]{1,0:T(8,128)(2,1)S(1)}, u32[]{:S(2)}, u32[]{:S(2)}) %collective-permute-start.16) | collective-permute-done | bytes 98336 | tf_op jit(solution)/shard_map/ppermute | solution.py:207
  43.5 1.5 %collective-permute-start.17 = (bf16[32,1536]{1,0:T(8,128)(2,1)S(1)}, bf16[32,1536]{1,0:T(8,128)(2,1)S(1)}, u32[]{:S(2)}, u32[]{:S(2)}) collective-permute-start(bf16[32,1536]{1,0:T(8,128)(2,1)S(1)} %relay.2), channel_id=1, source_target_pairs={{0,2},{1,3},{2,0},{3,1},{4,6},{5,7},{6,4},{7,5},{8,10},{9,11},{10,... | collective-permute-start | bytes 294920 | tf_op jit(solution)/shard_map/ppermute | solution.py:207
  45.1 5.1 %collective-permute-done.18.refs_4_ = bf16[32,1536]{1,0:T(8,128)(2,1)S(1)} collective-permute-done((bf16[32,1536]{1,0:T(8,128)(2,1)S(1)}, bf16[32,1536]{1,0:T(8,128)(2,1)S(1)}, u32[]{:S(2)}, u32[]{:S(2)}) %collective-permute-start.18) | collective-permute-done | bytes 98336 | tf_op jit(solution)/shard_map/ppermute | solution.py:207
  50.2 2.4 %collective-permute-done.17.refs_2_ = bf16[32,1536]{1,0:T(8,128)(2,1)S(1)} collective-permute-done((bf16[32,1536]{1,0:T(8,128)(2,1)S(1)}, bf16[32,1536]{1,0:T(8,128)(2,1)S(1)}, u32[]{:S(2)}, u32[]{:S(2)}) %collective-permute-start.17) | collective-permute-done | bytes 98336 | tf_op jit(solution)/shard_map/ppermute | solution.py:207
  52.7 0.9 %first_update.1 = (f32[32,3072]{1,0:T(8,128)S(1)}, f32[32,3072]{1,0:T(8,128)S(1)}, bf16[32,3072]{1,0:T(8,128)(2,1)S(1)}, bf16[32,1536]{1,0:T(8,128)(2,1)S(1)}, bf16[32,1536]{1,0:T(8,128)(2,1)S(1)}) custom-call(s32[2]{0:T(128)S(1)} %copy-done.4, bf16[32,3072]{1,0:T(8,128)(2,1)S(1)} %copy-done.3, f32[3,4,3072]{2,1,0:T(4,128)S(1)} %bitcast.4, ...), custom_call_target="tpu_custom_call" | custom-call | tf_op jit(solution)/shard_map/first_update/pallas_call | solution.py:310
  53.6 0.1 collective-permute-start.20
  53.7 2.3 %collective-permute-start.19 = (bf16[32,3072]{1,0:T(8,128)(2,1)S(1)}, bf16[32,3072]{1,0:T(8,128)(2,1)S(1)}, u32[]{:S(2)}, u32[]{:S(2)}) collective-permute-start(bf16[32,3072]{1,0:T(8,128)(2,1)S(1)} %get-tuple-element.67.refs_0_), channel_id=1, source_target_pairs={{0,1},{1,0},{2,3},{3,2},{4,5},{5,4},{6,7},{7,6},{8,9},{9,8},{10,11... | collective-permute-start | bytes 589832 | tf_op jit(solution)/shard_map/ppermute | solution.py:207
  56.0 2.1 %collective-permute-start.23 = (bf16[32,1536]{1,0:T(8,128)(2,1)S(1)}, bf16[32,1536]{1,0:T(8,128)(2,1)S(1)}, u32[]{:S(2)}, u32[]{:S(2)}) collective-permute-start(bf16[32,1536]{1,0:T(8,128)(2,1)S(1)} %get-tuple-element.69), channel_id=1, source_target_pairs={{0,3},{1,2},{2,1},{3,0},{4,7},{5,6},{6,5},{7,4},{8,11},{9,10},{10,... | collective-permute-start | bytes 294920 | tf_op jit(solution)/shard_map/ppermute | solution.py:207
  58.0 3.8 %collective-permute-done.20.refs_2_ = bf16[32,1536]{1,0:T(8,128)(2,1)S(1)} collective-permute-done((bf16[32,1536]{1,0:T(8,128)(2,1)S(1)}, bf16[32,1536]{1,0:T(8,128)(2,1)S(1)}, u32[]{:S(2)}, u32[]{:S(2)}) %collective-permute-start.20) | collective-permute-done | bytes 98336 | tf_op jit(solution)/shard_map/ppermute | solution.py:207
  61.9 4.1 %collective-permute-done.23.refs_5_ = bf16[32,1536]{1,0:T(8,128)(2,1)S(1)} collective-permute-done((bf16[32,1536]{1,0:T(8,128)(2,1)S(1)}, bf16[32,1536]{1,0:T(8,128)(2,1)S(1)}, u32[]{:S(2)}, u32[]{:S(2)}) %collective-permute-start.23) | collective-permute-done | bytes 98336 | tf_op jit(solution)/shard_map/ppermute | solution.py:207
  66.0 1.2 %collective-permute-done.22.refs_4_ = bf16[32,1536]{1,0:T(8,128)(2,1)S(1)} collective-permute-done((bf16[32,1536]{1,0:T(8,128)(2,1)S(1)}, bf16[32,1536]{1,0:T(8,128)(2,1)S(1)}, u32[]{:S(2)}, u32[]{:S(2)}) %collective-permute-start.22) | collective-permute-done | bytes 98336 | tf_op jit(solution)/shard_map/ppermute | solution.py:207
  67.3 6.7 %block.3 = (f32[32,3072]{1,0:T(8,128)S(1)}, bf16[32,3072]{1,0:T(8,128)(2,1)S(1)}, bf16[32,1536]{1,0:T(8,128)(2,1)S(1)}, f32[32,1536]{1,0:T(8,128)S(1)}, bf16[32,...) custom-call(bf16[32,3072]{1,0:T(8,128)(2,1)S(1)} %get-tuple-element.67.refs_0_, ...), custom_call_target="tpu_custom_call" | custom-call | flops 4831838208 | bytes 37748736 | tf_op jit(solution)/shard_map/block/pallas_call | solution.py:291
  74.0 0.7 collective-permute-start.25
  74.7 2.3 %collective-permute-start.26 = (bf16[32,1536]{1,0:T(8,128)(2,1)S(1)}, bf16[32,1536]{1,0:T(8,128)(2,1)S(1)}, u32[]{:S(2)}, u32[]{:S(2)}) collective-permute-start(bf16[32,1536]{1,0:T(8,128)(2,1)S(1)} %get-tuple-element.74), channel_id=1, source_target_pairs={{0,2},{1,3},{2,0},{3,1},{4,6},{5,7},{6,4},{7,5},{8,10},{9,11},{10,... | collective-permute-start | bytes 294920 | tf_op jit(solution)/shard_map/ppermute | solution.py:207
  76.9 0.7 collective-permute-start.24
  77.7 1.4 %collective-permute-start.28 = (bf16[32,1536]{1,0:T(8,128)(2,1)S(1)}, bf16[32,1536]{1,0:T(8,128)(2,1)S(1)}, u32[]{:S(2)}, u32[]{:S(2)}) collective-permute-start(bf16[32,1536]{1,0:T(8,128)(2,1)S(1)} %get-tuple-element.77), channel_id=1, source_target_pairs={{0,3},{1,2},{2,1},{3,0},{4,7},{5,6},{6,5},{7,4},{8,11},{9,10},{10,... | collective-permute-start | bytes 294920 | tf_op jit(solution)/shard_map/ppermute | solution.py:207
  79.1 2.8 %collective-permute-done.25.got_ref = bf16[32,1536]{1,0:T(8,128)(2,1)S(1)} collective-permute-done((bf16[32,1536]{1,0:T(8,128)(2,1)S(1)}, bf16[32,1536]{1,0:T(8,128)(2,1)S(1)}, u32[]{:S(2)}, u32[]{:S(2)}) %collective-permute-start.25) | collective-permute-done | bytes 98336 | tf_op jit(solution)/shard_map/ppermute | solution.py:207
  81.8 1.9 %collective-permute-start.27 = (bf16[32,1536]{1,0:T(8,128)(2,1)S(1)}, bf16[32,1536]{1,0:T(8,128)(2,1)S(1)}, u32[]{:S(2)}, u32[]{:S(2)}) collective-permute-start(bf16[32,1536]{1,0:T(8,128)(2,1)S(1)} %relay.3), channel_id=1, source_target_pairs={{0,2},{1,3},{2,0},{3,1},{4,6},{5,7},{6,4},{7,5},{8,10},{9,11},{10,... | collective-permute-start | bytes 294920 | tf_op jit(solution)/shard_map/ppermute | solution.py:207
  83.8 3.8 %collective-permute-done.28.refs_4_ = bf16[32,1536]{1,0:T(8,128)(2,1)S(1)} collective-permute-done((bf16[32,1536]{1,0:T(8,128)(2,1)S(1)}, bf16[32,1536]{1,0:T(8,128)(2,1)S(1)}, u32[]{:S(2)}, u32[]{:S(2)}) %collective-permute-start.28) | collective-permute-done | bytes 98336 | tf_op jit(solution)/shard_map/ppermute | solution.py:207
  87.6 1.9 %collective-permute-done.27.refs_2_ = bf16[32,1536]{1,0:T(8,128)(2,1)S(1)} collective-permute-done((bf16[32,1536]{1,0:T(8,128)(2,1)S(1)}, bf16[32,1536]{1,0:T(8,128)(2,1)S(1)}, u32[]{:S(2)}, u32[]{:S(2)}) %collective-permute-start.27) | collective-permute-done | bytes 98336 | tf_op jit(solution)/shard_map/ppermute | solution.py:207
  89.5 1.6 %second_update.1 = (f32[2,32,3072]{2,1,0:T(8,128)}, f32[32,3072]{1,0:T(8,128)}) custom-call(s32[2]{0:T(128)S(1)} %copy-done.4, f32[3,4,3072]{2,1,0:T(4,128)S(1)} %bitcast.5, f32[32,3072]{1,0:T(8,128)S(1)} %get-tuple-element.65.vel_ref, f32[32,3072]{1,0:T(8,128)S(1)} %get-tuple-element.66.state_ref, f32[32,3072]{1,0:T(8,128)S(1)} %get-tuple-element.70.refs_0_, ...), custom_call_target="tpu_custom_call" | custom-call | tf_op jit(solution)/shard_map/second_update/pallas_call | solution.py:319
  (29 shorter events, 0.1 us)
Async XLA Ops:
  0.6 27.6 %copy-start = (bf16[3072,3072]{1,0:T(8,128)(2,1)S(1)}, bf16[3072,3072]{1,0:T(8,128)(2,1)}, u32[]{:S(2)}) copy-start(bf16[3072,3072]{1,0:T(8,128)(2,1)} %refs_10_.3) | copy-start | bytes 56623108
  0.6 27.6 %copy-start.1 = (bf16[3072,3072]{1,0:T(8,128)(2,1)S(1)}, bf16[3072,3072]{1,0:T(8,128)(2,1)}, u32[]{:S(2)}) copy-start(bf16[3072,3072]{1,0:T(8,128)(2,1)} %refs_11_.3) | copy-start | bytes 56623108
  2.3 9.5 %collective-permute-start.2 = (bf16[32,768]{1,0:T(8,128)(2,1)S(1)}, bf16[32,768]{1,0:T(8,128)(2,1)S(1)}, u32[]{:S(2)}, u32[]{:S(2)}) collective-permute-start(bf16[32,768]{1,0:T(8,128)(2,1)S(1)} %get-tuple-element.41), channel_id=1, source_target_pairs={{0,3},{1,2},{2,1},{3,0},{4,7},{5,6},{6,5},{7,4},{8,11},{9,10},{10,... | collective-permute-start | bytes 147464 | tf_op jit(solution)/shard_map/ppermute | solution.py:207
  7.4 8.7 %collective-permute-start.1 = (bf16[32,768]{1,0:T(8,128)(2,1)S(1)}, bf16[32,768]{1,0:T(8,128)(2,1)S(1)}, u32[]{:S(2)}, u32[]{:S(2)}) collective-permute-start(bf16[32,768]{1,0:T(8,128)(2,1)S(1)} %get-tuple-element.41), channel_id=1, source_target_pairs={{0,2},{1,3},{2,0},{3,1},{4,6},{5,7},{6,4},{7,5},{8,10},{9,11},{10,... | collective-permute-start | bytes 147464 | tf_op jit(solution)/shard_map/ppermute | solution.py:207
  7.4 8.7 %collective-permute-start = (bf16[32,768]{1,0:T(8,128)(2,1)S(1)}, bf16[32,768]{1,0:T(8,128)(2,1)S(1)}, u32[]{:S(2)}, u32[]{:S(2)}) collective-permute-start(bf16[32,768]{1,0:T(8,128)(2,1)S(1)} %get-tuple-element.41), channel_id=1, source_target_pairs={{0,1},{1,0},{2,3},{3,2},{4,5},{5,4},{6,7},{7,6},{8,9},{9,8},{10,11... | collective-permute-start | bytes 147464 | tf_op jit(solution)/shard_map/ppermute | solution.py:207
  8.1 11.2 %collective-permute-start.8 = (bf16[32,1536]{1,0:T(8,128)(2,1)S(1)}, bf16[32,1536]{1,0:T(8,128)(2,1)S(1)}, u32[]{:S(2)}, u32[]{:S(2)}) collective-permute-start(bf16[32,1536]{1,0:T(8,128)(2,1)S(1)} %get-tuple-element.46), channel_id=1, source_target_pairs={{0,2},{1,3},{2,0},{3,1},{4,6},{5,7},{6,4},{7,5},{8,10},{9,11},{10,... | collective-permute-start | bytes 294920 | tf_op jit(solution)/shard_map/ppermute | solution.py:207
  10.3 9.0 %collective-permute-start.7 = (bf16[32,1536]{1,0:T(8,128)(2,1)S(1)}, bf16[32,1536]{1,0:T(8,128)(2,1)S(1)}, u32[]{:S(2)}, u32[]{:S(2)}) collective-permute-start(bf16[32,1536]{1,0:T(8,128)(2,1)S(1)} %get-tuple-element.45), channel_id=1, source_target_pairs={{0,3},{1,2},{2,1},{3,0},{4,7},{5,6},{6,5},{7,4},{8,11},{9,10},{10,... | collective-permute-start | bytes 294920 | tf_op jit(solution)/shard_map/ppermute | solution.py:207
  11.8 13.7 %collective-permute-start.5 = (bf16[32,3072]{1,0:T(8,128)(2,1)S(1)}, bf16[32,3072]{1,0:T(8,128)(2,1)S(1)}, u32[]{:S(2)}, u32[]{:S(2)}) collective-permute-start(bf16[32,3072]{1,0:T(8,128)(2,1)S(1)} %get-tuple-element.40.refs_0_), channel_id=1, source_target_pairs={{0,1},{1,0},{2,3},{3,2},{4,5},{5,4},{6,7},{7,6},{8,9},{9,8},{10,11... | collective-permute-start | bytes 589832 | tf_op jit(solution)/shard_map/ppermute | solution.py:207
  16.1 9.4 %collective-permute-start.3 = (bf16[32,3072]{1,0:T(8,128)(2,1)S(1)}, bf16[32,3072]{1,0:T(8,128)(2,1)S(1)}, u32[]{:S(2)}, u32[]{:S(2)}) collective-permute-start(bf16[32,3072]{1,0:T(8,128)(2,1)S(1)} %pad_maximum_fusion.refs_0_), channel_id=1, source_target_pairs={{0,8},{4,12},{8,0},{12,4},{1,9},{5,13},{9,1},{13,5},{2,10},{6,14},... | collective-permute-start | bytes 589832 | tf_op jit(solution)/shard_map/ppermute | solution.py:207
  17.7 7.9 %collective-permute-start.4 = (bf16[32,3072]{1,0:T(8,128)(2,1)S(1)}, bf16[32,3072]{1,0:T(8,128)(2,1)S(1)}, u32[]{:S(2)}, u32[]{:S(2)}) collective-permute-start(bf16[32,3072]{1,0:T(8,128)(2,1)S(1)} %get-tuple-element.44.refs_4_), channel_id=1, source_target_pairs={{0,8},{4,12},{8,0},{12,4},{1,9},{5,13},{9,1},{13,5},{2,10},{6,14},... | collective-permute-start | bytes 589832 | tf_op jit(solution)/shard_map/ppermute | solution.py:207
  19.3 5.7 %collective-permute-start.6 = (bf16[32,1536]{1,0:T(8,128)(2,1)S(1)}, bf16[32,1536]{1,0:T(8,128)(2,1)S(1)}, u32[]{:S(2)}, u32[]{:S(2)}) collective-permute-start(bf16[32,1536]{1,0:T(8,128)(2,1)S(1)} %get-tuple-element.45), channel_id=1, source_target_pairs={{0,2},{1,3},{2,0},{3,1},{4,6},{5,7},{6,4},{7,5},{8,10},{9,11},{10,... | collective-permute-start | bytes 294920 | tf_op jit(solution)/shard_map/ppermute | solution.py:207
  19.3 6.2 %collective-permute-start.9 = (bf16[32,1536]{1,0:T(8,128)(2,1)S(1)}, bf16[32,1536]{1,0:T(8,128)(2,1)S(1)}, u32[]{:S(2)}, u32[]{:S(2)}) collective-permute-start(bf16[32,1536]{1,0:T(8,128)(2,1)S(1)} %collective-permute-done.8.refs_2_), channel_id=1, source_target_pairs={{0,1},{1,0},{2,3},{3,2},{4,5},{5,4},{6,7},{7,6},{8,9},{9,8},{10,11... | collective-permute-start | bytes 294920 | tf_op jit(solution)/shard_map/ppermute | solution.py:207
  25.0 1.4 %collective-permute-start.10 = (bf16[32,3072]{1,0:T(8,128)(2,1)S(1)}, bf16[32,3072]{1,0:T(8,128)(2,1)S(1)}, u32[]{:S(2)}, u32[]{:S(2)}) collective-permute-start(bf16[32,3072]{1,0:T(8,128)(2,1)S(1)} %pad_maximum_fusion.refs_0_), channel_id=1, source_target_pairs={{0,4},{4,0},{8,12},{12,8},{1,5},{5,1},{9,13},{13,9},{2,6},{6,2},{1... | collective-permute-start | bytes 589832 | tf_op jit(solution)/shard_map/ppermute | solution.py:207
  25.5 1.4 %collective-permute-start.12 = (bf16[32,3072]{1,0:T(8,128)(2,1)S(1)}, bf16[32,3072]{1,0:T(8,128)(2,1)S(1)}, u32[]{:S(2)}, u32[]{:S(2)}) collective-permute-start(bf16[32,3072]{1,0:T(8,128)(2,1)S(1)} %get-tuple-element.44.refs_4_), channel_id=1, source_target_pairs={{0,4},{4,0},{8,12},{12,8},{1,5},{5,1},{9,13},{13,9},{2,6},{6,2},{1... | collective-permute-start | bytes 589832 | tf_op jit(solution)/shard_map/ppermute | solution.py:207
  25.6 1.7 %collective-permute-start.11 = (bf16[32,3072]{1,0:T(8,128)(2,1)S(1)}, bf16[32,3072]{1,0:T(8,128)(2,1)S(1)}, u32[]{:S(2)}, u32[]{:S(2)}) collective-permute-start(bf16[32,3072]{1,0:T(8,128)(2,1)S(1)} %collective-permute-done.3.refs_2_), channel_id=1, source_target_pairs={{0,4},{4,0},{8,12},{12,8},{1,5},{5,1},{9,13},{13,9},{2,6},{6,2},{1... | collective-permute-start | bytes 589832 | tf_op jit(solution)/shard_map/ppermute | solution.py:207
  26.1 1.4 %collective-permute-start.13 = (bf16[32,3072]{1,0:T(8,128)(2,1)S(1)}, bf16[32,3072]{1,0:T(8,128)(2,1)S(1)}, u32[]{:S(2)}, u32[]{:S(2)}) collective-permute-start(bf16[32,3072]{1,0:T(8,128)(2,1)S(1)} %collective-permute-done.4.refs_6_), channel_id=1, source_target_pairs={{0,4},{4,0},{8,12},{12,8},{1,5},{5,1},{9,13},{13,9},{2,6},{6,2},{1... | collective-permute-start | bytes 589832 | tf_op jit(solution)/shard_map/ppermute | solution.py:207
  28.2 24.4 %copy-start.2 = (f32[4,3,3072]{2,0,1:T(4,128)S(1)}, f32[4,3,3072]{2,0,1:T(4,128)}, u32[]{:S(2)}) copy-start(f32[4,3,3072]{2,0,1:T(4,128)} %param.11) | copy-start | bytes 442372
  28.2 24.4 %copy-start.3 = (bf16[32,3072]{1,0:T(8,128)(2,1)S(1)}, bf16[32,3072]{1,0:T(8,128)(2,1)}, u32[]{:S(2)}) copy-start(bf16[32,3072]{1,0:T(8,128)(2,1)} %lat_ref.1) | copy-start | bytes 589828
  28.2 24.4 %copy-start.4 = (s32[2]{0:T(128)S(1)}, s32[2]{0:T(128)}, u32[]{:S(2)}) copy-start(s32[2]{0:T(128)} %steps_ref.3) | copy-start | bytes 28
  34.8 7.3 %collective-permute-start.15 = (bf16[32,1536]{1,0:T(8,128)(2,1)S(1)}, bf16[32,1536]{1,0:T(8,128)(2,1)S(1)}, u32[]{:S(2)}, u32[]{:S(2)}) collective-permute-start(bf16[32,1536]{1,0:T(8,128)(2,1)S(1)} %get-tuple-element.60), channel_id=1, source_target_pairs={{0,1},{1,0},{2,3},{3,2},{4,5},{5,4},{6,7},{7,6},{8,9},{9,8},{10,11... | collective-permute-start | bytes 294920 | tf_op jit(solution)/shard_map/ppermute | solution.py:207
  35.7 7.8 %collective-permute-start.16 = (bf16[32,1536]{1,0:T(8,128)(2,1)S(1)}, bf16[32,1536]{1,0:T(8,128)(2,1)S(1)}, u32[]{:S(2)}, u32[]{:S(2)}) collective-permute-start(bf16[32,1536]{1,0:T(8,128)(2,1)S(1)} %get-tuple-element.61), channel_id=1, source_target_pairs={{0,2},{1,3},{2,0},{3,1},{4,6},{5,7},{6,4},{7,5},{8,10},{9,11},{10,... | collective-permute-start | bytes 294920 | tf_op jit(solution)/shard_map/ppermute | solution.py:207
  38.4 14.3 %collective-permute-start.14 = (bf16[32,3072]{1,0:T(8,128)(2,1)S(1)}, bf16[32,3072]{1,0:T(8,128)(2,1)S(1)}, u32[]{:S(2)}, u32[]{:S(2)}) collective-permute-start(bf16[32,3072]{1,0:T(8,128)(2,1)S(1)} %get-tuple-element.58), channel_id=1, source_target_pairs={{0,1},{1,0},{2,3},{3,2},{4,5},{5,4},{6,7},{7,6},{8,9},{9,8},{10,11... | collective-permute-start | bytes 589832 | tf_op jit(solution)/shard_map/ppermute | solution.py:207
  38.7 11.6 %collective-permute-start.18 = (bf16[32,1536]{1,0:T(8,128)(2,1)S(1)}, bf16[32,1536]{1,0:T(8,128)(2,1)S(1)}, u32[]{:S(2)}, u32[]{:S(2)}) collective-permute-start(bf16[32,1536]{1,0:T(8,128)(2,1)S(1)} %get-tuple-element.64), channel_id=1, source_target_pairs={{0,3},{1,2},{2,1},{3,0},{4,7},{5,6},{6,5},{7,4},{8,11},{9,10},{10,... | collective-permute-start | bytes 294920 | tf_op jit(solution)/shard_map/ppermute | solution.py:207
  43.5 9.1 %collective-permute-start.17 = (bf16[32,1536]{1,0:T(8,128)(2,1)S(1)}, bf16[32,1536]{1,0:T(8,128)(2,1)S(1)}, u32[]{:S(2)}, u32[]{:S(2)}) collective-permute-start(bf16[32,1536]{1,0:T(8,128)(2,1)S(1)} %relay.2), channel_id=1, source_target_pairs={{0,2},{1,3},{2,0},{3,1},{4,6},{5,7},{6,4},{7,5},{8,10},{9,11},{10,... | collective-permute-start | bytes 294920 | tf_op jit(solution)/shard_map/ppermute | solution.py:207
  53.6 8.3 %collective-permute-start.20 = (bf16[32,1536]{1,0:T(8,128)(2,1)S(1)}, bf16[32,1536]{1,0:T(8,128)(2,1)S(1)}, u32[]{:S(2)}, u32[]{:S(2)}) collective-permute-start(bf16[32,1536]{1,0:T(8,128)(2,1)S(1)} %get-tuple-element.68), channel_id=1, source_target_pairs={{0,2},{1,3},{2,0},{3,1},{4,6},{5,7},{6,4},{7,5},{8,10},{9,11},{10,... | collective-permute-start | bytes 294920 | tf_op jit(solution)/shard_map/ppermute | solution.py:207
  53.7 13.6 %collective-permute-start.19 = (bf16[32,3072]{1,0:T(8,128)(2,1)S(1)}, bf16[32,3072]{1,0:T(8,128)(2,1)S(1)}, u32[]{:S(2)}, u32[]{:S(2)}) collective-permute-start(bf16[32,3072]{1,0:T(8,128)(2,1)S(1)} %get-tuple-element.67.refs_0_), channel_id=1, source_target_pairs={{0,1},{1,0},{2,3},{3,2},{4,5},{5,4},{6,7},{7,6},{8,9},{9,8},{10,11... | collective-permute-start | bytes 589832 | tf_op jit(solution)/shard_map/ppermute | solution.py:207
  56.0 10.0 %collective-permute-start.23 = (bf16[32,1536]{1,0:T(8,128)(2,1)S(1)}, bf16[32,1536]{1,0:T(8,128)(2,1)S(1)}, u32[]{:S(2)}, u32[]{:S(2)}) collective-permute-start(bf16[32,1536]{1,0:T(8,128)(2,1)S(1)} %get-tuple-element.69), channel_id=1, source_target_pairs={{0,3},{1,2},{2,1},{3,0},{4,7},{5,6},{6,5},{7,4},{8,11},{9,10},{10,... | collective-permute-start | bytes 294920 | tf_op jit(solution)/shard_map/ppermute | solution.py:207
  58.0 9.2 %collective-permute-start.22 = (bf16[32,1536]{1,0:T(8,128)(2,1)S(1)}, bf16[32,1536]{1,0:T(8,128)(2,1)S(1)}, u32[]{:S(2)}, u32[]{:S(2)}) collective-permute-start(bf16[32,1536]{1,0:T(8,128)(2,1)S(1)} %get-tuple-element.69), channel_id=1, source_target_pairs={{0,2},{1,3},{2,0},{3,1},{4,6},{5,7},{6,4},{7,5},{8,10},{9,11},{10,... | collective-permute-start | bytes 294920 | tf_op jit(solution)/shard_map/ppermute | solution.py:207
  61.9 5.4 %collective-permute-start.21 = (bf16[32,1536]{1,0:T(8,128)(2,1)S(1)}, bf16[32,1536]{1,0:T(8,128)(2,1)S(1)}, u32[]{:S(2)}, u32[]{:S(2)}) collective-permute-start(bf16[32,1536]{1,0:T(8,128)(2,1)S(1)} %collective-permute-done.20.refs_2_), channel_id=1, source_target_pairs={{0,1},{1,0},{2,3},{3,2},{4,5},{5,4},{6,7},{7,6},{8,9},{9,8},{10,11... | collective-permute-start | bytes 294920 | tf_op jit(solution)/shard_map/ppermute | solution.py:207
  74.0 7.8 %collective-permute-start.25 = (bf16[32,1536]{1,0:T(8,128)(2,1)S(1)}, bf16[32,1536]{1,0:T(8,128)(2,1)S(1)}, u32[]{:S(2)}, u32[]{:S(2)}) collective-permute-start(bf16[32,1536]{1,0:T(8,128)(2,1)S(1)} %get-tuple-element.73), channel_id=1, source_target_pairs={{0,1},{1,0},{2,3},{3,2},{4,5},{5,4},{6,7},{7,6},{8,9},{9,8},{10,11... | collective-permute-start | bytes 294920 | tf_op jit(solution)/shard_map/ppermute | solution.py:207
  74.7 7.2 %collective-permute-start.26 = (bf16[32,1536]{1,0:T(8,128)(2,1)S(1)}, bf16[32,1536]{1,0:T(8,128)(2,1)S(1)}, u32[]{:S(2)}, u32[]{:S(2)}) collective-permute-start(bf16[32,1536]{1,0:T(8,128)(2,1)S(1)} %get-tuple-element.74), channel_id=1, source_target_pairs={{0,2},{1,3},{2,0},{3,1},{4,6},{5,7},{6,4},{7,5},{8,10},{9,11},{10,... | collective-permute-start | bytes 294920 | tf_op jit(solution)/shard_map/ppermute | solution.py:207
  76.9 10.7 %collective-permute-start.24 = (bf16[32,3072]{1,0:T(8,128)(2,1)S(1)}, bf16[32,3072]{1,0:T(8,128)(2,1)S(1)}, u32[]{:S(2)}, u32[]{:S(2)}) collective-permute-start(bf16[32,3072]{1,0:T(8,128)(2,1)S(1)} %get-tuple-element.71), channel_id=1, source_target_pairs={{0,1},{1,0},{2,3},{3,2},{4,5},{5,4},{6,7},{7,6},{8,9},{9,8},{10,11... | collective-permute-start | bytes 589832 | tf_op jit(solution)/shard_map/ppermute | solution.py:207
  77.7 9.9 %collective-permute-start.28 = (bf16[32,1536]{1,0:T(8,128)(2,1)S(1)}, bf16[32,1536]{1,0:T(8,128)(2,1)S(1)}, u32[]{:S(2)}, u32[]{:S(2)}) collective-permute-start(bf16[32,1536]{1,0:T(8,128)(2,1)S(1)} %get-tuple-element.77), channel_id=1, source_target_pairs={{0,3},{1,2},{2,1},{3,0},{4,7},{5,6},{6,5},{7,4},{8,11},{9,10},{10,... | collective-permute-start | bytes 294920 | tf_op jit(solution)/shard_map/ppermute | solution.py:207
  81.8 7.7 %collective-permute-start.27 = (bf16[32,1536]{1,0:T(8,128)(2,1)S(1)}, bf16[32,1536]{1,0:T(8,128)(2,1)S(1)}, u32[]{:S(2)}, u32[]{:S(2)}) collective-permute-start(bf16[32,1536]{1,0:T(8,128)(2,1)S(1)} %relay.3), channel_id=1, source_target_pairs={{0,2},{1,3},{2,0},{3,1},{4,6},{5,7},{6,4},{7,5},{8,10},{9,11},{10,... | collective-permute-start | bytes 294920 | tf_op jit(solution)/shard_map/ppermute | solution.py:207

commit v6 on v5

--- a/solution.py
+++ b/solution.py
@@ -136,11 +136,18 @@
     low = jnp.dot(x_all[...], p_ref[...], preferred_element_type=F32)
     low = jnp.where(first_half, low, 0.0).astype(BF16)
     tile = hidden.shape[1] // 3
+
+    def upper(i):
+        cols = slice(i * tile, (i + 1) * tile)
+        out = jnp.dot(x_all[...], wu_ref[:, cols], preferred_element_type=F32)
+        return out + jnp.dot(low, q_ref[:, cols], preferred_element_type=F32)
+
+    ahead = upper(0)
     for i in range(3):
-        cols = slice(i * tile, (i + 1) * tile)
-        upper = jnp.dot(x_all[...], wu_ref[:, cols], preferred_element_type=F32)
-        upper += jnp.dot(low, q_ref[:, cols], preferred_element_type=F32)
-        hidden[:, cols] = gelu(upper).astype(BF16)
+        now = ahead
+        if i < 2:
+            ahead = upper(i + 1)
+        hidden[:, i * tile : (i + 1) * tile] = gelu(now).astype(BF16)
     low = jnp.dot(hidden[...], qt_ref[...], preferred_element_type=F32)
     low = jnp.where(first_half, 0.0, low).astype(BF16)
     own_out, near_out, over_out, far_out, rest_2_out, rest_3_out = outs

time: 91.4 us -> 91.4 us (level)
  no operation moved by 1% of the time
where the time goes in v6:
time: 91.4 us; the launch traced here: 91.3 us
  waiting for transfers between devices  38.7 us (42%)
  starting transfers between devices  33.5 us (37%)
  Pallas kernels  18.1 us (20%)
  between operations  0.96 us (1%)
    ppermute x29, waiting for transfers between devices, swap(): lax.ppermute(x, axis, [(i, i ^ flip) for i in range(lax.axis_size(axis))])  38.7 us
    ppermute x29, starting transfers between devices, swap(): lax.ppermute(x, axis, [(i, i ^ flip) for i in range(lax.axis_size(axis))])  33.5 us
    pallas_call x2, Pallas kernels, block(): call(functools.partial(block_body, rank), (shape((count, width), F32), sh...  13.2 us
  transfers between devices with their start and end apart: 29, of which 18 were waited for; matrix products, arithmetic and copies ran while one was open for 0% of the time, Pallas kernels for 0%

profile of v6, /device:TPU:0, one launch (start us, length us, event | category | flops | bytes accessed | tf_op | source)
XLA Modules:
  0.0 91.3 jit_solution(14117489512892527387)
XLA Ops:
  0.7 1.6 %prepare.1 = (bf16[32,768]{1,0:T(8,128)(2,1)S(1)}, bf16[32,3072]{1,0:T(8,128)(2,1)S(1)}, bf16[32,3072]{1,0:T(8,128)(2,1)S(1)}, bf16[32,1536]{1,0:T(8,128)(2,1)S(1)}, bf16[32,1536]{1,0:T(8,128)(2,1)S(1)}) custom-call(bf16[64,192]{1,0:T(8,128)(2,1)} %bitcast.7, bf16[64,192]{1,0:T(8,128)(2,1)} %refs_1_.1, bf16[16,3072]{1,0:T(8,128)(2,1)} %refs_2_.1, ...), custom_call_target="tpu_custom_call" | custom-call | flops 19327352832 | tf_op jit(solution)/shard_map/prepare/pallas_call | solution.py:258
  2.3 5.1 %collective-permute-start.2 = (bf16[32,768]{1,0:T(8,128)(2,1)S(1)}, bf16[32,768]{1,0:T(8,128)(2,1)S(1)}, u32[]{:S(2)}, u32[]{:S(2)}) collective-permute-start(bf16[32,768]{1,0:T(8,128)(2,1)S(1)} %get-tuple-element.41), channel_id=1, source_target_pairs={{0,3},{1,2},{2,1},{3,0},{4,7},{5,6},{6,5},{7,4},{8,11},{9,10},{10,... | collective-permute-start | bytes 147464 | tf_op jit(solution)/shard_map/ppermute | solution.py:214
  7.4 0.6 collective-permute-start
  8.1 2.3 %collective-permute-start.8 = (bf16[32,1536]{1,0:T(8,128)(2,1)S(1)}, bf16[32,1536]{1,0:T(8,128)(2,1)S(1)}, u32[]{:S(2)}, u32[]{:S(2)}) collective-permute-start(bf16[32,1536]{1,0:T(8,128)(2,1)S(1)} %get-tuple-element.46), channel_id=1, source_target_pairs={{0,2},{1,3},{2,0},{3,1},{4,6},{5,7},{6,4},{7,5},{8,10},{9,11},{10,... | collective-permute-start | bytes 294920 | tf_op jit(solution)/shard_map/ppermute | solution.py:214
  10.3 1.5 %collective-permute-start.7 = (bf16[32,1536]{1,0:T(8,128)(2,1)S(1)}, bf16[32,1536]{1,0:T(8,128)(2,1)S(1)}, u32[]{:S(2)}, u32[]{:S(2)}) collective-permute-start(bf16[32,1536]{1,0:T(8,128)(2,1)S(1)} %get-tuple-element.45), channel_id=1, source_target_pairs={{0,3},{1,2},{2,1},{3,0},{4,7},{5,6},{6,5},{7,4},{8,11},{9,10},{10,... | collective-permute-start | bytes 294920 | tf_op jit(solution)/shard_map/ppermute | solution.py:214
  11.8 0.6 collective-permute-start.5
  12.4 3.7 %collective-permute-done.1 = bf16[32,768]{1,0:T(8,128)(2,1)S(1)} collective-permute-done((bf16[32,768]{1,0:T(8,128)(2,1)S(1)}, bf16[32,768]{1,0:T(8,128)(2,1)S(1)}, u32[]{:S(2)}, u32[]{:S(2)}) %collective-permute-start.1) | collective-permute-done | bytes 49184 | tf_op jit(solution)/shard_map/ppermute | solution.py:214
  16.1 1.6 %collective-permute-start.3 = (bf16[32,3072]{1,0:T(8,128)(2,1)S(1)}, bf16[32,3072]{1,0:T(8,128)(2,1)S(1)}, u32[]{:S(2)}, u32[]{:S(2)}) collective-permute-start(bf16[32,3072]{1,0:T(8,128)(2,1)S(1)} %pad_maximum_fusion.refs_0_), channel_id=1, source_target_pairs={{0,8},{4,12},{8,0},{12,4},{1,9},{5,13},{9,1},{13,5},{2,10},{6,14},... | collective-permute-start | bytes 589832 | tf_op jit(solution)/shard_map/ppermute | solution.py:214
  17.7 0.5 collective-permute-start.4
  18.2 1.1 %collective-permute-done.8.refs_2_ = bf16[32,1536]{1,0:T(8,128)(2,1)S(1)} collective-permute-done((bf16[32,1536]{1,0:T(8,128)(2,1)S(1)}, bf16[32,1536]{1,0:T(8,128)(2,1)S(1)}, u32[]{:S(2)}, u32[]{:S(2)}) %collective-permute-start.8) | collective-permute-done | bytes 98336 | tf_op jit(solution)/shard_map/ppermute | solution.py:214
  19.3 2.5 %collective-permute-start.9 = (bf16[32,1536]{1,0:T(8,128)(2,1)S(1)}, bf16[32,1536]{1,0:T(8,128)(2,1)S(1)}, u32[]{:S(2)}, u32[]{:S(2)}) collective-permute-start(bf16[32,1536]{1,0:T(8,128)(2,1)S(1)} %collective-permute-done.8.refs_2_), channel_id=1, source_target_pairs={{0,1},{1,0},{2,3},{3,2},{4,5},{5,4},{6,7},{7,6},{8,9},{9,8},{10,11... | collective-permute-start | bytes 294920 | tf_op jit(solution)/shard_map/ppermute | solution.py:214
  21.8 3.2 %collective-permute-done.6.refs_4_ = bf16[32,1536]{1,0:T(8,128)(2,1)S(1)} collective-permute-done((bf16[32,1536]{1,0:T(8,128)(2,1)S(1)}, bf16[32,1536]{1,0:T(8,128)(2,1)S(1)}, u32[]{:S(2)}, u32[]{:S(2)}) %collective-permute-start.6) | collective-permute-done | bytes 98336 | tf_op jit(solution)/shard_map/ppermute | solution.py:214
  25.0 0.6 collective-permute-done.9.refs_3_
  25.6 0.6 collective-permute-start.11
  26.1 0.1 collective-permute-start.13
  26.2 0.2 collective-permute-done.10.refs_1_
  26.4 0.6 collective-permute-done.12.refs_5_
  27.0 0.3 collective-permute-done.11.refs_3_
  27.3 0.3 collective-permute-done.13.refs_7_
  27.6 0.6 assemble_factors.1
  28.2 0.0 copy-start.2
  28.3 6.5 %block.2 = (f32[32,3072]{1,0:T(8,128)S(1)}, bf16[32,3072]{1,0:T(8,128)(2,1)S(1)}, bf16[32,1536]{1,0:T(8,128)(2,1)S(1)}, f32[32,1536]{1,0:T(8,128)S(1)}, bf16[32,...) custom-call(bf16[32,3072]{1,0:T(8,128)(2,1)S(1)} %get-tuple-element.40.refs_0_, ...), custom_call_target="tpu_custom_call" | custom-call | flops 4831838208 | bytes 37748736 | tf_op jit(solution)/shard_map/block/pallas_call | solution.py:298
  34.8 0.9 %collective-permute-start.15 = (bf16[32,1536]{1,0:T(8,128)(2,1)S(1)}, bf16[32,1536]{1,0:T(8,128)(2,1)S(1)}, u32[]{:S(2)}, u32[]{:S(2)}) collective-permute-start(bf16[32,1536]{1,0:T(8,128)(2,1)S(1)} %get-tuple-element.60), channel_id=1, source_target_pairs={{0,1},{1,0},{2,3},{3,2},{4,5},{5,4},{6,7},{7,6},{8,9},{9,8},{10,11... | collective-permute-start | bytes 294920 | tf_op jit(solution)/shard_map/ppermute | solution.py:214
  35.7 2.7 %collective-permute-start.16 = (bf16[32,1536]{1,0:T(8,128)(2,1)S(1)}, bf16[32,1536]{1,0:T(8,128)(2,1)S(1)}, u32[]{:S(2)}, u32[]{:S(2)}) collective-permute-start(bf16[32,1536]{1,0:T(8,128)(2,1)S(1)} %get-tuple-element.61), channel_id=1, source_target_pairs={{0,2},{1,3},{2,0},{3,1},{4,6},{5,7},{6,4},{7,5},{8,10},{9,11},{10,... | collective-permute-start | bytes 294920 | tf_op jit(solution)/shard_map/ppermute | solution.py:214
  38.4 0.3 collective-permute-start.14
  38.7 1.4 %collective-permute-start.18 = (bf16[32,1536]{1,0:T(8,128)(2,1)S(1)}, bf16[32,1536]{1,0:T(8,128)(2,1)S(1)}, u32[]{:S(2)}, u32[]{:S(2)}) collective-permute-start(bf16[32,1536]{1,0:T(8,128)(2,1)S(1)} %get-tuple-element.64), channel_id=1, source_target_pairs={{0,3},{1,2},{2,1},{3,0},{4,7},{5,6},{6,5},{7,4},{8,11},{9,10},{10,... | collective-permute-start | bytes 294920 | tf_op jit(solution)/shard_map/ppermute | solution.py:214
  40.1 2.0 %collective-permute-done.15.got_ref = bf16[32,1536]{1,0:T(8,128)(2,1)S(1)} collective-permute-done((bf16[32,1536]{1,0:T(8,128)(2,1)S(1)}, bf16[32,1536]{1,0:T(8,128)(2,1)S(1)}, u32[]{:S(2)}, u32[]{:S(2)}) %collective-permute-start.15) | collective-permute-done | bytes 98336 | tf_op jit(solution)/shard_map/ppermute | solution.py:214
  42.0 1.5 %collective-permute-done.16.refs_3_ = bf16[32,1536]{1,0:T(8,128)(2,1)S(1)} collective-permute-done((bf16[32,1536]{1,0:T(8,128)(2,1)S(1)}, bf16[32,1536]{1,0:T(8,128)(2,1)S(1)}, u32[]{:S(2)}, u32[]{:S(2)}) %collective-permute-start.16) | collective-permute-done | bytes 98336 | tf_op jit(solution)/shard_map/ppermute | solution.py:214
  43.5 1.5 %collective-permute-start.17 = (bf16[32,1536]{1,0:T(8,128)(2,1)S(1)}, bf16[32,1536]{1,0:T(8,128)(2,1)S(1)}, u32[]{:S(2)}, u32[]{:S(2)}) collective-permute-start(bf16[32,1536]{1,0:T(8,128)(2,1)S(1)} %relay.2), channel_id=1, source_target_pairs={{0,2},{1,3},{2,0},{3,1},{4,6},{5,7},{6,4},{7,5},{8,10},{9,11},{10,... | collective-permute-start | bytes 294920 | tf_op jit(solution)/shard_map/ppermute | solution.py:214
  45.1 5.1 %collective-permute-done.18.refs_4_ = bf16[32,1536]{1,0:T(8,128)(2,1)S(1)} collective-permute-done((bf16[32,1536]{1,0:T(8,128)(2,1)S(1)}, bf16[32,1536]{1,0:T(8,128)(2,1)S(1)}, u32[]{:S(2)}, u32[]{:S(2)}) %collective-permute-start.18) | collective-permute-done | bytes 98336 | tf_op jit(solution)/shard_map/ppermute | solution.py:214
  50.2 2.4 %collective-permute-done.17.refs_2_ = bf16[32,1536]{1,0:T(8,128)(2,1)S(1)} collective-permute-done((bf16[32,1536]{1,0:T(8,128)(2,1)S(1)}, bf16[32,1536]{1,0:T(8,128)(2,1)S(1)}, u32[]{:S(2)}, u32[]{:S(2)}) %collective-permute-start.17) | collective-permute-done | bytes 98336 | tf_op jit(solution)/shard_map/ppermute | solution.py:214
  52.7 0.9 %first_update.1 = (f32[32,3072]{1,0:T(8,128)S(1)}, f32[32,3072]{1,0:T(8,128)S(1)}, bf16[32,3072]{1,0:T(8,128)(2,1)S(1)}, bf16[32,1536]{1,0:T(8,128)(2,1)S(1)}, bf16[32,1536]{1,0:T(8,128)(2,1)S(1)}) custom-call(s32[2]{0:T(128)S(1)} %copy-done.4, bf16[32,3072]{1,0:T(8,128)(2,1)S(1)} %copy-done.3, f32[3,4,3072]{2,1,0:T(4,128)S(1)} %bitcast.4, ...), custom_call_target="tpu_custom_call" | custom-call | tf_op jit(solution)/shard_map/first_update/pallas_call | solution.py:317
  53.6 0.1 collective-permute-start.20
  53.7 2.3 %collective-permute-start.19 = (bf16[32,3072]{1,0:T(8,128)(2,1)S(1)}, bf16[32,3072]{1,0:T(8,128)(2,1)S(1)}, u32[]{:S(2)}, u32[]{:S(2)}) collective-permute-start(bf16[32,3072]{1,0:T(8,128)(2,1)S(1)} %get-tuple-element.67.refs_0_), channel_id=1, source_target_pairs={{0,1},{1,0},{2,3},{3,2},{4,5},{5,4},{6,7},{7,6},{8,9},{9,8},{10,11... | collective-permute-start | bytes 589832 | tf_op jit(solution)/shard_map/ppermute | solution.py:214
  56.0 2.1 %collective-permute-start.23 = (bf16[32,1536]{1,0:T(8,128)(2,1)S(1)}, bf16[32,1536]{1,0:T(8,128)(2,1)S(1)}, u32[]{:S(2)}, u32[]{:S(2)}) collective-permute-start(bf16[32,1536]{1,0:T(8,128)(2,1)S(1)} %get-tuple-element.69), channel_id=1, source_target_pairs={{0,3},{1,2},{2,1},{3,0},{4,7},{5,6},{6,5},{7,4},{8,11},{9,10},{10,... | collective-permute-start | bytes 294920 | tf_op jit(solution)/shard_map/ppermute | solution.py:214
  58.0 3.8 %collective-permute-done.20.refs_2_ = bf16[32,1536]{1,0:T(8,128)(2,1)S(1)} collective-permute-done((bf16[32,1536]{1,0:T(8,128)(2,1)S(1)}, bf16[32,1536]{1,0:T(8,128)(2,1)S(1)}, u32[]{:S(2)}, u32[]{:S(2)}) %collective-permute-start.20) | collective-permute-done | bytes 98336 | tf_op jit(solution)/shard_map/ppermute | solution.py:214
  61.9 4.1 %collective-permute-done.23.refs_5_ = bf16[32,1536]{1,0:T(8,128)(2,1)S(1)} collective-permute-done((bf16[32,1536]{1,0:T(8,128)(2,1)S(1)}, bf16[32,1536]{1,0:T(8,128)(2,1)S(1)}, u32[]{:S(2)}, u32[]{:S(2)}) %collective-permute-start.23) | collective-permute-done | bytes 98336 | tf_op jit(solution)/shard_map/ppermute | solution.py:214
  66.0 1.2 %collective-permute-done.22.refs_4_ = bf16[32,1536]{1,0:T(8,128)(2,1)S(1)} collective-permute-done((bf16[32,1536]{1,0:T(8,128)(2,1)S(1)}, bf16[32,1536]{1,0:T(8,128)(2,1)S(1)}, u32[]{:S(2)}, u32[]{:S(2)}) %collective-permute-start.22) | collective-permute-done | bytes 98336 | tf_op jit(solution)/shard_map/ppermute | solution.py:214
  67.3 6.7 %block.3 = (f32[32,3072]{1,0:T(8,128)S(1)}, bf16[32,3072]{1,0:T(8,128)(2,1)S(1)}, bf16[32,1536]{1,0:T(8,128)(2,1)S(1)}, f32[32,1536]{1,0:T(8,128)S(1)}, bf16[32,...) custom-call(bf16[32,3072]{1,0:T(8,128)(2,1)S(1)} %get-tuple-element.67.refs_0_, ...), custom_call_target="tpu_custom_call" | custom-call | flops 4831838208 | bytes 37748736 | tf_op jit(solution)/shard_map/block/pallas_call | solution.py:298
  74.0 0.7 collective-permute-start.25
  74.7 2.3 %collective-permute-start.26 = (bf16[32,1536]{1,0:T(8,128)(2,1)S(1)}, bf16[32,1536]{1,0:T(8,128)(2,1)S(1)}, u32[]{:S(2)}, u32[]{:S(2)}) collective-permute-start(bf16[32,1536]{1,0:T(8,128)(2,1)S(1)} %get-tuple-element.74), channel_id=1, source_target_pairs={{0,2},{1,3},{2,0},{3,1},{4,6},{5,7},{6,4},{7,5},{8,10},{9,11},{10,... | collective-permute-start | bytes 294920 | tf_op jit(solution)/shard_map/ppermute | solution.py:214
  76.9 0.7 collective-permute-start.24
  77.7 1.4 %collective-permute-start.28 = (bf16[32,1536]{1,0:T(8,128)(2,1)S(1)}, bf16[32,1536]{1,0:T(8,128)(2,1)S(1)}, u32[]{:S(2)}, u32[]{:S(2)}) collective-permute-start(bf16[32,1536]{1,0:T(8,128)(2,1)S(1)} %get-tuple-element.77), channel_id=1, source_target_pairs={{0,3},{1,2},{2,1},{3,0},{4,7},{5,6},{6,5},{7,4},{8,11},{9,10},{10,... | collective-permute-start | bytes 294920 | tf_op jit(solution)/shard_map/ppermute | solution.py:214
  79.1 2.8 %collective-permute-done.25.got_ref = bf16[32,1536]{1,0:T(8,128)(2,1)S(1)} collective-permute-done((bf16[32,1536]{1,0:T(8,128)(2,1)S(1)}, bf16[32,1536]{1,0:T(8,128)(2,1)S(1)}, u32[]{:S(2)}, u32[]{:S(2)}) %collective-permute-start.25) | collective-permute-done | bytes 98336 | tf_op jit(solution)/shard_map/ppermute | solution.py:214
  81.8 1.9 %collective-permute-start.27 = (bf16[32,1536]{1,0:T(8,128)(2,1)S(1)}, bf16[32,1536]{1,0:T(8,128)(2,1)S(1)}, u32[]{:S(2)}, u32[]{:S(2)}) collective-permute-start(bf16[32,1536]{1,0:T(8,128)(2,1)S(1)} %relay.3), channel_id=1, source_target_pairs={{0,2},{1,3},{2,0},{3,1},{4,6},{5,7},{6,4},{7,5},{8,10},{9,11},{10,... | collective-permute-start | bytes 294920 | tf_op jit(solution)/shard_map/ppermute | solution.py:214
  83.8 3.8 %collective-permute-done.28.refs_4_ = bf16[32,1536]{1,0:T(8,128)(2,1)S(1)} collective-permute-done((bf16[32,1536]{1,0:T(8,128)(2,1)S(1)}, bf16[32,1536]{1,0:T(8,128)(2,1)S(1)}, u32[]{:S(2)}, u32[]{:S(2)}) %collective-permute-start.28) | collective-permute-done | bytes 98336 | tf_op jit(solution)/shard_map/ppermute | solution.py:214
  87.6 1.9 %collective-permute-done.27.refs_2_ = bf16[32,1536]{1,0:T(8,128)(2,1)S(1)} collective-permute-done((bf16[32,1536]{1,0:T(8,128)(2,1)S(1)}, bf16[32,1536]{1,0:T(8,128)(2,1)S(1)}, u32[]{:S(2)}, u32[]{:S(2)}) %collective-permute-start.27) | collective-permute-done | bytes 98336 | tf_op jit(solution)/shard_map/ppermute | solution.py:214
  89.5 1.6 %second_update.1 = (f32[2,32,3072]{2,1,0:T(8,128)}, f32[32,3072]{1,0:T(8,128)}) custom-call(s32[2]{0:T(128)S(1)} %copy-done.4, f32[3,4,3072]{2,1,0:T(4,128)S(1)} %bitcast.5, f32[32,3072]{1,0:T(8,128)S(1)} %get-tuple-element.65.vel_ref, f32[32,3072]{1,0:T(8,128)S(1)} %get-tuple-element.66.state_ref, f32[32,3072]{1,0:T(8,128)S(1)} %get-tuple-element.70.refs_0_, ...), custom_call_target="tpu_custom_call" | custom-call | tf_op jit(solution)/shard_map/second_update/pallas_call | solution.py:326
  (29 shorter events, 0.1 us)
Async XLA Ops:
  0.6 27.6 %copy-start = (bf16[3072,3072]{1,0:T(8,128)(2,1)S(1)}, bf16[3072,3072]{1,0:T(8,128)(2,1)}, u32[]{:S(2)}) copy-start(bf16[3072,3072]{1,0:T(8,128)(2,1)} %refs_10_.3) | copy-start | bytes 56623108
  0.6 27.6 %copy-start.1 = (bf16[3072,3072]{1,0:T(8,128)(2,1)S(1)}, bf16[3072,3072]{1,0:T(8,128)(2,1)}, u32[]{:S(2)}) copy-start(bf16[3072,3072]{1,0:T(8,128)(2,1)} %refs_11_.3) | copy-start | bytes 56623108
  2.3 9.5 %collective-permute-start.2 = (bf16[32,768]{1,0:T(8,128)(2,1)S(1)}, bf16[32,768]{1,0:T(8,128)(2,1)S(1)}, u32[]{:S(2)}, u32[]{:S(2)}) collective-permute-start(bf16[32,768]{1,0:T(8,128)(2,1)S(1)} %get-tuple-element.41), channel_id=1, source_target_pairs={{0,3},{1,2},{2,1},{3,0},{4,7},{5,6},{6,5},{7,4},{8,11},{9,10},{10,... | collective-permute-start | bytes 147464 | tf_op jit(solution)/shard_map/ppermute | solution.py:214
  7.4 8.7 %collective-permute-start.1 = (bf16[32,768]{1,0:T(8,128)(2,1)S(1)}, bf16[32,768]{1,0:T(8,128)(2,1)S(1)}, u32[]{:S(2)}, u32[]{:S(2)}) collective-permute-start(bf16[32,768]{1,0:T(8,128)(2,1)S(1)} %get-tuple-element.41), channel_id=1, source_target_pairs={{0,2},{1,3},{2,0},{3,1},{4,6},{5,7},{6,4},{7,5},{8,10},{9,11},{10,... | collective-permute-start | bytes 147464 | tf_op jit(solution)/shard_map/ppermute | solution.py:214
  7.4 8.7 %collective-permute-start = (bf16[32,768]{1,0:T(8,128)(2,1)S(1)}, bf16[32,768]{1,0:T(8,128)(2,1)S(1)}, u32[]{:S(2)}, u32[]{:S(2)}) collective-permute-start(bf16[32,768]{1,0:T(8,128)(2,1)S(1)} %get-tuple-element.41), channel_id=1, source_target_pairs={{0,1},{1,0},{2,3},{3,2},{4,5},{5,4},{6,7},{7,6},{8,9},{9,8},{10,11... | collective-permute-start | bytes 147464 | tf_op jit(solution)/shard_map/ppermute | solution.py:214
  8.1 11.2 %collective-permute-start.8 = (bf16[32,1536]{1,0:T(8,128)(2,1)S(1)}, bf16[32,1536]{1,0:T(8,128)(2,1)S(1)}, u32[]{:S(2)}, u32[]{:S(2)}) collective-permute-start(bf16[32,1536]{1,0:T(8,128)(2,1)S(1)} %get-tuple-element.46), channel_id=1, source_target_pairs={{0,2},{1,3},{2,0},{3,1},{4,6},{5,7},{6,4},{7,5},{8,10},{9,11},{10,... | collective-permute-start | bytes 294920 | tf_op jit(solution)/shard_map/ppermute | solution.py:214
  10.3 9.0 %collective-permute-start.7 = (bf16[32,1536]{1,0:T(8,128)(2,1)S(1)}, bf16[32,1536]{1,0:T(8,128)(2,1)S(1)}, u32[]{:S(2)}, u32[]{:S(2)}) collective-permute-start(bf16[32,1536]{1,0:T(8,128)(2,1)S(1)} %get-tuple-element.45), channel_id=1, source_target_pairs={{0,3},{1,2},{2,1},{3,0},{4,7},{5,6},{6,5},{7,4},{8,11},{9,10},{10,... | collective-permute-start | bytes 294920 | tf_op jit(solution)/shard_map/ppermute | solution.py:214
  11.8 13.7 %collective-permute-start.5 = (bf16[32,3072]{1,0:T(8,128)(2,1)S(1)}, bf16[32,3072]{1,0:T(8,128)(2,1)S(1)}, u32[]{:S(2)}, u32[]{:S(2)}) collective-permute-start(bf16[32,3072]{1,0:T(8,128)(2,1)S(1)} %get-tuple-element.40.refs_0_), channel_id=1, source_target_pairs={{0,1},{1,0},{2,3},{3,2},{4,5},{5,4},{6,7},{7,6},{8,9},{9,8},{10,11... | collective-permute-start | bytes 589832 | tf_op jit(solution)/shard_map/ppermute | solution.py:214
  16.1 9.4 %collective-permute-start.3 = (bf16[32,3072]{1,0:T(8,128)(2,1)S(1)}, bf16[32,3072]{1,0:T(8,128)(2,1)S(1)}, u32[]{:S(2)}, u32[]{:S(2)}) collective-permute-start(bf16[32,3072]{1,0:T(8,128)(2,1)S(1)} %pad_maximum_fusion.refs_0_), channel_id=1, source_target_pairs={{0,8},{4,12},{8,0},{12,4},{1,9},{5,13},{9,1},{13,5},{2,10},{6,14},... | collective-permute-start | bytes 589832 | tf_op jit(solution)/shard_map/ppermute | solution.py:214
  17.7 7.9 %collective-permute-start.4 = (bf16[32,3072]{1,0:T(8,128)(2,1)S(1)}, bf16[32,3072]{1,0:T(8,128)(2,1)S(1)}, u32[]{:S(2)}, u32[]{:S(2)}) collective-permute-start(bf16[32,3072]{1,0:T(8,128)(2,1)S(1)} %get-tuple-element.44.refs_4_), channel_id=1, source_target_pairs={{0,8},{4,12},{8,0},{12,4},{1,9},{5,13},{9,1},{13,5},{2,10},{6,14},... | collective-permute-start | bytes 589832 | tf_op jit(solution)/shard_map/ppermute | solution.py:214
  19.3 5.7 %collective-permute-start.6 = (bf16[32,1536]{1,0:T(8,128)(2,1)S(1)}, bf16[32,1536]{1,0:T(8,128)(2,1)S(1)}, u32[]{:S(2)}, u32[]{:S(2)}) collective-permute-start(bf16[32,1536]{1,0:T(8,128)(2,1)S(1)} %get-tuple-element.45), channel_id=1, source_target_pairs={{0,2},{1,3},{2,0},{3,1},{4,6},{5,7},{6,4},{7,5},{8,10},{9,11},{10,... | collective-permute-start | bytes 294920 | tf_op jit(solution)/shard_map/ppermute | solution.py:214
  19.3 6.2 %collective-permute-start.9 = (bf16[32,1536]{1,0:T(8,128)(2,1)S(1)}, bf16[32,1536]{1,0:T(8,128)(2,1)S(1)}, u32[]{:S(2)}, u32[]{:S(2)}) collective-permute-start(bf16[32,1536]{1,0:T(8,128)(2,1)S(1)} %collective-permute-done.8.refs_2_), channel_id=1, source_target_pairs={{0,1},{1,0},{2,3},{3,2},{4,5},{5,4},{6,7},{7,6},{8,9},{9,8},{10,11... | collective-permute-start | bytes 294920 | tf_op jit(solution)/shard_map/ppermute | solution.py:214
  25.0 1.4 %collective-permute-start.10 = (bf16[32,3072]{1,0:T(8,128)(2,1)S(1)}, bf16[32,3072]{1,0:T(8,128)(2,1)S(1)}, u32[]{:S(2)}, u32[]{:S(2)}) collective-permute-start(bf16[32,3072]{1,0:T(8,128)(2,1)S(1)} %pad_maximum_fusion.refs_0_), channel_id=1, source_target_pairs={{0,4},{4,0},{8,12},{12,8},{1,5},{5,1},{9,13},{13,9},{2,6},{6,2},{1... | collective-permute-start | bytes 589832 | tf_op jit(solution)/shard_map/ppermute | solution.py:214
  25.5 1.4 %collective-permute-start.12 = (bf16[32,3072]{1,0:T(8,128)(2,1)S(1)}, bf16[32,3072]{1,0:T(8,128)(2,1)S(1)}, u32[]{:S(2)}, u32[]{:S(2)}) collective-permute-start(bf16[32,3072]{1,0:T(8,128)(2,1)S(1)} %get-tuple-element.44.refs_4_), channel_id=1, source_target_pairs={{0,4},{4,0},{8,12},{12,8},{1,5},{5,1},{9,13},{13,9},{2,6},{6,2},{1... | collective-permute-start | bytes 589832 | tf_op jit(solution)/shard_map/ppermute | solution.py:214
  25.6 1.7 %collective-permute-start.11 = (bf16[32,3072]{1,0:T(8,128)(2,1)S(1)}, bf16[32,3072]{1,0:T(8,128)(2,1)S(1)}, u32[]{:S(2)}, u32[]{:S(2)}) collective-permute-start(bf16[32,3072]{1,0:T(8,128)(2,1)S(1)} %collective-permute-done.3.refs_2_), channel_id=1, source_target_pairs={{0,4},{4,0},{8,12},{12,8},{1,5},{5,1},{9,13},{13,9},{2,6},{6,2},{1... | collective-permute-start | bytes 589832 | tf_op jit(solution)/shard_map/ppermute | solution.py:214
  26.1 1.4 %collective-permute-start.13 = (bf16[32,3072]{1,0:T(8,128)(2,1)S(1)}, bf16[32,3072]{1,0:T(8,128)(2,1)S(1)}, u32[]{:S(2)}, u32[]{:S(2)}) collective-permute-start(bf16[32,3072]{1,0:T(8,128)(2,1)S(1)} %collective-permute-done.4.refs_6_), channel_id=1, source_target_pairs={{0,4},{4,0},{8,12},{12,8},{1,5},{5,1},{9,13},{13,9},{2,6},{6,2},{1... | collective-permute-start | bytes 589832 | tf_op jit(solution)/shard_map/ppermute | solution.py:214
  28.2 24.4 %copy-start.2 = (f32[4,3,3072]{2,0,1:T(4,128)S(1)}, f32[4,3,3072]{2,0,1:T(4,128)}, u32[]{:S(2)}) copy-start(f32[4,3,3072]{2,0,1:T(4,128)} %param.11) | copy-start | bytes 442372
  28.2 24.4 %copy-start.3 = (bf16[32,3072]{1,0:T(8,128)(2,1)S(1)}, bf16[32,3072]{1,0:T(8,128)(2,1)}, u32[]{:S(2)}) copy-start(bf16[32,3072]{1,0:T(8,128)(2,1)} %lat_ref.1) | copy-start | bytes 589828
  28.2 24.4 %copy-start.4 = (s32[2]{0:T(128)S(1)}, s32[2]{0:T(128)}, u32[]{:S(2)}) copy-start(s32[2]{0:T(128)} %steps_ref.3) | copy-start | bytes 28
  34.8 7.3 %collective-permute-start.15 = (bf16[32,1536]{1,0:T(8,128)(2,1)S(1)}, bf16[32,1536]{1,0:T(8,128)(2,1)S(1)}, u32[]{:S(2)}, u32[]{:S(2)}) collective-permute-start(bf16[32,1536]{1,0:T(8,128)(2,1)S(1)} %get-tuple-element.60), channel_id=1, source_target_pairs={{0,1},{1,0},{2,3},{3,2},{4,5},{5,4},{6,7},{7,6},{8,9},{9,8},{10,11... | collective-permute-start | bytes 294920 | tf_op jit(solution)/shard_map/ppermute | solution.py:214
  35.7 7.8 %collective-permute-start.16 = (bf16[32,1536]{1,0:T(8,128)(2,1)S(1)}, bf16[32,1536]{1,0:T(8,128)(2,1)S(1)}, u32[]{:S(2)}, u32[]{:S(2)}) collective-permute-start(bf16[32,1536]{1,0:T(8,128)(2,1)S(1)} %get-tuple-element.61), channel_id=1, source_target_pairs={{0,2},{1,3},{2,0},{3,1},{4,6},{5,7},{6,4},{7,5},{8,10},{9,11},{10,... | collective-permute-start | bytes 294920 | tf_op jit(solution)/shard_map/ppermute | solution.py:214
  38.4 14.3 %collective-permute-start.14 = (bf16[32,3072]{1,0:T(8,128)(2,1)S(1)}, bf16[32,3072]{1,0:T(8,128)(2,1)S(1)}, u32[]{:S(2)}, u32[]{:S(2)}) collective-permute-start(bf16[32,3072]{1,0:T(8,128)(2,1)S(1)} %get-tuple-element.58), channel_id=1, source_target_pairs={{0,1},{1,0},{2,3},{3,2},{4,5},{5,4},{6,7},{7,6},{8,9},{9,8},{10,11... | collective-permute-start | bytes 589832 | tf_op jit(solution)/shard_map/ppermute | solution.py:214
  38.7 11.6 %collective-permute-start.18 = (bf16[32,1536]{1,0:T(8,128)(2,1)S(1)}, bf16[32,1536]{1,0:T(8,128)(2,1)S(1)}, u32[]{:S(2)}, u32[]{:S(2)}) collective-permute-start(bf16[32,1536]{1,0:T(8,128)(2,1)S(1)} %get-tuple-element.64), channel_id=1, source_target_pairs={{0,3},{1,2},{2,1},{3,0},{4,7},{5,6},{6,5},{7,4},{8,11},{9,10},{10,... | collective-permute-start | bytes 294920 | tf_op jit(solution)/shard_map/ppermute | solution.py:214
  43.5 9.1 %collective-permute-start.17 = (bf16[32,1536]{1,0:T(8,128)(2,1)S(1)}, bf16[32,1536]{1,0:T(8,128)(2,1)S(1)}, u32[]{:S(2)}, u32[]{:S(2)}) collective-permute-start(bf16[32,1536]{1,0:T(8,128)(2,1)S(1)} %relay.2), channel_id=1, source_target_pairs={{0,2},{1,3},{2,0},{3,1},{4,6},{5,7},{6,4},{7,5},{8,10},{9,11},{10,... | collective-permute-start | bytes 294920 | tf_op jit(solution)/shard_map/ppermute | solution.py:214
  53.6 8.3 %collective-permute-start.20 = (bf16[32,1536]{1,0:T(8,128)(2,1)S(1)}, bf16[32,1536]{1,0:T(8,128)(2,1)S(1)}, u32[]{:S(2)}, u32[]{:S(2)}) collective-permute-start(bf16[32,1536]{1,0:T(8,128)(2,1)S(1)} %get-tuple-element.68), channel_id=1, source_target_pairs={{0,2},{1,3},{2,0},{3,1},{4,6},{5,7},{6,4},{7,5},{8,10},{9,11},{10,... | collective-permute-start | bytes 294920 | tf_op jit(solution)/shard_map/ppermute | solution.py:214
  53.7 13.6 %collective-permute-start.19 = (bf16[32,3072]{1,0:T(8,128)(2,1)S(1)}, bf16[32,3072]{1,0:T(8,128)(2,1)S(1)}, u32[]{:S(2)}, u32[]{:S(2)}) collective-permute-start(bf16[32,3072]{1,0:T(8,128)(2,1)S(1)} %get-tuple-element.67.refs_0_), channel_id=1, source_target_pairs={{0,1},{1,0},{2,3},{3,2},{4,5},{5,4},{6,7},{7,6},{8,9},{9,8},{10,11... | collective-permute-start | bytes 589832 | tf_op jit(solution)/shard_map/ppermute | solution.py:214
  56.0 10.0 %collective-permute-start.23 = (bf16[32,1536]{1,0:T(8,128)(2,1)S(1)}, bf16[32,1536]{1,0:T(8,128)(2,1)S(1)}, u32[]{:S(2)}, u32[]{:S(2)}) collective-permute-start(bf16[32,1536]{1,0:T(8,128)(2,1)S(1)} %get-tuple-element.69), channel_id=1, source_target_pairs={{0,3},{1,2},{2,1},{3,0},{4,7},{5,6},{6,5},{7,4},{8,11},{9,10},{10,... | collective-permute-start | bytes 294920 | tf_op jit(solution)/shard_map/ppermute | solution.py:214
  58.0 9.2 %collective-permute-start.22 = (bf16[32,1536]{1,0:T(8,128)(2,1)S(1)}, bf16[32,1536]{1,0:T(8,128)(2,1)S(1)}, u32[]{:S(2)}, u32[]{:S(2)}) collective-permute-start(bf16[32,1536]{1,0:T(8,128)(2,1)S(1)} %get-tuple-element.69), channel_id=1, source_target_pairs={{0,2},{1,3},{2,0},{3,1},{4,6},{5,7},{6,4},{7,5},{8,10},{9,11},{10,... | collective-permute-start | bytes 294920 | tf_op jit(solution)/shard_map/ppermute | solution.py:214
  61.9 5.4 %collective-permute-start.21 = (bf16[32,1536]{1,0:T(8,128)(2,1)S(1)}, bf16[32,1536]{1,0:T(8,128)(2,1)S(1)}, u32[]{:S(2)}, u32[]{:S(2)}) collective-permute-start(bf16[32,1536]{1,0:T(8,128)(2,1)S(1)} %collective-permute-done.20.refs_2_), channel_id=1, source_target_pairs={{0,1},{1,0},{2,3},{3,2},{4,5},{5,4},{6,7},{7,6},{8,9},{9,8},{10,11... | collective-permute-start | bytes 294920 | tf_op jit(solution)/shard_map/ppermute | solution.py:214
  74.0 7.8 %collective-permute-start.25 = (bf16[32,1536]{1,0:T(8,128)(2,1)S(1)}, bf16[32,1536]{1,0:T(8,128)(2,1)S(1)}, u32[]{:S(2)}, u32[]{:S(2)}) collective-permute-start(bf16[32,1536]{1,0:T(8,128)(2,1)S(1)} %get-tuple-element.73), channel_id=1, source_target_pairs={{0,1},{1,0},{2,3},{3,2},{4,5},{5,4},{6,7},{7,6},{8,9},{9,8},{10,11... | collective-permute-start | bytes 294920 | tf_op jit(solution)/shard_map/ppermute | solution.py:214
  74.7 7.2 %collective-permute-start.26 = (bf16[32,1536]{1,0:T(8,128)(2,1)S(1)}, bf16[32,1536]{1,0:T(8,128)(2,1)S(1)}, u32[]{:S(2)}, u32[]{:S(2)}) collective-permute-start(bf16[32,1536]{1,0:T(8,128)(2,1)S(1)} %get-tuple-element.74), channel_id=1, source_target_pairs={{0,2},{1,3},{2,0},{3,1},{4,6},{5,7},{6,4},{7,5},{8,10},{9,11},{10,... | collective-permute-start | bytes 294920 | tf_op jit(solution)/shard_map/ppermute | solution.py:214
  76.9 10.7 %collective-permute-start.24 = (bf16[32,3072]{1,0:T(8,128)(2,1)S(1)}, bf16[32,3072]{1,0:T(8,128)(2,1)S(1)}, u32[]{:S(2)}, u32[]{:S(2)}) collective-permute-start(bf16[32,3072]{1,0:T(8,128)(2,1)S(1)} %get-tuple-element.71), channel_id=1, source_target_pairs={{0,1},{1,0},{2,3},{3,2},{4,5},{5,4},{6,7},{7,6},{8,9},{9,8},{10,11... | collective-permute-start | bytes 589832 | tf_op jit(solution)/shard_map/ppermute | solution.py:214
  77.7 9.9 %collective-permute-start.28 = (bf16[32,1536]{1,0:T(8,128)(2,1)S(1)}, bf16[32,1536]{1,0:T(8,128)(2,1)S(1)}, u32[]{:S(2)}, u32[]{:S(2)}) collective-permute-start(bf16[32,1536]{1,0:T(8,128)(2,1)S(1)} %get-tuple-element.77), channel_id=1, source_target_pairs={{0,3},{1,2},{2,1},{3,0},{4,7},{5,6},{6,5},{7,4},{8,11},{9,10},{10,... | collective-permute-start | bytes 294920 | tf_op jit(solution)/shard_map/ppermute | solution.py:214
  81.8 7.7 %collective-permute-start.27 = (bf16[32,1536]{1,0:T(8,128)(2,1)S(1)}, bf16[32,1536]{1,0:T(8,128)(2,1)S(1)}, u32[]{:S(2)}, u32[]{:S(2)}) collective-permute-start(bf16[32,1536]{1,0:T(8,128)(2,1)S(1)} %relay.3), channel_id=1, source_target_pairs={{0,2},{1,3},{2,0},{3,1},{4,6},{5,7},{6,4},{7,5},{8,10},{9,11},{10,... | collective-permute-start | bytes 294920 | tf_op jit(solution)/shard_map/ppermute | solution.py:214

commit v7 on v6

--- a/solution.py
+++ b/solution.py
@@ -151,18 +151,14 @@
     low = jnp.dot(hidden[...], qt_ref[...], preferred_element_type=F32)
     low = jnp.where(first_half, 0.0, low).astype(BF16)
     own_out, near_out, over_out, far_out, rest_2_out, rest_3_out = outs
-    for i in range(2):
-        cols = slice(i * half, (i + 1) * half)
-        out = jnp.dot(hidden[...], wd_ref[:, cols], preferred_element_type=F32)
-        out += jnp.dot(low, pt_ref[:, cols], preferred_element_type=F32)
-        own_out[:, cols] = out[:count]
-        near_out[:, cols] = out[count : 2 * count].astype(BF16)
-        if i == 0:
-            far_out[...] = out[2 * count : 3 * count]
-            over_out[...] = out[3 * count :].astype(BF16)
-        else:
-            rest_2_out[...] = out[2 * count : 3 * count].astype(BF16)
-            rest_3_out[...] = out[3 * count :].astype(BF16)
+    out = jnp.dot(hidden[...], wd_ref[...], preferred_element_type=F32)
+    out += jnp.dot(low, pt_ref[...], preferred_element_type=F32)
+    own_out[...] = out[:count]
+    near_out[...] = out[count : 2 * count].astype(BF16)
+    far_out[...] = out[2 * count : 3 * count, :half]
+    over_out[...] = out[3 * count :, :half].astype(BF16)
+    rest_2_out[...] = out[2 * count : 3 * count, half:].astype(BF16)
+    rest_3_out[...] = out[3 * count :, half:].astype(BF16)
 
 
 def relay_body(mine_ref, got_ref, out_ref):

time: 91.4 us -> 91.4 us (level)
  no operation moved by 1% of the time
where the time goes in v7:
time: 91.4 us; the launch traced here: 91.3 us
  waiting for transfers between devices  38.7 us (42%)
  starting transfers between devices  33.5 us (37%)
  Pallas kernels  18.1 us (20%)
  between operations  0.96 us (1%)
    ppermute x29, waiting for transfers between devices, swap(): lax.ppermute(x, axis, [(i, i ^ flip) for i in range(lax.axis_size(axis))])  38.7 us
    ppermute x29, starting transfers between devices, swap(): lax.ppermute(x, axis, [(i, i ^ flip) for i in range(lax.axis_size(axis))])  33.5 us
    pallas_call x2, Pallas kernels, block(): call(functools.partial(block_body, rank), (shape((count, width), F32), sh...  13.2 us
  transfers between devices with their start and end apart: 29, of which 18 were waited for; matrix products, arithmetic and copies ran while one was open for 0% of the time, Pallas kernels for 0%

profile of v7, /device:TPU:0, one launch (start us, length us, event | category | flops | bytes accessed | tf_op | source)
XLA Modules:
  0.0 91.3 jit_solution(3667993757088697537)
XLA Ops:
  0.7 1.6 %prepare.1 = (bf16[32,768]{1,0:T(8,128)(2,1)S(1)}, bf16[32,3072]{1,0:T(8,128)(2,1)S(1)}, bf16[32,3072]{1,0:T(8,128)(2,1)S(1)}, bf16[32,1536]{1,0:T(8,128)(2,1)S(1)}, bf16[32,1536]{1,0:T(8,128)(2,1)S(1)}) custom-call(bf16[64,192]{1,0:T(8,128)(2,1)} %bitcast.7, bf16[64,192]{1,0:T(8,128)(2,1)} %refs_1_.1, bf16[16,3072]{1,0:T(8,128)(2,1)} %refs_2_.1, ...), custom_call_target="tpu_custom_call" | custom-call | flops 19327352832 | tf_op jit(solution)/shard_map/prepare/pallas_call | solution.py:254
  2.3 5.1 %collective-permute-start.2 = (bf16[32,768]{1,0:T(8,128)(2,1)S(1)}, bf16[32,768]{1,0:T(8,128)(2,1)S(1)}, u32[]{:S(2)}, u32[]{:S(2)}) collective-permute-start(bf16[32,768]{1,0:T(8,128)(2,1)S(1)} %get-tuple-element.41), channel_id=1, source_target_pairs={{0,3},{1,2},{2,1},{3,0},{4,7},{5,6},{6,5},{7,4},{8,11},{9,10},{10,... | collective-permute-start | bytes 147464 | tf_op jit(solution)/shard_map/ppermute | solution.py:210
  7.4 0.6 collective-permute-start
  8.1 2.3 %collective-permute-start.8 = (bf16[32,1536]{1,0:T(8,128)(2,1)S(1)}, bf16[32,1536]{1,0:T(8,128)(2,1)S(1)}, u32[]{:S(2)}, u32[]{:S(2)}) collective-permute-start(bf16[32,1536]{1,0:T(8,128)(2,1)S(1)} %get-tuple-element.46), channel_id=1, source_target_pairs={{0,2},{1,3},{2,0},{3,1},{4,6},{5,7},{6,4},{7,5},{8,10},{9,11},{10,... | collective-permute-start | bytes 294920 | tf_op jit(solution)/shard_map/ppermute | solution.py:210
  10.3 1.5 %collective-permute-start.7 = (bf16[32,1536]{1,0:T(8,128)(2,1)S(1)}, bf16[32,1536]{1,0:T(8,128)(2,1)S(1)}, u32[]{:S(2)}, u32[]{:S(2)}) collective-permute-start(bf16[32,1536]{1,0:T(8,128)(2,1)S(1)} %get-tuple-element.45), channel_id=1, source_target_pairs={{0,3},{1,2},{2,1},{3,0},{4,7},{5,6},{6,5},{7,4},{8,11},{9,10},{10,... | collective-permute-start | bytes 294920 | tf_op jit(solution)/shard_map/ppermute | solution.py:210
  11.8 0.6 collective-permute-start.5
  12.4 3.7 %collective-permute-done.1 = bf16[32,768]{1,0:T(8,128)(2,1)S(1)} collective-permute-done((bf16[32,768]{1,0:T(8,128)(2,1)S(1)}, bf16[32,768]{1,0:T(8,128)(2,1)S(1)}, u32[]{:S(2)}, u32[]{:S(2)}) %collective-permute-start.1) | collective-permute-done | bytes 49184 | tf_op jit(solution)/shard_map/ppermute | solution.py:210
  16.1 1.6 %collective-permute-start.3 = (bf16[32,3072]{1,0:T(8,128)(2,1)S(1)}, bf16[32,3072]{1,0:T(8,128)(2,1)S(1)}, u32[]{:S(2)}, u32[]{:S(2)}) collective-permute-start(bf16[32,3072]{1,0:T(8,128)(2,1)S(1)} %pad_maximum_fusion.refs_0_), channel_id=1, source_target_pairs={{0,8},{4,12},{8,0},{12,4},{1,9},{5,13},{9,1},{13,5},{2,10},{6,14},... | collective-permute-start | bytes 589832 | tf_op jit(solution)/shard_map/ppermute | solution.py:210
  17.7 0.5 collective-permute-start.4
  18.2 1.1 %collective-permute-done.8.refs_2_ = bf16[32,1536]{1,0:T(8,128)(2,1)S(1)} collective-permute-done((bf16[32,1536]{1,0:T(8,128)(2,1)S(1)}, bf16[32,1536]{1,0:T(8,128)(2,1)S(1)}, u32[]{:S(2)}, u32[]{:S(2)}) %collective-permute-start.8) | collective-permute-done | bytes 98336 | tf_op jit(solution)/shard_map/ppermute | solution.py:210
  19.3 2.5 %collective-permute-start.9 = (bf16[32,1536]{1,0:T(8,128)(2,1)S(1)}, bf16[32,1536]{1,0:T(8,128)(2,1)S(1)}, u32[]{:S(2)}, u32[]{:S(2)}) collective-permute-start(bf16[32,1536]{1,0:T(8,128)(2,1)S(1)} %collective-permute-done.8.refs_2_), channel_id=1, source_target_pairs={{0,1},{1,0},{2,3},{3,2},{4,5},{5,4},{6,7},{7,6},{8,9},{9,8},{10,11... | collective-permute-start | bytes 294920 | tf_op jit(solution)/shard_map/ppermute | solution.py:210
  21.8 3.2 %collective-permute-done.6.refs_4_ = bf16[32,1536]{1,0:T(8,128)(2,1)S(1)} collective-permute-done((bf16[32,1536]{1,0:T(8,128)(2,1)S(1)}, bf16[32,1536]{1,0:T(8,128)(2,1)S(1)}, u32[]{:S(2)}, u32[]{:S(2)}) %collective-permute-start.6) | collective-permute-done | bytes 98336 | tf_op jit(solution)/shard_map/ppermute | solution.py:210
  25.0 0.6 collective-permute-done.9.refs_3_
  25.6 0.6 collective-permute-start.11
  26.1 0.1 collective-permute-start.13
  26.2 0.2 collective-permute-done.10.refs_1_
  26.4 0.6 collective-permute-done.12.refs_5_
  27.0 0.3 collective-permute-done.11.refs_3_
  27.3 0.3 collective-permute-done.13.refs_7_
  27.6 0.6 assemble_factors.1
  28.2 0.0 copy-start.2
  28.3 6.5 %block.2 = (f32[32,3072]{1,0:T(8,128)S(1)}, bf16[32,3072]{1,0:T(8,128)(2,1)S(1)}, bf16[32,1536]{1,0:T(8,128)(2,1)S(1)}, f32[32,1536]{1,0:T(8,128)S(1)}, bf16[32,...) custom-call(bf16[32,3072]{1,0:T(8,128)(2,1)S(1)} %get-tuple-element.40.refs_0_, ...), custom_call_target="tpu_custom_call" | custom-call | flops 4831838208 | bytes 37748736 | tf_op jit(solution)/shard_map/block/pallas_call | solution.py:294
  34.8 0.9 %collective-permute-start.15 = (bf16[32,1536]{1,0:T(8,128)(2,1)S(1)}, bf16[32,1536]{1,0:T(8,128)(2,1)S(1)}, u32[]{:S(2)}, u32[]{:S(2)}) collective-permute-start(bf16[32,1536]{1,0:T(8,128)(2,1)S(1)} %get-tuple-element.60), channel_id=1, source_target_pairs={{0,1},{1,0},{2,3},{3,2},{4,5},{5,4},{6,7},{7,6},{8,9},{9,8},{10,11... | collective-permute-start | bytes 294920 | tf_op jit(solution)/shard_map/ppermute | solution.py:210
  35.7 2.7 %collective-permute-start.16 = (bf16[32,1536]{1,0:T(8,128)(2,1)S(1)}, bf16[32,1536]{1,0:T(8,128)(2,1)S(1)}, u32[]{:S(2)}, u32[]{:S(2)}) collective-permute-start(bf16[32,1536]{1,0:T(8,128)(2,1)S(1)} %get-tuple-element.61), channel_id=1, source_target_pairs={{0,2},{1,3},{2,0},{3,1},{4,6},{5,7},{6,4},{7,5},{8,10},{9,11},{10,... | collective-permute-start | bytes 294920 | tf_op jit(solution)/shard_map/ppermute | solution.py:210
  38.4 0.3 collective-permute-start.14
  38.7 1.4 %collective-permute-start.18 = (bf16[32,1536]{1,0:T(8,128)(2,1)S(1)}, bf16[32,1536]{1,0:T(8,128)(2,1)S(1)}, u32[]{:S(2)}, u32[]{:S(2)}) collective-permute-start(bf16[32,1536]{1,0:T(8,128)(2,1)S(1)} %get-tuple-element.64), channel_id=1, source_target_pairs={{0,3},{1,2},{2,1},{3,0},{4,7},{5,6},{6,5},{7,4},{8,11},{9,10},{10,... | collective-permute-start | bytes 294920 | tf_op jit(solution)/shard_map/ppermute | solution.py:210
  40.1 2.0 %collective-permute-done.15.got_ref = bf16[32,1536]{1,0:T(8,128)(2,1)S(1)} collective-permute-done((bf16[32,1536]{1,0:T(8,128)(2,1)S(1)}, bf16[32,1536]{1,0:T(8,128)(2,1)S(1)}, u32[]{:S(2)}, u32[]{:S(2)}) %collective-permute-start.15) | collective-permute-done | bytes 98336 | tf_op jit(solution)/shard_map/ppermute | solution.py:210
  42.0 1.5 %collective-permute-done.16.refs_3_ = bf16[32,1536]{1,0:T(8,128)(2,1)S(1)} collective-permute-done((bf16[32,1536]{1,0:T(8,128)(2,1)S(1)}, bf16[32,1536]{1,0:T(8,128)(2,1)S(1)}, u32[]{:S(2)}, u32[]{:S(2)}) %collective-permute-start.16) | collective-permute-done | bytes 98336 | tf_op jit(solution)/shard_map/ppermute | solution.py:210
  43.5 1.5 %collective-permute-start.17 = (bf16[32,1536]{1,0:T(8,128)(2,1)S(1)}, bf16[32,1536]{1,0:T(8,128)(2,1)S(1)}, u32[]{:S(2)}, u32[]{:S(2)}) collective-permute-start(bf16[32,1536]{1,0:T(8,128)(2,1)S(1)} %relay.2), channel_id=1, source_target_pairs={{0,2},{1,3},{2,0},{3,1},{4,6},{5,7},{6,4},{7,5},{8,10},{9,11},{10,... | collective-permute-start | bytes 294920 | tf_op jit(solution)/shard_map/ppermute | solution.py:210
  45.1 5.1 %collective-permute-done.18.refs_4_ = bf16[32,1536]{1,0:T(8,128)(2,1)S(1)} collective-permute-done((bf16[32,1536]{1,0:T(8,128)(2,1)S(1)}, bf16[32,1536]{1,0:T(8,128)(2,1)S(1)}, u32[]{:S(2)}, u32[]{:S(2)}) %collective-permute-start.18) | collective-permute-done | bytes 98336 | tf_op jit(solution)/shard_map/ppermute | solution.py:210
  50.2 2.4 %collective-permute-done.17.refs_2_ = bf16[32,1536]{1,0:T(8,128)(2,1)S(1)} collective-permute-done((bf16[32,1536]{1,0:T(8,128)(2,1)S(1)}, bf16[32,1536]{1,0:T(8,128)(2,1)S(1)}, u32[]{:S(2)}, u32[]{:S(2)}) %collective-permute-start.17) | collective-permute-done | bytes 98336 | tf_op jit(solution)/shard_map/ppermute | solution.py:210
  52.7 0.9 %first_update.1 = (f32[32,3072]{1,0:T(8,128)S(1)}, f32[32,3072]{1,0:T(8,128)S(1)}, bf16[32,3072]{1,0:T(8,128)(2,1)S(1)}, bf16[32,1536]{1,0:T(8,128)(2,1)S(1)}, bf16[32,1536]{1,0:T(8,128)(2,1)S(1)}) custom-call(s32[2]{0:T(128)S(1)} %copy-done.4, bf16[32,3072]{1,0:T(8,128)(2,1)S(1)} %copy-done.3, f32[3,4,3072]{2,1,0:T(4,128)S(1)} %bitcast.4, ...), custom_call_target="tpu_custom_call" | custom-call | tf_op jit(solution)/shard_map/first_update/pallas_call | solution.py:313
  53.6 0.1 collective-permute-start.20
  53.7 2.3 %collective-permute-start.19 = (bf16[32,3072]{1,0:T(8,128)(2,1)S(1)}, bf16[32,3072]{1,0:T(8,128)(2,1)S(1)}, u32[]{:S(2)}, u32[]{:S(2)}) collective-permute-start(bf16[32,3072]{1,0:T(8,128)(2,1)S(1)} %get-tuple-element.67.refs_0_), channel_id=1, source_target_pairs={{0,1},{1,0},{2,3},{3,2},{4,5},{5,4},{6,7},{7,6},{8,9},{9,8},{10,11... | collective-permute-start | bytes 589832 | tf_op jit(solution)/shard_map/ppermute | solution.py:210
  56.0 2.1 %collective-permute-start.23 = (bf16[32,1536]{1,0:T(8,128)(2,1)S(1)}, bf16[32,1536]{1,0:T(8,128)(2,1)S(1)}, u32[]{:S(2)}, u32[]{:S(2)}) collective-permute-start(bf16[32,1536]{1,0:T(8,128)(2,1)S(1)} %get-tuple-element.69), channel_id=1, source_target_pairs={{0,3},{1,2},{2,1},{3,0},{4,7},{5,6},{6,5},{7,4},{8,11},{9,10},{10,... | collective-permute-start | bytes 294920 | tf_op jit(solution)/shard_map/ppermute | solution.py:210
  58.0 3.8 %collective-permute-done.20.refs_2_ = bf16[32,1536]{1,0:T(8,128)(2,1)S(1)} collective-permute-done((bf16[32,1536]{1,0:T(8,128)(2,1)S(1)}, bf16[32,1536]{1,0:T(8,128)(2,1)S(1)}, u32[]{:S(2)}, u32[]{:S(2)}) %collective-permute-start.20) | collective-permute-done | bytes 98336 | tf_op jit(solution)/shard_map/ppermute | solution.py:210
  61.9 4.1 %collective-permute-done.23.refs_5_ = bf16[32,1536]{1,0:T(8,128)(2,1)S(1)} collective-permute-done((bf16[32,1536]{1,0:T(8,128)(2,1)S(1)}, bf16[32,1536]{1,0:T(8,128)(2,1)S(1)}, u32[]{:S(2)}, u32[]{:S(2)}) %collective-permute-start.23) | collective-permute-done | bytes 98336 | tf_op jit(solution)/shard_map/ppermute | solution.py:210
  66.0 1.2 %collective-permute-done.22.refs_4_ = bf16[32,1536]{1,0:T(8,128)(2,1)S(1)} collective-permute-done((bf16[32,1536]{1,0:T(8,128)(2,1)S(1)}, bf16[32,1536]{1,0:T(8,128)(2,1)S(1)}, u32[]{:S(2)}, u32[]{:S(2)}) %collective-permute-start.22) | collective-permute-done | bytes 98336 | tf_op jit(solution)/shard_map/ppermute | solution.py:210
  67.3 6.7 %block.3 = (f32[32,3072]{1,0:T(8,128)S(1)}, bf16[32,3072]{1,0:T(8,128)(2,1)S(1)}, bf16[32,1536]{1,0:T(8,128)(2,1)S(1)}, f32[32,1536]{1,0:T(8,128)S(1)}, bf16[32,...) custom-call(bf16[32,3072]{1,0:T(8,128)(2,1)S(1)} %get-tuple-element.67.refs_0_, ...), custom_call_target="tpu_custom_call" | custom-call | flops 4831838208 | bytes 37748736 | tf_op jit(solution)/shard_map/block/pallas_call | solution.py:294
  74.0 0.7 collective-permute-start.25
  74.7 2.3 %collective-permute-start.26 = (bf16[32,1536]{1,0:T(8,128)(2,1)S(1)}, bf16[32,1536]{1,0:T(8,128)(2,1)S(1)}, u32[]{:S(2)}, u32[]{:S(2)}) collective-permute-start(bf16[32,1536]{1,0:T(8,128)(2,1)S(1)} %get-tuple-element.74), channel_id=1, source_target_pairs={{0,2},{1,3},{2,0},{3,1},{4,6},{5,7},{6,4},{7,5},{8,10},{9,11},{10,... | collective-permute-start | bytes 294920 | tf_op jit(solution)/shard_map/ppermute | solution.py:210
  76.9 0.7 collective-permute-start.24
  77.7 1.4 %collective-permute-start.28 = (bf16[32,1536]{1,0:T(8,128)(2,1)S(1)}, bf16[32,1536]{1,0:T(8,128)(2,1)S(1)}, u32[]{:S(2)}, u32[]{:S(2)}) collective-permute-start(bf16[32,1536]{1,0:T(8,128)(2,1)S(1)} %get-tuple-element.77), channel_id=1, source_target_pairs={{0,3},{1,2},{2,1},{3,0},{4,7},{5,6},{6,5},{7,4},{8,11},{9,10},{10,... | collective-permute-start | bytes 294920 | tf_op jit(solution)/shard_map/ppermute | solution.py:210
  79.1 2.8 %collective-permute-done.25.got_ref = bf16[32,1536]{1,0:T(8,128)(2,1)S(1)} collective-permute-done((bf16[32,1536]{1,0:T(8,128)(2,1)S(1)}, bf16[32,1536]{1,0:T(8,128)(2,1)S(1)}, u32[]{:S(2)}, u32[]{:S(2)}) %collective-permute-start.25) | collective-permute-done | bytes 98336 | tf_op jit(solution)/shard_map/ppermute | solution.py:210
  81.9 1.9 %collective-permute-start.27 = (bf16[32,1536]{1,0:T(8,128)(2,1)S(1)}, bf16[32,1536]{1,0:T(8,128)(2,1)S(1)}, u32[]{:S(2)}, u32[]{:S(2)}) collective-permute-start(bf16[32,1536]{1,0:T(8,128)(2,1)S(1)} %relay.3), channel_id=1, source_target_pairs={{0,2},{1,3},{2,0},{3,1},{4,6},{5,7},{6,4},{7,5},{8,10},{9,11},{10,... | collective-permute-start | bytes 294920 | tf_op jit(solution)/shard_map/ppermute | solution.py:210
  83.8 3.8 %collective-permute-done.28.refs_4_ = bf16[32,1536]{1,0:T(8,128)(2,1)S(1)} collective-permute-done((bf16[32,1536]{1,0:T(8,128)(2,1)S(1)}, bf16[32,1536]{1,0:T(8,128)(2,1)S(1)}, u32[]{:S(2)}, u32[]{:S(2)}) %collective-permute-start.28) | collective-permute-done | bytes 98336 | tf_op jit(solution)/shard_map/ppermute | solution.py:210
  87.6 1.9 %collective-permute-done.27.refs_2_ = bf16[32,1536]{1,0:T(8,128)(2,1)S(1)} collective-permute-done((bf16[32,1536]{1,0:T(8,128)(2,1)S(1)}, bf16[32,1536]{1,0:T(8,128)(2,1)S(1)}, u32[]{:S(2)}, u32[]{:S(2)}) %collective-permute-start.27) | collective-permute-done | bytes 98336 | tf_op jit(solution)/shard_map/ppermute | solution.py:210
  89.5 1.6 %second_update.1 = (f32[2,32,3072]{2,1,0:T(8,128)}, f32[32,3072]{1,0:T(8,128)}) custom-call(s32[2]{0:T(128)S(1)} %copy-done.4, f32[3,4,3072]{2,1,0:T(4,128)S(1)} %bitcast.5, f32[32,3072]{1,0:T(8,128)S(1)} %get-tuple-element.65.vel_ref, f32[32,3072]{1,0:T(8,128)S(1)} %get-tuple-element.66.state_ref, f32[32,3072]{1,0:T(8,128)S(1)} %get-tuple-element.70.refs_0_, ...), custom_call_target="tpu_custom_call" | custom-call | tf_op jit(solution)/shard_map/second_update/pallas_call | solution.py:322
  (29 shorter events, 0.1 us)
Async XLA Ops:
  0.6 27.6 %copy-start = (bf16[3072,3072]{1,0:T(8,128)(2,1)S(1)}, bf16[3072,3072]{1,0:T(8,128)(2,1)}, u32[]{:S(2)}) copy-start(bf16[3072,3072]{1,0:T(8,128)(2,1)} %refs_10_.3) | copy-start | bytes 56623108
  0.6 27.6 %copy-start.1 = (bf16[3072,3072]{1,0:T(8,128)(2,1)S(1)}, bf16[3072,3072]{1,0:T(8,128)(2,1)}, u32[]{:S(2)}) copy-start(bf16[3072,3072]{1,0:T(8,128)(2,1)} %refs_11_.3) | copy-start | bytes 56623108
  2.3 9.5 %collective-permute-start.2 = (bf16[32,768]{1,0:T(8,128)(2,1)S(1)}, bf16[32,768]{1,0:T(8,128)(2,1)S(1)}, u32[]{:S(2)}, u32[]{:S(2)}) collective-permute-start(bf16[32,768]{1,0:T(8,128)(2,1)S(1)} %get-tuple-element.41), channel_id=1, source_target_pairs={{0,3},{1,2},{2,1},{3,0},{4,7},{5,6},{6,5},{7,4},{8,11},{9,10},{10,... | collective-permute-start | bytes 147464 | tf_op jit(solution)/shard_map/ppermute | solution.py:210
  7.4 8.7 %collective-permute-start.1 = (bf16[32,768]{1,0:T(8,128)(2,1)S(1)}, bf16[32,768]{1,0:T(8,128)(2,1)S(1)}, u32[]{:S(2)}, u32[]{:S(2)}) collective-permute-start(bf16[32,768]{1,0:T(8,128)(2,1)S(1)} %get-tuple-element.41), channel_id=1, source_target_pairs={{0,2},{1,3},{2,0},{3,1},{4,6},{5,7},{6,4},{7,5},{8,10},{9,11},{10,... | collective-permute-start | bytes 147464 | tf_op jit(solution)/shard_map/ppermute | solution.py:210
  7.4 8.7 %collective-permute-start = (bf16[32,768]{1,0:T(8,128)(2,1)S(1)}, bf16[32,768]{1,0:T(8,128)(2,1)S(1)}, u32[]{:S(2)}, u32[]{:S(2)}) collective-permute-start(bf16[32,768]{1,0:T(8,128)(2,1)S(1)} %get-tuple-element.41), channel_id=1, source_target_pairs={{0,1},{1,0},{2,3},{3,2},{4,5},{5,4},{6,7},{7,6},{8,9},{9,8},{10,11... | collective-permute-start | bytes 147464 | tf_op jit(solution)/shard_map/ppermute | solution.py:210
  8.1 11.2 %collective-permute-start.8 = (bf16[32,1536]{1,0:T(8,128)(2,1)S(1)}, bf16[32,1536]{1,0:T(8,128)(2,1)S(1)}, u32[]{:S(2)}, u32[]{:S(2)}) collective-permute-start(bf16[32,1536]{1,0:T(8,128)(2,1)S(1)} %get-tuple-element.46), channel_id=1, source_target_pairs={{0,2},{1,3},{2,0},{3,1},{4,6},{5,7},{6,4},{7,5},{8,10},{9,11},{10,... | collective-permute-start | bytes 294920 | tf_op jit(solution)/shard_map/ppermute | solution.py:210
  10.3 9.0 %collective-permute-start.7 = (bf16[32,1536]{1,0:T(8,128)(2,1)S(1)}, bf16[32,1536]{1,0:T(8,128)(2,1)S(1)}, u32[]{:S(2)}, u32[]{:S(2)}) collective-permute-start(bf16[32,1536]{1,0:T(8,128)(2,1)S(1)} %get-tuple-element.45), channel_id=1, source_target_pairs={{0,3},{1,2},{2,1},{3,0},{4,7},{5,6},{6,5},{7,4},{8,11},{9,10},{10,... | collective-permute-start | bytes 294920 | tf_op jit(solution)/shard_map/ppermute | solution.py:210
  11.8 13.7 %collective-permute-start.5 = (bf16[32,3072]{1,0:T(8,128)(2,1)S(1)}, bf16[32,3072]{1,0:T(8,128)(2,1)S(1)}, u32[]{:S(2)}, u32[]{:S(2)}) collective-permute-start(bf16[32,3072]{1,0:T(8,128)(2,1)S(1)} %get-tuple-element.40.refs_0_), channel_id=1, source_target_pairs={{0,1},{1,0},{2,3},{3,2},{4,5},{5,4},{6,7},{7,6},{8,9},{9,8},{10,11... | collective-permute-start | bytes 589832 | tf_op jit(solution)/shard_map/ppermute | solution.py:210
  16.1 9.4 %collective-permute-start.3 = (bf16[32,3072]{1,0:T(8,128)(2,1)S(1)}, bf16[32,3072]{1,0:T(8,128)(2,1)S(1)}, u32[]{:S(2)}, u32[]{:S(2)}) collective-permute-start(bf16[32,3072]{1,0:T(8,128)(2,1)S(1)} %pad_maximum_fusion.refs_0_), channel_id=1, source_target_pairs={{0,8},{4,12},{8,0},{12,4},{1,9},{5,13},{9,1},{13,5},{2,10},{6,14},... | collective-permute-start | bytes 589832 | tf_op jit(solution)/shard_map/ppermute | solution.py:210
  17.7 7.9 %collective-permute-start.4 = (bf16[32,3072]{1,0:T(8,128)(2,1)S(1)}, bf16[32,3072]{1,0:T(8,128)(2,1)S(1)}, u32[]{:S(2)}, u32[]{:S(2)}) collective-permute-start(bf16[32,3072]{1,0:T(8,128)(2,1)S(1)} %get-tuple-element.44.refs_4_), channel_id=1, source_target_pairs={{0,8},{4,12},{8,0},{12,4},{1,9},{5,13},{9,1},{13,5},{2,10},{6,14},... | collective-permute-start | bytes 589832 | tf_op jit(solution)/shard_map/ppermute | solution.py:210
  19.3 5.7 %collective-permute-start.6 = (bf16[32,1536]{1,0:T(8,128)(2,1)S(1)}, bf16[32,1536]{1,0:T(8,128)(2,1)S(1)}, u32[]{:S(2)}, u32[]{:S(2)}) collective-permute-start(bf16[32,1536]{1,0:T(8,128)(2,1)S(1)} %get-tuple-element.45), channel_id=1, source_target_pairs={{0,2},{1,3},{2,0},{3,1},{4,6},{5,7},{6,4},{7,5},{8,10},{9,11},{10,... | collective-permute-start | bytes 294920 | tf_op jit(solution)/shard_map/ppermute | solution.py:210
  19.3 6.2 %collective-permute-start.9 = (bf16[32,1536]{1,0:T(8,128)(2,1)S(1)}, bf16[32,1536]{1,0:T(8,128)(2,1)S(1)}, u32[]{:S(2)}, u32[]{:S(2)}) collective-permute-start(bf16[32,1536]{1,0:T(8,128)(2,1)S(1)} %collective-permute-done.8.refs_2_), channel_id=1, source_target_pairs={{0,1},{1,0},{2,3},{3,2},{4,5},{5,4},{6,7},{7,6},{8,9},{9,8},{10,11... | collective-permute-start | bytes 294920 | tf_op jit(solution)/shard_map/ppermute | solution.py:210
  25.0 1.4 %collective-permute-start.10 = (bf16[32,3072]{1,0:T(8,128)(2,1)S(1)}, bf16[32,3072]{1,0:T(8,128)(2,1)S(1)}, u32[]{:S(2)}, u32[]{:S(2)}) collective-permute-start(bf16[32,3072]{1,0:T(8,128)(2,1)S(1)} %pad_maximum_fusion.refs_0_), channel_id=1, source_target_pairs={{0,4},{4,0},{8,12},{12,8},{1,5},{5,1},{9,13},{13,9},{2,6},{6,2},{1... | collective-permute-start | bytes 589832 | tf_op jit(solution)/shard_map/ppermute | solution.py:210
  25.5 1.4 %collective-permute-start.12 = (bf16[32,3072]{1,0:T(8,128)(2,1)S(1)}, bf16[32,3072]{1,0:T(8,128)(2,1)S(1)}, u32[]{:S(2)}, u32[]{:S(2)}) collective-permute-start(bf16[32,3072]{1,0:T(8,128)(2,1)S(1)} %get-tuple-element.44.refs_4_), channel_id=1, source_target_pairs={{0,4},{4,0},{8,12},{12,8},{1,5},{5,1},{9,13},{13,9},{2,6},{6,2},{1... | collective-permute-start | bytes 589832 | tf_op jit(solution)/shard_map/ppermute | solution.py:210
  25.6 1.7 %collective-permute-start.11 = (bf16[32,3072]{1,0:T(8,128)(2,1)S(1)}, bf16[32,3072]{1,0:T(8,128)(2,1)S(1)}, u32[]{:S(2)}, u32[]{:S(2)}) collective-permute-start(bf16[32,3072]{1,0:T(8,128)(2,1)S(1)} %collective-permute-done.3.refs_2_), channel_id=1, source_target_pairs={{0,4},{4,0},{8,12},{12,8},{1,5},{5,1},{9,13},{13,9},{2,6},{6,2},{1... | collective-permute-start | bytes 589832 | tf_op jit(solution)/shard_map/ppermute | solution.py:210
  26.1 1.4 %collective-permute-start.13 = (bf16[32,3072]{1,0:T(8,128)(2,1)S(1)}, bf16[32,3072]{1,0:T(8,128)(2,1)S(1)}, u32[]{:S(2)}, u32[]{:S(2)}) collective-permute-start(bf16[32,3072]{1,0:T(8,128)(2,1)S(1)} %collective-permute-done.4.refs_6_), channel_id=1, source_target_pairs={{0,4},{4,0},{8,12},{12,8},{1,5},{5,1},{9,13},{13,9},{2,6},{6,2},{1... | collective-permute-start | bytes 589832 | tf_op jit(solution)/shard_map/ppermute | solution.py:210
  28.2 24.4 %copy-start.2 = (f32[4,3,3072]{2,0,1:T(4,128)S(1)}, f32[4,3,3072]{2,0,1:T(4,128)}, u32[]{:S(2)}) copy-start(f32[4,3,3072]{2,0,1:T(4,128)} %param.11) | copy-start | bytes 442372
  28.2 24.4 %copy-start.3 = (bf16[32,3072]{1,0:T(8,128)(2,1)S(1)}, bf16[32,3072]{1,0:T(8,128)(2,1)}, u32[]{:S(2)}) copy-start(bf16[32,3072]{1,0:T(8,128)(2,1)} %lat_ref.1) | copy-start | bytes 589828
  28.2 24.4 %copy-start.4 = (s32[2]{0:T(128)S(1)}, s32[2]{0:T(128)}, u32[]{:S(2)}) copy-start(s32[2]{0:T(128)} %steps_ref.3) | copy-start | bytes 28
  34.8 7.3 %collective-permute-start.15 = (bf16[32,1536]{1,0:T(8,128)(2,1)S(1)}, bf16[32,1536]{1,0:T(8,128)(2,1)S(1)}, u32[]{:S(2)}, u32[]{:S(2)}) collective-permute-start(bf16[32,1536]{1,0:T(8,128)(2,1)S(1)} %get-tuple-element.60), channel_id=1, source_target_pairs={{0,1},{1,0},{2,3},{3,2},{4,5},{5,4},{6,7},{7,6},{8,9},{9,8},{10,11... | collective-permute-start | bytes 294920 | tf_op jit(solution)/shard_map/ppermute | solution.py:210
  35.7 7.8 %collective-permute-start.16 = (bf16[32,1536]{1,0:T(8,128)(2,1)S(1)}, bf16[32,1536]{1,0:T(8,128)(2,1)S(1)}, u32[]{:S(2)}, u32[]{:S(2)}) collective-permute-start(bf16[32,1536]{1,0:T(8,128)(2,1)S(1)} %get-tuple-element.61), channel_id=1, source_target_pairs={{0,2},{1,3},{2,0},{3,1},{4,6},{5,7},{6,4},{7,5},{8,10},{9,11},{10,... | collective-permute-start | bytes 294920 | tf_op jit(solution)/shard_map/ppermute | solution.py:210
  38.4 14.3 %collective-permute-start.14 = (bf16[32,3072]{1,0:T(8,128)(2,1)S(1)}, bf16[32,3072]{1,0:T(8,128)(2,1)S(1)}, u32[]{:S(2)}, u32[]{:S(2)}) collective-permute-start(bf16[32,3072]{1,0:T(8,128)(2,1)S(1)} %get-tuple-element.58), channel_id=1, source_target_pairs={{0,1},{1,0},{2,3},{3,2},{4,5},{5,4},{6,7},{7,6},{8,9},{9,8},{10,11... | collective-permute-start | bytes 589832 | tf_op jit(solution)/shard_map/ppermute | solution.py:210
  38.7 11.6 %collective-permute-start.18 = (bf16[32,1536]{1,0:T(8,128)(2,1)S(1)}, bf16[32,1536]{1,0:T(8,128)(2,1)S(1)}, u32[]{:S(2)}, u32[]{:S(2)}) collective-permute-start(bf16[32,1536]{1,0:T(8,128)(2,1)S(1)} %get-tuple-element.64), channel_id=1, source_target_pairs={{0,3},{1,2},{2,1},{3,0},{4,7},{5,6},{6,5},{7,4},{8,11},{9,10},{10,... | collective-permute-start | bytes 294920 | tf_op jit(solution)/shard_map/ppermute | solution.py:210
  43.5 9.1 %collective-permute-start.17 = (bf16[32,1536]{1,0:T(8,128)(2,1)S(1)}, bf16[32,1536]{1,0:T(8,128)(2,1)S(1)}, u32[]{:S(2)}, u32[]{:S(2)}) collective-permute-start(bf16[32,1536]{1,0:T(8,128)(2,1)S(1)} %relay.2), channel_id=1, source_target_pairs={{0,2},{1,3},{2,0},{3,1},{4,6},{5,7},{6,4},{7,5},{8,10},{9,11},{10,... | collective-permute-start | bytes 294920 | tf_op jit(solution)/shard_map/ppermute | solution.py:210
  53.6 8.3 %collective-permute-start.20 = (bf16[32,1536]{1,0:T(8,128)(2,1)S(1)}, bf16[32,1536]{1,0:T(8,128)(2,1)S(1)}, u32[]{:S(2)}, u32[]{:S(2)}) collective-permute-start(bf16[32,1536]{1,0:T(8,128)(2,1)S(1)} %get-tuple-element.68), channel_id=1, source_target_pairs={{0,2},{1,3},{2,0},{3,1},{4,6},{5,7},{6,4},{7,5},{8,10},{9,11},{10,... | collective-permute-start | bytes 294920 | tf_op jit(solution)/shard_map/ppermute | solution.py:210
  53.7 13.6 %collective-permute-start.19 = (bf16[32,3072]{1,0:T(8,128)(2,1)S(1)}, bf16[32,3072]{1,0:T(8,128)(2,1)S(1)}, u32[]{:S(2)}, u32[]{:S(2)}) collective-permute-start(bf16[32,3072]{1,0:T(8,128)(2,1)S(1)} %get-tuple-element.67.refs_0_), channel_id=1, source_target_pairs={{0,1},{1,0},{2,3},{3,2},{4,5},{5,4},{6,7},{7,6},{8,9},{9,8},{10,11... | collective-permute-start | bytes 589832 | tf_op jit(solution)/shard_map/ppermute | solution.py:210
  56.0 10.0 %collective-permute-start.23 = (bf16[32,1536]{1,0:T(8,128)(2,1)S(1)}, bf16[32,1536]{1,0:T(8,128)(2,1)S(1)}, u32[]{:S(2)}, u32[]{:S(2)}) collective-permute-start(bf16[32,1536]{1,0:T(8,128)(2,1)S(1)} %get-tuple-element.69), channel_id=1, source_target_pairs={{0,3},{1,2},{2,1},{3,0},{4,7},{5,6},{6,5},{7,4},{8,11},{9,10},{10,... | collective-permute-start | bytes 294920 | tf_op jit(solution)/shard_map/ppermute | solution.py:210
  58.0 9.2 %collective-permute-start.22 = (bf16[32,1536]{1,0:T(8,128)(2,1)S(1)}, bf16[32,1536]{1,0:T(8,128)(2,1)S(1)}, u32[]{:S(2)}, u32[]{:S(2)}) collective-permute-start(bf16[32,1536]{1,0:T(8,128)(2,1)S(1)} %get-tuple-element.69), channel_id=1, source_target_pairs={{0,2},{1,3},{2,0},{3,1},{4,6},{5,7},{6,4},{7,5},{8,10},{9,11},{10,... | collective-permute-start | bytes 294920 | tf_op jit(solution)/shard_map/ppermute | solution.py:210
  61.9 5.4 %collective-permute-start.21 = (bf16[32,1536]{1,0:T(8,128)(2,1)S(1)}, bf16[32,1536]{1,0:T(8,128)(2,1)S(1)}, u32[]{:S(2)}, u32[]{:S(2)}) collective-permute-start(bf16[32,1536]{1,0:T(8,128)(2,1)S(1)} %collective-permute-done.20.refs_2_), channel_id=1, source_target_pairs={{0,1},{1,0},{2,3},{3,2},{4,5},{5,4},{6,7},{7,6},{8,9},{9,8},{10,11... | collective-permute-start | bytes 294920 | tf_op jit(solution)/shard_map/ppermute | solution.py:210
  74.0 7.8 %collective-permute-start.25 = (bf16[32,1536]{1,0:T(8,128)(2,1)S(1)}, bf16[32,1536]{1,0:T(8,128)(2,1)S(1)}, u32[]{:S(2)}, u32[]{:S(2)}) collective-permute-start(bf16[32,1536]{1,0:T(8,128)(2,1)S(1)} %get-tuple-element.73), channel_id=1, source_target_pairs={{0,1},{1,0},{2,3},{3,2},{4,5},{5,4},{6,7},{7,6},{8,9},{9,8},{10,11... | collective-permute-start | bytes 294920 | tf_op jit(solution)/shard_map/ppermute | solution.py:210
  74.7 7.2 %collective-permute-start.26 = (bf16[32,1536]{1,0:T(8,128)(2,1)S(1)}, bf16[32,1536]{1,0:T(8,128)(2,1)S(1)}, u32[]{:S(2)}, u32[]{:S(2)}) collective-permute-start(bf16[32,1536]{1,0:T(8,128)(2,1)S(1)} %get-tuple-element.74), channel_id=1, source_target_pairs={{0,2},{1,3},{2,0},{3,1},{4,6},{5,7},{6,4},{7,5},{8,10},{9,11},{10,... | collective-permute-start | bytes 294920 | tf_op jit(solution)/shard_map/ppermute | solution.py:210
  76.9 10.7 %collective-permute-start.24 = (bf16[32,3072]{1,0:T(8,128)(2,1)S(1)}, bf16[32,3072]{1,0:T(8,128)(2,1)S(1)}, u32[]{:S(2)}, u32[]{:S(2)}) collective-permute-start(bf16[32,3072]{1,0:T(8,128)(2,1)S(1)} %get-tuple-element.71), channel_id=1, source_target_pairs={{0,1},{1,0},{2,3},{3,2},{4,5},{5,4},{6,7},{7,6},{8,9},{9,8},{10,11... | collective-permute-start | bytes 589832 | tf_op jit(solution)/shard_map/ppermute | solution.py:210
  77.7 9.9 %collective-permute-start.28 = (bf16[32,1536]{1,0:T(8,128)(2,1)S(1)}, bf16[32,1536]{1,0:T(8,128)(2,1)S(1)}, u32[]{:S(2)}, u32[]{:S(2)}) collective-permute-start(bf16[32,1536]{1,0:T(8,128)(2,1)S(1)} %get-tuple-element.77), channel_id=1, source_target_pairs={{0,3},{1,2},{2,1},{3,0},{4,7},{5,6},{6,5},{7,4},{8,11},{9,10},{10,... | collective-permute-start | bytes 294920 | tf_op jit(solution)/shard_map/ppermute | solution.py:210
  81.9 7.7 %collective-permute-start.27 = (bf16[32,1536]{1,0:T(8,128)(2,1)S(1)}, bf16[32,1536]{1,0:T(8,128)(2,1)S(1)}, u32[]{:S(2)}, u32[]{:S(2)}) collective-permute-start(bf16[32,1536]{1,0:T(8,128)(2,1)S(1)} %relay.3), channel_id=1, source_target_pairs={{0,2},{1,3},{2,0},{3,1},{4,6},{5,7},{6,4},{7,5},{8,10},{9,11},{10,... | collective-permute-start | bytes 294920 | tf_op jit(solution)/shard_map/ppermute | solution.py:210
